TPU v7x, 32 devices: a whole 2x2x4 slice. The times are simulated.
32 devices in a mesh: tiles: 8 (over z, y), rep: 4 (over x, core).
Axes of the slice: x: 2, y: 2, z: 4, core: 2. Of those that a mesh axis runs over, the one named last changes fastest.
Arguments:
- tiles: bfloat16 [64, 64, 4096], P(('tiles', 'rep')), may hold values from -6 to 6
- block_one: int32 [64], P(('tiles', 'rep')), may hold values from 0 to 7
- block_two: int32 [64], P(('tiles', 'rep')), may hold values from 0 to 15
- block_three: int32 [64], P(('tiles', 'rep')), may hold values from 0 to 15
- owner_map: int32 [8], replicated, may hold values from 0 to 7, each once
- u_one: float32 [32, 512], P(None, 'tiles'), may hold values from -6 to 6
- u_two: bfloat16 [32, 1024], P(None, 'tiles'), may hold values from -6 to 6
- u_three: bfloat16 [32, 1024], replicated, may hold values from -6 to 6
Outputs:
- factor: float32 [32, 512], P(None, 'tiles')
- tile_factor: bfloat16 [64, 2048], P(('tiles', 'rep'))
All inputs are finite; a program needn't handle non-finite values.
Results may differ from a plain program's by a relative error of at most 0.0081.
Values may be sent and summed in bfloat16 or wider, within the bound.
No kernel may reach another device: no remote copies, remote signals or barrier semaphores. Data moves between devices by JAX's collectives and lax.ppermute only.
A program may use at most 64 MiB of HBM per device.

v0:
```python
import jax
import jax.numpy as jnp
from jax import lax
from jax.sharding import PartitionSpec as P

NS_STEPS = 2


def pick(table, index, width):
    grid = table.reshape(table.shape[0], -1, width)
    return jnp.transpose(jnp.take(grid, index, axis=1), (1, 0, 2))


def orthonormal(rows, rows_total):
    hi = lax.Precision.HIGHEST
    rank = rows.shape[0]
    g0 = jnp.dot(rows, rows.T, precision=hi, preferred_element_type=jnp.float32)
    msq = jnp.trace(g0) / rows_total
    inv = 1.0 / jnp.sqrt(msq + 1e-06)
    x = rows * inv
    g = g0 * (inv * inv) / rows_total
    eye = jnp.eye(rank, dtype=jnp.float32)
    for step in range(NS_STEPS):
        if step > 0:
            g = jnp.dot(x, x.T, precision=hi, preferred_element_type=jnp.float32) / rows_total
        x = jnp.dot(1.5 * eye - 0.5 * g, x, precision=hi, preferred_element_type=jnp.float32)
    return x


def spread(current):
    cast = current.astype(jnp.bfloat16)
    return cast


def per_device(tiles, block_one, block_two, block_three, owner_map, u_one, u_two, u_three):
    hi = lax.Precision.HIGHEST
    count = tiles.shape[0]
    width = tiles.shape[1]
    rank = u_three.shape[0]
    blocks_total = owner_map.shape[0]
    rows_total = blocks_total * width
    two_full = lax.all_gather(u_two, "tiles", axis=1, tiled=True)
    two_pick = pick(two_full, block_two, width)
    three_pick = pick(u_three, block_three, width)
    cube = tiles.reshape(count, width, width, width)
    first = jnp.einsum(
        "tijk,tsk->tijs", cube, three_pick, preferred_element_type=jnp.float32
    ).astype(jnp.bfloat16)
    second = jnp.einsum("tijs,trj->tirs", first, two_pick, preferred_element_type=jnp.float32)
    products = second.reshape(count, width, rank * rank).astype(jnp.bfloat16)
    positions = jnp.take(owner_map, block_one)
    onehot = (positions[:, None] == jnp.arange(blocks_total, dtype=jnp.int32)[None, :]).astype(
        jnp.float32
    )
    current = lax.all_gather(u_one, "tiles", axis=1, tiled=True)
    readers = pick(spread(current), positions, width)
    partial_value = jnp.einsum("tic,tri->rc", products, readers, preferred_element_type=jnp.float32)
    project = lax.psum(partial_value, ("tiles", "rep")).astype(jnp.bfloat16)
    z_tile = jnp.einsum("rc,tic->tri", project, products, preferred_element_type=jnp.float32)
    term = jnp.einsum("tri,tn->rni", z_tile, onehot, precision=hi).reshape(rank, rows_total)
    rows = lax.psum(term, ("tiles", "rep"))
    current = orthonormal(rows, rows_total)
    tile_factor = pick(spread(current), positions, width).reshape(count, rank * width)
    own = current.shape[1] // lax.axis_size("tiles")
    factor = lax.dynamic_slice_in_dim(current, lax.axis_index("tiles") * own, own, 1)
    return (factor, tile_factor)


def solution(mesh):
    in_specs = (
        P(("tiles", "rep"), None, None),
        P(("tiles", "rep")),
        P(("tiles", "rep")),
        P(("tiles", "rep")),
        P(),
        P(None, "tiles"),
        P(None, "tiles"),
        P(),
    )
    out_specs = (P(None, "tiles"), P(("tiles", "rep"), None))
    return jax.shard_map(
        per_device, mesh=mesh, in_specs=in_specs, out_specs=out_specs, check_vma=False
    )
```

profile of v0, /device:TPU:0, one launch (start us, length us, event | category | flops | bytes accessed | tf_op | source)
XLA Modules:
  0.0 249.4 jit_solution(1242714139501248820)
XLA Ops:
  7.2 0.7 compare_select_fusion.1
  7.9 0.7 compare_and_fusion.1
  8.6 0.7 compare_select_fusion.2
  9.2 0.7 compare_and_fusion.2
  9.9 3.3 %reshape.47 = bf16[2,64,64,64]{3,2,1,0:T(8,128)(2,1)S(1)} reshape(bf16[2,64,4096]{2,1,0:T(8,128)(2,1)} %param.12) | data formatting | bytes 2097152 | tf_op jit(solution)/shard_map/reshape | solution.py:45
  13.2 0.1 reshape.46
  13.4 27.8 %all_gather.6 = bf16[32,1024]{1,0:T(8,128)(2,1)S(1)} all-gather(bf16[32,128]{1,0:T(8,128)(2,1)S(1)} %copy-done.3), channel_id=1, replica_groups=mesh['tiles'=8,'rep'=4] {'tiles'}, dimensions={1}, use_global_device_ids=true | all-gather | bytes 73728 | tf_op jit(solution)/shard_map/all_gather | solution.py:42
  41.1 0.1 reshape.45
  41.3 0.6 gather_fusion.2
  41.9 0.6 gather_fusion.1
  42.5 2.0 fusion
  44.5 1.1 fusion.1
  45.6 0.2 copy.27
  45.9 30.5 %all-gather = bf16[8,64,32]{1,2,0:T(8,128)(2,1)S(1)} all-gather(bf16[1,64,32]{1,2,0:T(8,128)(2,1)S(1)} %bitcast_convert_fusion), channel_id=1, replica_groups=mesh['tiles'=8,'rep'=4] {'tiles'}, dimensions={0}, use_global_device_ids=true | all-gather | bytes 36864 | tf_op jit(solution)/shard_map/all_gather | solution.py:55
  76.4 0.1 reshape.99
  76.5 0.1 reshape.48
  76.7 0.6 gather_fusion
  77.4 0.6 gather_fusion.3
  77.9 0.2 convolution_bitcast_fusion.1
  78.2 39.0 %all-reduce.4 = bf16[32,1024]{1,0:T(8,128)(2,1)S(1)} all-reduce(f32[32,1024]{1,0:T(8,128)S(1)} %convolution_bitcast_fusion.1), channel_id=1, replica_groups=mesh['tiles'=8,'rep'=4] {'tiles','rep'}, use_global_device_ids=true, to_apply=%region_0.3 | all-reduce | flops 32768 | bytes 196608 | tf_op jit(solution)/shard_map/psum | solution.py:58
  117.2 0.2 convolution_bitcast_fusion.2
  117.4 0.3 convolution_bitcast_fusion
  117.7 0.7 reshape.49
  118.4 118.1 %all-reduce.3.cloned.1.call-done = f32[32,512]{1,0:T(8,128)} async-done(((f32[32,512]{1,0:T(8,128)}), f32[32,512]{1,0:T(8,128)}) %all-reduce.3.cloned.1.call-update) | async-done | bytes 65552 | tf_op jit(solution)/shard_map/psum | solution.py:61
  236.6 1.7 select_reduce_fusion
  239.0 1.0 fusion.5
  240.0 0.2 fusion.2
  240.2 0.2 fusion.37
  240.4 0.1 reshape.50
  240.5 0.6 gather_fusion.4
  241.2 0.7 reshape.51
  241.9 0.7 constant_dynamic-slice_fusion
  (26 shorter events, 0.3 us)
Async XLA Ops:
  7.2 69.5 %copy-start = (s32[8]{0:T(128)S(1)}, s32[8]{0:T(128)}, u32[]{:S(2)}) copy-start(s32[8]{0:T(128)} %param.16) | copy-start | bytes 100
  7.2 6.0 %copy-start.1 = (bf16[32,1024]{1,0:T(8,128)(2,1)S(1)}, bf16[32,1024]{1,0:T(8,128)(2,1)}, u32[]{:S(2)}) copy-start(bf16[32,1024]{1,0:T(8,128)(2,1)} %param.19) | copy-start | bytes 196612
  7.2 6.2 %copy-start.3 = (bf16[32,128]{1,0:T(8,128)(2,1)S(1)}, bf16[32,128]{1,0:T(8,128)(2,1)}, u32[]{:S(2)}) copy-start(bf16[32,128]{1,0:T(8,128)(2,1)} %param.18) | copy-start | bytes 24580
  7.2 229.4 %all-reduce.3.cloned.1.call-start = ((), (), s32[]{:S(2)}) async-start(), calls=%async_computation | async-start | bytes 131072 | tf_op jit(solution)/shard_map/psum | solution.py:61
  44.5 1.3 copy-start.2
  44.5 32.1 %copy-start.4 = (s32[2]{0:T(128)S(1)}, s32[2]{0:T(128)}, u32[]{:S(2)}) copy-start(s32[2]{0:T(128)} %param.13) | copy-start | bytes 28
Sparse Core Ops, SparseCore 0:
  118.6 117.9 all-reduce.2
where the time goes:
time: 251 us; the launch traced here: 249 us
  waiting for transfers between devices  118 us (47%)
  blocking collectives  97.3 us (39%)
  between operations  15 us (6%)
  local copies, waits for them, and re-layouts  9.22 us (4%)
  matrix products  7.02 us (3%)
  other arithmetic  2.77 us (1%)
    psum x1, waiting for transfers between devices, per_device(): rows = lax.psum(term, ('tiles', 'rep'))  118 us
    psum x1, blocking collectives, per_device(): project = lax.psum(partial_value, ('tiles', 'rep')).astype(jnp.bfloat16)  39 us
    all_gather x1, blocking collectives, per_device(): current = lax.all_gather(u_one, 'tiles', axis=1, tiled=True)  30.5 us
    all_gather x1, blocking collectives, per_device(): two_full = lax.all_gather(u_two, 'tiles', axis=1, tiled=True)  27.8 us
  transfers between devices with their start and end apart: 1, of which 1 were waited for; matrix products, arithmetic and copies ran while one was open for 0% of the time, Pallas kernels for 0%

commit v1 on v0

v1 whole, which is shorter than its diff:
```python
import functools

import jax
import jax.numpy as jnp
from jax import lax
from jax.experimental import pallas as pl
from jax.experimental.pallas import tpu as pltpu
from jax.sharding import PartitionSpec as P

NS_STEPS = 2
HI = lax.Precision.HIGHEST
LANES = 128
META = 16
F32 = jnp.float32
BF16 = jnp.bfloat16


def pick(table, index, width):
    grid = table.reshape(table.shape[0], -1, width)
    return jnp.transpose(jnp.take(grid, index, axis=1), (1, 0, 2))


def orthonormal(rows, rows_total):
    rank = rows.shape[0]
    g0 = jnp.dot(rows, rows.T, precision=HI, preferred_element_type=F32)
    msq = jnp.trace(g0) / rows_total
    inv = 1.0 / jnp.sqrt(msq + 1e-06)
    x = rows * inv
    g = g0 * (inv * inv) / rows_total
    eye = jnp.eye(rank, dtype=F32)
    for step in range(NS_STEPS):
        if step > 0:
            g = jnp.dot(x, x.T, precision=HI, preferred_element_type=F32) / rows_total
        x = jnp.dot(1.5 * eye - 0.5 * g, x, precision=HI, preferred_element_type=F32)
    return x


def general(tiles, block_one, block_two, block_three, owner_map, u_one, u_two, u_three):
    count, width = tiles.shape[:2]
    rank = u_three.shape[0]
    blocks_total = owner_map.shape[0]
    rows_total = blocks_total * width
    two_full = lax.all_gather(u_two, "tiles", axis=1, tiled=True)
    two_pick = pick(two_full, block_two, width)
    three_pick = pick(u_three, block_three, width)
    cube = tiles.reshape(count, width, width, width)
    first = jnp.einsum("tijk,tsk->tijs", cube, three_pick, preferred_element_type=F32).astype(BF16)
    second = jnp.einsum("tijs,trj->tirs", first, two_pick, preferred_element_type=F32)
    products = second.reshape(count, width, rank * rank).astype(BF16)
    positions = jnp.take(owner_map, block_one)
    onehot = (positions[:, None] == jnp.arange(blocks_total, dtype=jnp.int32)[None, :]).astype(F32)
    current = lax.all_gather(u_one.astype(BF16), "tiles", axis=1, tiled=True)
    readers = pick(current, positions, width)
    partial_value = jnp.einsum("tic,tri->rc", products, readers, preferred_element_type=F32)
    project = lax.psum(partial_value, ("tiles", "rep")).astype(BF16)
    z_tile = jnp.einsum("rc,tic->tri", project, products, preferred_element_type=F32)
    term = jnp.einsum("tri,tn->rni", z_tile, onehot, precision=HI).reshape(rank, rows_total)
    rows = lax.psum(term, ("tiles", "rep"))
    current = orthonormal(rows, rows_total)
    tile_factor = pick(current.astype(BF16), positions, width).reshape(count, rank * width)
    own = u_one.shape[1]
    factor = lax.dynamic_slice_in_dim(current, lax.axis_index("tiles") * own, own, 1)
    return (factor, tile_factor)


def lane_iota(shape):
    return lax.broadcasted_iota(jnp.int32, shape, len(shape) - 1)


def row_iota(shape):
    return lax.broadcasted_iota(jnp.int32, shape, len(shape) - 2)


def nt(a, b, precision=None):
    return lax.dot_general(
        a, b, (((1,), (1,)), ((), ())), precision=precision, preferred_element_type=F32
    )


def first_kernel(one, two, three, owner, tiles, u_three, u_two, u_one, out, scratch, two_f32):
    count, width = tiles.shape[:2]
    rank = u_three.shape[0]
    half = LANES // 2
    group = LANES // rank
    span = group * width
    weights = []
    for t in range(count):
        block = three[t]
        start = pl.multiple_of((block // 2) * LANES, LANES)
        window = u_three[:, pl.ds(start, LANES)].astype(F32)
        same = (lane_iota(window.shape) // half) == (block % 2)
        both = jnp.where(same, window, pltpu.roll(window, half, 1))
        full = jnp.concatenate([jnp.concatenate([both] * (span // LANES), axis=1)] * group, axis=0)
        keep = (row_iota(full.shape) // rank) == (lane_iota(full.shape) // width)
        weights.append(jnp.where(keep, full, 0.0).astype(BF16))
    for g in range(tiles.shape[2] // span):
        parts = [nt(weights[t], tiles[t, :, g * span : (g + 1) * span]) for t in range(count)]
        scratch[g * LANES : (g + 1) * LANES, :] = jnp.concatenate(parts, axis=1)

    share = META // 2
    q = lax.axis_index("rep")
    two_f32[...] = u_two[...].astype(F32)
    top = two_f32[pl.ds(pl.multiple_of(q * share, share), share), :]
    low = u_one[pl.ds(pl.multiple_of(q * share, share), share), :]
    lane = lane_iota((share, half))
    ints = jnp.zeros((share, half), F32)
    for t in range(count):
        ints = jnp.where(lane == t, two[t].astype(F32), ints)
        ints = jnp.where(lane == count + t, owner[one[t]].astype(F32), ints)
    meta = jnp.concatenate([top, jnp.concatenate([low, ints], axis=1)], axis=0).astype(BF16)
    for s in range(rank):
        out[s, 0:width, :] = scratch[pl.ds(s, width, stride=rank), :].astype(BF16)
        out[s, width : width + META, :] = meta


def rows_kernel(reps, got, out, two, one, ints, ints_smem, total):
    sources, depth = got.shape[:2]
    width = depth - META
    half = LANES // 2
    share = META // 2
    rank = share * reps
    count = LANES // width
    owners = sources // reps
    for src in range(sources):
        t, q = divmod(src, reps)
        meta = got[src, width:depth, :].astype(F32)
        two[t, q * share : (q + 1) * share, :] = meta[:share]
        one[t, q * share : (q + 1) * share, :] = meta[share:]
        ints[src : src + 1, :] = meta[share : share + 1].astype(jnp.int32)
    pltpu.sync_copy(ints, ints_smem)
    total[...] = jnp.zeros_like(total)
    lane = lane_iota((rank, LANES))
    for src in range(sources):
        block = got[src, 0:width, :]
        moving = jnp.concatenate([block, block], axis=0)
        picks = []
        for t in range(count):
            b = ints_smem[src, half + t]
            picks.append(jnp.where((lane // half) == (b % 2), two[b // 2], 0.0))
        stacked = jnp.concatenate(picks, axis=0).astype(BF16)
        product = jnp.dot(stacked, moving, preferred_element_type=F32)
        for t in range(count):
            p = ints_smem[src, half + count + t]
            mine = product[t * rank : (t + 1) * rank].astype(BF16).astype(F32)
            total[p] += jnp.where((lane // width) == t, mine, 0.0)
    sums = []
    for p in range(owners):
        value = total[p]
        sums.append((value + pltpu.roll(value, half, 1))[:, :half])
    table = jnp.concatenate(sums, axis=1)
    readers = jnp.concatenate([one[p][:, :half] for p in range(owners)], axis=1)
    project = nt(readers, table, HI).astype(BF16).astype(F32)
    out[...] = jnp.dot(project, table, precision=HI, preferred_element_type=F32).astype(BF16)


def final_kernel(one, owner, a, b, c, d, factor, tile_factor, table):
    rank, rows_total = a.shape
    half = LANES // 2
    rows = (a[...].astype(F32) + b[...].astype(F32)) + (c[...].astype(F32) + d[...].astype(F32))
    g0 = nt(rows, rows, HI)
    eye = (row_iota(g0.shape) == lane_iota(g0.shape)).astype(F32)
    msq = jnp.sum(g0 * eye, keepdims=True) / rows_total
    inv = 1.0 / jnp.sqrt(msq + 1e-06)
    x = rows * inv
    g = g0 * (inv * inv) / rows_total
    for step in range(NS_STEPS):
        if step > 0:
            g = nt(x, x, HI) / rows_total
        x = jnp.dot(1.5 * eye - 0.5 * g, x, precision=HI, preferred_element_type=F32)
    table[...] = x

    def block(p):
        window = table[:, pl.ds(pl.multiple_of((p // 2) * LANES, LANES), LANES)]
        return jnp.where(p % 2 == 1, pltpu.roll(window, half, 1), window)[:, :half]

    factor[...] = block(lax.axis_index("tiles"))
    for t in range(tile_factor.shape[0]):
        value = block(owner[one[t]])
        for r in range(0, rank, 2):
            line = jnp.concatenate([value[r : r + 1], value[r + 1 : r + 2]], axis=1)
            tile_factor[t : t + 1, r * half : (r + 2) * half] = line.astype(BF16)


def swap(x, size, mask):
    return lax.ppermute(x, ("tiles", "rep"), [(i, i ^ mask) for i in range(size)])


def sliced(tiles, block_one, block_two, block_three, owner_map, u_one, u_two, u_three):
    count, width = tiles.shape[:2]
    rank = u_three.shape[0]
    owners = lax.axis_size("tiles")
    reps = lax.axis_size("rep")
    size = owners * reps
    rows_total = owner_map.shape[0] * width
    smem = pl.BlockSpec(memory_space=pltpu.SMEM)
    vmem = pl.BlockSpec(memory_space=pltpu.VMEM)
    params = pltpu.CompilerParams(vmem_limit_bytes=32 * 1024 * 1024)
    sends = pl.pallas_call(
        first_kernel,
        out_shape=jax.ShapeDtypeStruct((rank, width + META, LANES), BF16),
        in_specs=[smem] * 4 + [vmem] * 4,
        out_specs=vmem,
        scratch_shapes=[
            pltpu.VMEM((width * rank, LANES), F32),
            pltpu.VMEM(u_two.shape, F32),
        ],
        compiler_params=params,
        name="first",
    )(block_one, block_two, block_three, owner_map, tiles, u_three, u_two, u_one)
    got = lax.all_to_all(sends, ("tiles", "rep"), 0, 0, tiled=True)
    part = pl.pallas_call(
        functools.partial(rows_kernel, reps),
        out_shape=jax.ShapeDtypeStruct((rank, rows_total), BF16),
        in_specs=[vmem],
        out_specs=vmem,
        scratch_shapes=[
            pltpu.VMEM((owners, rank, LANES), F32),
            pltpu.VMEM((owners, rank, LANES), F32),
            pltpu.VMEM((size, LANES), jnp.int32),
            pltpu.SMEM((size, LANES), jnp.int32),
            pltpu.VMEM((owners, rank, LANES), F32),
        ],
        compiler_params=params,
        name="rows_part",
    )(got)
    part = (part.astype(F32) + swap(part, size, 1).astype(F32)).astype(BF16)
    m, n = 2, 4
    pair = part.astype(F32) + swap(part, size, m | 1).astype(F32)
    other = swap(part, size, n | 1).astype(F32) + swap(part, size, m ^ n).astype(F32)
    part = (pair + other).astype(BF16)
    m, n = 8, 16
    parts = [part, swap(part, size, m | 1), swap(part, size, n | 1), swap(part, size, m ^ n)]
    return pl.pallas_call(
        final_kernel,
        out_shape=(
            jax.ShapeDtypeStruct(u_one.shape, F32),
            jax.ShapeDtypeStruct((count, rank * width), BF16),
        ),
        in_specs=[smem] * 2 + [vmem] * 4,
        out_specs=(vmem, vmem),
        scratch_shapes=[pltpu.VMEM((rank, rows_total), F32)],
        compiler_params=params,
        name="final",
    )(block_one, owner_map, *parts)


def per_device(*args):
    tiles, _, _, _, owner_map, u_one, u_two, u_three = args
    count, width = tiles.shape[:2]
    rank = u_three.shape[0]
    owners = lax.axis_size("tiles")
    reps = lax.axis_size("rep")
    fits = (
        owners * reps == rank == 32
        and reps * META // 2 == rank
        and width * 2 == LANES
        and count == 2
        and owner_map.shape[0] == owners
        and u_one.shape[1] == width
        and u_two.shape[1] == LANES
    )
    return (sliced if fits else general)(*args)


def solution(mesh):
    in_specs = (
        P(("tiles", "rep"), None, None),
        P(("tiles", "rep")),
        P(("tiles", "rep")),
        P(("tiles", "rep")),
        P(),
        P(None, "tiles"),
        P(None, "tiles"),
        P(),
    )
    out_specs = (P(None, "tiles"), P(("tiles", "rep"), None))
    return jax.shard_map(
        per_device, mesh=mesh, in_specs=in_specs, out_specs=out_specs, check_vma=False
    )
```

time: 251 us -> 52.7 us (0.21)
  waiting for transfers between devices: 118 us -> 6.72 us
  blocking collectives: 97.3 us -> 25 us
  between operations: 15 us -> 0.69 us
  starting transfers between devices: 0.04 us -> 7.58 us
  matrix products: 7.02 us -> 0 us
  Pallas kernels: 0 us -> 6.25 us
  local copies, waits for them, and re-layouts: 9.22 us -> 6.1 us
  other arithmetic: 2.77 us -> 0.03 us
    psum x1 -> x0, waiting for transfers between devices: 118 us -> none  [per_device(): rows = lax.psum(term, ('tiles', 'rep'))]
    all_gather x2 -> x0, blocking collectives: 58.3 us -> none  [the longest x1 30.5 us: per_device(): current = lax.all_gather(u_one, 'tiles', axis=1, tiled=True)]
    psum x1 -> x0, blocking collectives: 39 us -> none  [per_device(): project = lax.psum(partial_value, ('tiles', 'rep')).astype(jnp.bfloat16)]
    all_to_all x0 -> x1, blocking collectives: none -> 25 us  [sliced(): got = lax.all_to_all(sends, ('tiles', 'rep'), 0, 0, tiled=True)]
    ppermute x0 -> x7, starting transfers between devices: none -> 7.58 us  [swap(): lax.ppermute(x, ('tiles', 'rep'), [(i, i ^ mask) for i in range(size)])]
    dot_general x9 -> x0, matrix products: 7.02 us -> none  [the longest x1 2.04 us: per_device(): jnp.einsum('tijk,tsk->tijs', cube, three_pick, preferred_element_type=jnp...]
    ppermute x0 -> x7, waiting for transfers between devices: none -> 6.72 us  [swap(): lax.ppermute(x, ('tiles', 'rep'), [(i, i ^ mask) for i in range(size)])]
    pallas_call x0 -> x3, Pallas kernels: none -> 6.25 us  [the longest x1 2.29 us: sliced(): pl.pallas_call(final_kernel, out_shape=(jax.ShapeDtypeStruct(u_one.shape,...]
  transfers between devices with their start and end apart: 1 -> 7, of which waited for: 1 -> 6; matrix products, arithmetic and copies ran while one was open for 0% -> 0% of each run, Pallas kernels for 0% -> 0%
where the time goes in v1:
time: 52.7 us; the launch traced here: 52.4 us
  blocking collectives  25 us (47%)
  starting transfers between devices  7.58 us (14%)
  waiting for transfers between devices  6.72 us (13%)
  Pallas kernels  6.25 us (12%)
  local copies, waits for them, and re-layouts  6.1 us (12%)
  between operations  0.69 us (1%)
    all_to_all x1, blocking collectives, sliced(): got = lax.all_to_all(sends, ('tiles', 'rep'), 0, 0, tiled=True)  25 us
    ppermute x7, starting transfers between devices, swap(): lax.ppermute(x, ('tiles', 'rep'), [(i, i ^ mask) for i in range(size)])  7.58 us
    ppermute x7, waiting for transfers between devices, swap(): lax.ppermute(x, ('tiles', 'rep'), [(i, i ^ mask) for i in range(size)])  6.72 us
    unnamed x20, local copies, waits for them, and re-layouts  6.1 us
    pallas_call x1, Pallas kernels, sliced(): pl.pallas_call(final_kernel, out_shape=(jax.ShapeDtypeStruct(u_one.shape,...  2.29 us
    pallas_call x1, Pallas kernels, sliced(): pl.pallas_call(functools.partial(rows_kernel, reps), out_shape=jax.ShapeD...  2.01 us
    pallas_call x1, Pallas kernels, sliced(): pl.pallas_call(first_kernel, out_shape=jax.ShapeDtypeStruct((rank, width...  1.96 us
  transfers between devices with their start and end apart: 7, of which 6 were waited for; matrix products, arithmetic and copies ran while one was open for 0% of the time, Pallas kernels for 0%

profile of v1, /device:TPU:0, one launch (start us, length us, event | category | flops | bytes accessed | tf_op | source)
XLA Modules:
  0.0 52.4 jit_solution(10511091397164390115)
XLA Ops:
  0.6 0.0 copy-start
  0.6 1.2 %copy-done = bf16[2,64,4096]{2,1,0:T(8,128)(2,1)S(1)} copy-done((bf16[2,64,4096]{2,1,0:T(8,128)(2,1)S(1)}, bf16[2,64,4096]{2,1,0:T(8,128)(2,1)}, u32[]{:S(2)}) %copy-start) | copy-done | bytes 1048600
  1.9 0.0 copy-start.1
  1.9 0.8 %copy-done.1 = bf16[32,1024]{1,0:T(8,128)(2,1)S(1)} copy-done((bf16[32,1024]{1,0:T(8,128)(2,1)S(1)}, bf16[32,1024]{1,0:T(8,128)(2,1)}, u32[]{:S(2)}) %copy-start.1) | copy-done | bytes 65560
  2.7 0.7 %copy-done.2 = f32[32,64]{1,0:T(8,128)S(1)} copy-done((f32[32,64]{1,0:T(8,128)S(1)}, f32[32,64]{1,0:T(8,128)}, u32[]{:S(2)}) %copy-start.2) | copy-done | bytes 8216
  3.4 0.7 %copy-done.3 = bf16[32,128]{1,0:T(8,128)(2,1)S(1)} copy-done((bf16[32,128]{1,0:T(8,128)(2,1)S(1)}, bf16[32,128]{1,0:T(8,128)(2,1)}, u32[]{:S(2)}) %copy-start.3) | copy-done | bytes 8216
  4.1 0.7 %copy-done.4 = s32[2]{0:T(128)S(1)} copy-done((s32[2]{0:T(128)S(1)}, s32[2]{0:T(128)}, u32[]{:S(2)}) %copy-start.4) | copy-done | bytes 32
  4.8 0.7 %copy-done.6 = s32[8]{0:T(128)S(1)} copy-done((s32[8]{0:T(128)S(1)}, s32[8]{0:T(128)}, u32[]{:S(2)}) %copy-start.6) | copy-done | bytes 56
  5.4 0.7 %copy-done.8 = s32[2]{0:T(128)S(1)} copy-done((s32[2]{0:T(128)S(1)}, s32[2]{0:T(128)}, u32[]{:S(2)}) %copy-start.8) | copy-done | bytes 32
  6.1 0.7 %copy-done.9 = s32[2]{0:T(128)S(1)} copy-done((s32[2]{0:T(128)S(1)}, s32[2]{0:T(128)}, u32[]{:S(2)}) %copy-start.9) | copy-done | bytes 32
  6.7 2.0 %first.1 = bf16[32,80,128]{2,1,0:T(8,128)(2,1)S(1)} custom-call(s32[2]{0:T(128)S(1)} %copy-done.4, s32[2]{0:T(128)S(1)} %copy-done.8, s32[2]{0:T(128)S(1)} %copy-done.9, s32[8]{0:T(128)S(1)} %copy-done.6, bf16[2,64,4096]{2,1,0:T(8,128)(2,1)S(1)} %copy-done, bf16[32,1024]{1,0:T(8,128)(2,1)S(1)} %copy-done.1, bf16[32,128]{1,0:T(8,128)(2,1)S(1)} %copy-done.3, ...), custom_call_target="tpu_custom_call" | custom-call | tf_op jit(solution)/shard_map/first/pallas_call | solution.py:198
  8.7 25.0 %all_to_all.5.got = bf16[32,80,128]{2,1,0:T(8,128)(2,1)S(1)} all-to-all(bf16[32,80,128]{2,1,0:T(8,128)(2,1)S(1)} %first.1), channel_id=1, replica_groups=mesh['tiles'=8,'rep'=4] {'tiles','rep'}, dimensions={0} | all-to-all | bytes 1310720 | tf_op jit(solution)/shard_map/all_to_all | solution.py:210
  33.7 2.0 %rows_part.1 = bf16[32,512]{1,0:T(8,128)(2,1)S(1)} custom-call(bf16[32,80,128]{2,1,0:T(8,128)(2,1)S(1)} %all_to_all.5.got), custom_call_target="tpu_custom_call" | custom-call | tf_op jit(solution)/shard_map/rows_part/pallas_call | solution.py:211
  35.7 0.1 collective-permute-start
  35.8 1.1 %collective-permute-done = bf16[32,512]{1,0:T(8,128)(2,1)S(1)} collective-permute-done((bf16[32,512]{1,0:T(8,128)(2,1)S(1)}, bf16[32,512]{1,0:T(8,128)(2,1)S(1)}, u32[]{:S(2)}, u32[]{:S(2)}) %collective-permute-start) | collective-permute-done | bytes 32800 | tf_op jit(solution)/shard_map/ppermute | solution.py:185
  37.0 0.0 copy-start.5
  37.0 0.0 copy-start.7
  37.0 2.4 %collective-permute-start.3 = (bf16[32,512]{1,0:T(8,128)(2,1)S(1)}, bf16[32,512]{1,0:T(8,128)(2,1)S(1)}, u32[]{:S(2)}, u32[]{:S(2)}) collective-permute-start(bf16[32,512]{1,0:T(8,128)(2,1)S(1)} %add_convert_fusion.1), channel_id=1, source_target_pairs={{0,6},{1,7},{2,4},{3,5},{4,2},{5,3},{6,0},{7,1},{8,14},{9,15},{10,... | collective-permute-start | bytes 98312 | tf_op jit(solution)/shard_map/ppermute | solution.py:185
  39.4 0.2 collective-permute-start.2
  39.5 0.8 %collective-permute-start.1 = (bf16[32,512]{1,0:T(8,128)(2,1)S(1)}, bf16[32,512]{1,0:T(8,128)(2,1)S(1)}, u32[]{:S(2)}, u32[]{:S(2)}) collective-permute-start(bf16[32,512]{1,0:T(8,128)(2,1)S(1)} %add_convert_fusion.1), channel_id=1, source_target_pairs={{0,3},{1,2},{2,1},{3,0},{4,7},{5,6},{6,5},{7,4},{8,11},{9,10},{10,... | collective-permute-start | bytes 98312 | tf_op jit(solution)/shard_map/ppermute | solution.py:185
  40.3 1.6 %collective-permute-done.3 = bf16[32,512]{1,0:T(8,128)(2,1)S(1)} collective-permute-done((bf16[32,512]{1,0:T(8,128)(2,1)S(1)}, bf16[32,512]{1,0:T(8,128)(2,1)S(1)}, u32[]{:S(2)}, u32[]{:S(2)}) %collective-permute-start.3) | collective-permute-done | bytes 32800 | tf_op jit(solution)/shard_map/ppermute | solution.py:185
  41.9 1.1 %collective-permute-done.2 = bf16[32,512]{1,0:T(8,128)(2,1)S(1)} collective-permute-done((bf16[32,512]{1,0:T(8,128)(2,1)S(1)}, bf16[32,512]{1,0:T(8,128)(2,1)S(1)}, u32[]{:S(2)}, u32[]{:S(2)}) %collective-permute-start.2) | collective-permute-done | bytes 32800 | tf_op jit(solution)/shard_map/ppermute | solution.py:185
  43.0 0.0 collective-permute-done.1
  43.0 1.5 %collective-permute-start.6 = (bf16[32,512]{1,0:T(8,128)(2,1)S(1)}, bf16[32,512]{1,0:T(8,128)(2,1)S(1)}, u32[]{:S(2)}, u32[]{:S(2)}) collective-permute-start(bf16[32,512]{1,0:T(8,128)(2,1)S(1)} %add_convert_fusion.a), channel_id=1, source_target_pairs={{0,24},{1,25},{2,26},{3,27},{4,28},{5,29},{6,30},{7,31},{8,16},{9,... | collective-permute-start | bytes 98312 | tf_op jit(solution)/shard_map/ppermute | solution.py:185
  44.5 0.4 collective-permute-start.5
  45.0 2.2 %collective-permute-start.4 = (bf16[32,512]{1,0:T(8,128)(2,1)S(1)}, bf16[32,512]{1,0:T(8,128)(2,1)S(1)}, u32[]{:S(2)}, u32[]{:S(2)}) collective-permute-start(bf16[32,512]{1,0:T(8,128)(2,1)S(1)} %add_convert_fusion.a), channel_id=1, source_target_pairs={{0,9},{1,8},{2,11},{3,10},{4,13},{5,12},{6,15},{7,14},{8,1},{9,0},... | collective-permute-start | bytes 98312 | tf_op jit(solution)/shard_map/ppermute | solution.py:185
  47.2 1.8 %collective-permute-done.6.d = bf16[32,512]{1,0:T(8,128)(2,1)S(1)} collective-permute-done((bf16[32,512]{1,0:T(8,128)(2,1)S(1)}, bf16[32,512]{1,0:T(8,128)(2,1)S(1)}, u32[]{:S(2)}, u32[]{:S(2)}) %collective-permute-start.6) | collective-permute-done | bytes 32800 | tf_op jit(solution)/shard_map/ppermute | solution.py:185
  49.0 1.0 %collective-permute-done.5.c = bf16[32,512]{1,0:T(8,128)(2,1)S(1)} collective-permute-done((bf16[32,512]{1,0:T(8,128)(2,1)S(1)}, bf16[32,512]{1,0:T(8,128)(2,1)S(1)}, u32[]{:S(2)}, u32[]{:S(2)}) %collective-permute-start.5) | collective-permute-done | bytes 32800 | tf_op jit(solution)/shard_map/ppermute | solution.py:185
  50.0 0.1 collective-permute-done.4.b
  50.1 0.0 copy-done.5
  50.1 0.0 copy-done.7
  50.1 2.3 %final.1 = (f32[32,64]{1,0:T(8,128)}, bf16[2,2048]{1,0:T(2,128)(2,1)}) custom-call(s32[2]{0:T(128)S(1)} %copy-done.5, s32[8]{0:T(128)S(1)} %copy-done.7, bf16[32,512]{1,0:T(8,128)(2,1)S(1)} %add_convert_fusion.a, bf16[32,512]{1,0:T(8,128)(2,1)S(1)} %collective-permute-done.4.b, bf16[32,512]{1,0:T(8,128)(2,1)S(1)} %collective-permute-done.5.c, ...), custom_call_target="tpu_custom_call" | custom-call | tf_op jit(solution)/shard_map/final/pallas_call | solution.py:233
  (8 shorter events, 0.0 us)
Async XLA Ops:
  0.6 1.2 %copy-start = (bf16[2,64,4096]{2,1,0:T(8,128)(2,1)S(1)}, bf16[2,64,4096]{2,1,0:T(8,128)(2,1)}, u32[]{:S(2)}) copy-start(bf16[2,64,4096]{2,1,0:T(8,128)(2,1)} %tiles.1) | copy-start | bytes 3145732
  1.9 0.8 %copy-start.1 = (bf16[32,1024]{1,0:T(8,128)(2,1)S(1)}, bf16[32,1024]{1,0:T(8,128)(2,1)}, u32[]{:S(2)}) copy-start(bf16[32,1024]{1,0:T(8,128)(2,1)} %u_three.1) | copy-start | bytes 196612
  2.7 0.7 %copy-start.2 = (f32[32,64]{1,0:T(8,128)S(1)}, f32[32,64]{1,0:T(8,128)}, u32[]{:S(2)}) copy-start(f32[32,64]{1,0:T(8,128)} %u_one.1) | copy-start | bytes 24580
  3.4 0.7 %copy-start.3 = (bf16[32,128]{1,0:T(8,128)(2,1)S(1)}, bf16[32,128]{1,0:T(8,128)(2,1)}, u32[]{:S(2)}) copy-start(bf16[32,128]{1,0:T(8,128)(2,1)} %u_two.1) | copy-start | bytes 24580
  4.1 0.7 %copy-start.4 = (s32[2]{0:T(128)S(1)}, s32[2]{0:T(128)}, u32[]{:S(2)}) copy-start(s32[2]{0:T(128)} %one.3) | copy-start | bytes 28
  4.8 0.7 %copy-start.6 = (s32[8]{0:T(128)S(1)}, s32[8]{0:T(128)}, u32[]{:S(2)}) copy-start(s32[8]{0:T(128)} %owner.3) | copy-start | bytes 100
  5.4 0.7 %copy-start.8 = (s32[2]{0:T(128)S(1)}, s32[2]{0:T(128)}, u32[]{:S(2)}) copy-start(s32[2]{0:T(128)} %two.1) | copy-start | bytes 28
  6.1 0.7 %copy-start.9 = (s32[2]{0:T(128)S(1)}, s32[2]{0:T(128)}, u32[]{:S(2)}) copy-start(s32[2]{0:T(128)} %three.1) | copy-start | bytes 28
  35.7 1.2 %collective-permute-start = (bf16[32,512]{1,0:T(8,128)(2,1)S(1)}, bf16[32,512]{1,0:T(8,128)(2,1)S(1)}, u32[]{:S(2)}, u32[]{:S(2)}) collective-permute-start(bf16[32,512]{1,0:T(8,128)(2,1)S(1)} %rows_part.1), channel_id=1, source_target_pairs={{0,1},{1,0},{2,3},{3,2},{4,5},{5,4},{6,7},{7,6},{8,9},{9,8},{10,11... | collective-permute-start | bytes 98312 | tf_op jit(solution)/shard_map/ppermute | solution.py:185
  37.0 13.1 %copy-start.5 = (s32[2]{0:T(128)S(1)}, s32[2]{0:T(128)}, u32[]{:S(2)}) copy-start(s32[2]{0:T(128)} %one.3) | copy-start | bytes 28
  37.0 13.1 %copy-start.7 = (s32[8]{0:T(128)S(1)}, s32[8]{0:T(128)}, u32[]{:S(2)}) copy-start(s32[8]{0:T(128)} %owner.3) | copy-start | bytes 100
  37.0 4.9 %collective-permute-start.3 = (bf16[32,512]{1,0:T(8,128)(2,1)S(1)}, bf16[32,512]{1,0:T(8,128)(2,1)S(1)}, u32[]{:S(2)}, u32[]{:S(2)}) collective-permute-start(bf16[32,512]{1,0:T(8,128)(2,1)S(1)} %add_convert_fusion.1), channel_id=1, source_target_pairs={{0,6},{1,7},{2,4},{3,5},{4,2},{5,3},{6,0},{7,1},{8,14},{9,15},{10,... | collective-permute-start | bytes 98312 | tf_op jit(solution)/shard_map/ppermute | solution.py:185
  39.4 3.6 %collective-permute-start.2 = (bf16[32,512]{1,0:T(8,128)(2,1)S(1)}, bf16[32,512]{1,0:T(8,128)(2,1)S(1)}, u32[]{:S(2)}, u32[]{:S(2)}) collective-permute-start(bf16[32,512]{1,0:T(8,128)(2,1)S(1)} %add_convert_fusion.1), channel_id=1, source_target_pairs={{0,5},{1,4},{2,7},{3,6},{4,1},{5,0},{6,3},{7,2},{8,13},{9,12},{10,... | collective-permute-start | bytes 98312 | tf_op jit(solution)/shard_map/ppermute | solution.py:185
  39.5 3.5 %collective-permute-start.1 = (bf16[32,512]{1,0:T(8,128)(2,1)S(1)}, bf16[32,512]{1,0:T(8,128)(2,1)S(1)}, u32[]{:S(2)}, u32[]{:S(2)}) collective-permute-start(bf16[32,512]{1,0:T(8,128)(2,1)S(1)} %add_convert_fusion.1), channel_id=1, source_target_pairs={{0,3},{1,2},{2,1},{3,0},{4,7},{5,6},{6,5},{7,4},{8,11},{9,10},{10,... | collective-permute-start | bytes 98312 | tf_op jit(solution)/shard_map/ppermute | solution.py:185
  43.0 6.0 %collective-permute-start.6 = (bf16[32,512]{1,0:T(8,128)(2,1)S(1)}, bf16[32,512]{1,0:T(8,128)(2,1)S(1)}, u32[]{:S(2)}, u32[]{:S(2)}) collective-permute-start(bf16[32,512]{1,0:T(8,128)(2,1)S(1)} %add_convert_fusion.a), channel_id=1, source_target_pairs={{0,24},{1,25},{2,26},{3,27},{4,28},{5,29},{6,30},{7,31},{8,16},{9,... | collective-permute-start | bytes 98312 | tf_op jit(solution)/shard_map/ppermute | solution.py:185
  44.5 5.4 %collective-permute-start.5 = (bf16[32,512]{1,0:T(8,128)(2,1)S(1)}, bf16[32,512]{1,0:T(8,128)(2,1)S(1)}, u32[]{:S(2)}, u32[]{:S(2)}) collective-permute-start(bf16[32,512]{1,0:T(8,128)(2,1)S(1)} %add_convert_fusion.a), channel_id=1, source_target_pairs={{0,17},{1,16},{2,19},{3,18},{4,21},{5,20},{6,23},{7,22},{8,25},{9,... | collective-permute-start | bytes 98312 | tf_op jit(solution)/shard_map/ppermute | solution.py:185
  45.0 5.1 %collective-permute-start.4 = (bf16[32,512]{1,0:T(8,128)(2,1)S(1)}, bf16[32,512]{1,0:T(8,128)(2,1)S(1)}, u32[]{:S(2)}, u32[]{:S(2)}) collective-permute-start(bf16[32,512]{1,0:T(8,128)(2,1)S(1)} %add_convert_fusion.a), channel_id=1, source_target_pairs={{0,9},{1,8},{2,11},{3,10},{4,13},{5,12},{6,15},{7,14},{8,1},{9,0},... | collective-permute-start | bytes 98312 | tf_op jit(solution)/shard_map/ppermute | solution.py:185

commit v2 on v1

--- a/solution.py
+++ b/solution.py
@@ -10,6 +10,8 @@
 NS_STEPS = 2
 HI = lax.Precision.HIGHEST
 LANES = 128
+WIDE = 60 * 1024 * 1024
+NARROW = 16 * 1024 * 1024
 META = 16
 F32 = jnp.float32
 BF16 = jnp.bfloat16
@@ -77,12 +79,24 @@
     )
 
 
-def first_kernel(one, two, three, owner, tiles, u_three, u_two, u_one, out, scratch, two_f32):
+def first_kernel(
+    one_hbm, two_hbm, three_hbm, owner_hbm, tiles_hbm, u_three_hbm, u_two_hbm, u_one_hbm, out,
+    one, two, three, owner, tiles, u_three, u_two, u_one, scratch, two_f32, sems,
+):
     count, width = tiles.shape[:2]
     rank = u_three.shape[0]
     half = LANES // 2
     group = LANES // rank
     span = group * width
+    moves = [(three_hbm, three), (u_three_hbm, u_three)]
+    moves += [(tiles_hbm.at[t], tiles.at[t]) for t in range(count)]
+    moves += [(u_two_hbm, u_two), (u_one_hbm, u_one)]
+    moves += [(two_hbm, two), (one_hbm, one), (owner_hbm, owner)]
+    copies = [pltpu.make_async_copy(a, b, sems.at[i]) for i, (a, b) in enumerate(moves)]
+    for copy in copies:
+        copy.start()
+    copies[0].wait()
+    copies[1].wait()
     weights = []
     for t in range(count):
         block = three[t]
@@ -93,6 +107,8 @@
         full = jnp.concatenate([jnp.concatenate([both] * (span // LANES), axis=1)] * group, axis=0)
         keep = (row_iota(full.shape) // rank) == (lane_iota(full.shape) // width)
         weights.append(jnp.where(keep, full, 0.0).astype(BF16))
+    for copy in copies[2:]:
+        copy.wait()
     for g in range(tiles.shape[2] // span):
         parts = [nt(weights[t], tiles[t, :, g * span : (g + 1) * span]) for t in range(count)]
         scratch[g * LANES : (g + 1) * LANES, :] = jnp.concatenate(parts, axis=1)
@@ -194,19 +210,25 @@
     rows_total = owner_map.shape[0] * width
     smem = pl.BlockSpec(memory_space=pltpu.SMEM)
     vmem = pl.BlockSpec(memory_space=pltpu.VMEM)
-    params = pltpu.CompilerParams(vmem_limit_bytes=32 * 1024 * 1024)
+    wide = pltpu.CompilerParams(vmem_limit_bytes=WIDE)
+    narrow = pltpu.CompilerParams(vmem_limit_bytes=NARROW)
+    ints = (block_one, block_two, block_three, owner_map)
+    arrays = (tiles, u_three, u_two, u_one)
     sends = pl.pallas_call(
         first_kernel,
         out_shape=jax.ShapeDtypeStruct((rank, width + META, LANES), BF16),
-        in_specs=[smem] * 4 + [vmem] * 4,
+        in_specs=[pl.BlockSpec(memory_space=pltpu.HBM)] * 8,
         out_specs=vmem,
-        scratch_shapes=[
+        scratch_shapes=[pltpu.SMEM(x.shape, x.dtype) for x in ints]
+        + [pltpu.VMEM(x.shape, x.dtype) for x in arrays]
+        + [
             pltpu.VMEM((width * rank, LANES), F32),
             pltpu.VMEM(u_two.shape, F32),
+            pltpu.SemaphoreType.DMA((len(ints) + len(arrays) + count - 1,)),
         ],
-        compiler_params=params,
+        compiler_params=wide,
         name="first",
-    )(block_one, block_two, block_three, owner_map, tiles, u_three, u_two, u_one)
+    )(*ints, *arrays)
     got = lax.all_to_all(sends, ("tiles", "rep"), 0, 0, tiled=True)
     part = pl.pallas_call(
         functools.partial(rows_kernel, reps),
@@ -220,7 +242,7 @@
             pltpu.SMEM((size, LANES), jnp.int32),
             pltpu.VMEM((owners, rank, LANES), F32),
         ],
-        compiler_params=params,
+        compiler_params=narrow,
         name="rows_part",
     )(got)
     part = (part.astype(F32) + swap(part, size, 1).astype(F32)).astype(BF16)
@@ -239,7 +261,7 @@
         in_specs=[smem] * 2 + [vmem] * 4,
         out_specs=(vmem, vmem),
         scratch_shapes=[pltpu.VMEM((rank, rows_total), F32)],
-        compiler_params=params,
+        compiler_params=narrow,
         name="final",
     )(block_one, owner_map, *parts)
 

time: 52.7 us -> 48.3 us (0.917)
  local copies, waits for them, and re-layouts: 6.1 us -> 0.01 us
  Pallas kernels: 6.25 us -> 7.83 us
    unnamed x20 -> x4, local copies, waits for them, and re-layouts: 6.1 us -> 0.01 us
    pallas_call x1, Pallas kernels: 1.96 us -> 3.53 us  [sliced(): pl.pallas_call(first_kernel, out_shape=jax.ShapeDtypeStruct((rank, width...]
where the time goes in v2:
time: 48.3 us; the launch traced here: 48.1 us
  blocking collectives  25.2 us (52%)
  Pallas kernels  7.83 us (16%)
  starting transfers between devices  7.58 us (16%)
  waiting for transfers between devices  6.72 us (14%)
  between operations  0.67 us (1%)
    all_to_all x1, blocking collectives, sliced(): got = lax.all_to_all(sends, ('tiles', 'rep'), 0, 0, tiled=True)  25.2 us
    ppermute x7, starting transfers between devices, swap(): lax.ppermute(x, ('tiles', 'rep'), [(i, i ^ mask) for i in range(size)])  7.58 us
    ppermute x7, waiting for transfers between devices, swap(): lax.ppermute(x, ('tiles', 'rep'), [(i, i ^ mask) for i in range(size)])  6.72 us
    pallas_call x1, Pallas kernels, sliced(): pl.pallas_call(first_kernel, out_shape=jax.ShapeDtypeStruct((rank, width...  3.53 us
    pallas_call x1, Pallas kernels, sliced(): pl.pallas_call(final_kernel, out_shape=(jax.ShapeDtypeStruct(u_one.shape,...  2.29 us
    pallas_call x1, Pallas kernels, sliced(): pl.pallas_call(functools.partial(rows_kernel, reps), out_shape=jax.ShapeD...  2.02 us
  transfers between devices with their start and end apart: 7, of which 6 were waited for; matrix products, arithmetic and copies ran while one was open for 0% of the time, Pallas kernels for 0%

profile of v2, /device:TPU:0, one launch (start us, length us, event | category | flops | bytes accessed | tf_op | source)
XLA Modules:
  0.0 48.1 jit_solution(11408991363187580391)
XLA Ops:
  0.6 3.5 %first.1 = bf16[32,80,128]{2,1,0:T(8,128)(2,1)} custom-call(s32[2]{0:T(128)} %one.1, s32[2]{0:T(128)} %two_hbm.1, s32[2]{0:T(128)} %three_hbm.1, s32[8]{0:T(128)} %owner.1, bf16[2,64,4096]{2,1,0:T(8,128)(2,1)} %tiles_hbm.1, bf16[32,1024]{1,0:T(8,128)(2,1)} %u_three_hbm.1, bf16[32,128]{1,0:T(8,128)(2,1)} %u_two_hbm.1, f32[32,64]{1,0:T(8,128)} %u_one_hbm.1), custom_call_target="tpu_custom_call" | custom-call | tf_op jit(solution)/shard_map/first/pallas_call | solution.py:217
  4.2 25.2 %all_to_all.5.got = bf16[32,80,128]{2,1,0:T(8,128)(2,1)S(1)} all-to-all(bf16[32,80,128]{2,1,0:T(8,128)(2,1)} %first.1), channel_id=1, replica_groups=mesh['tiles'=8,'rep'=4] {'tiles','rep'}, dimensions={0} | all-to-all | bytes 1310720 | tf_op jit(solution)/shard_map/all_to_all | solution.py:232
  29.4 2.0 %rows_part.1 = bf16[32,512]{1,0:T(8,128)(2,1)S(1)} custom-call(bf16[32,80,128]{2,1,0:T(8,128)(2,1)S(1)} %all_to_all.5.got), custom_call_target="tpu_custom_call" | custom-call | tf_op jit(solution)/shard_map/rows_part/pallas_call | solution.py:233
  31.4 0.1 collective-permute-start
  31.5 1.1 %collective-permute-done = bf16[32,512]{1,0:T(8,128)(2,1)S(1)} collective-permute-done((bf16[32,512]{1,0:T(8,128)(2,1)S(1)}, bf16[32,512]{1,0:T(8,128)(2,1)S(1)}, u32[]{:S(2)}, u32[]{:S(2)}) %collective-permute-start) | collective-permute-done | bytes 32800 | tf_op jit(solution)/shard_map/ppermute | solution.py:201
  32.7 0.0 copy-start
  32.7 0.0 copy-start.1
  32.7 2.4 %collective-permute-start.3 = (bf16[32,512]{1,0:T(8,128)(2,1)S(1)}, bf16[32,512]{1,0:T(8,128)(2,1)S(1)}, u32[]{:S(2)}, u32[]{:S(2)}) collective-permute-start(bf16[32,512]{1,0:T(8,128)(2,1)S(1)} %add_convert_fusion.1), channel_id=1, source_target_pairs={{0,6},{1,7},{2,4},{3,5},{4,2},{5,3},{6,0},{7,1},{8,14},{9,15},{10,... | collective-permute-start | bytes 98312 | tf_op jit(solution)/shard_map/ppermute | solution.py:201
  35.1 0.2 collective-permute-start.2
  35.2 0.8 %collective-permute-start.1 = (bf16[32,512]{1,0:T(8,128)(2,1)S(1)}, bf16[32,512]{1,0:T(8,128)(2,1)S(1)}, u32[]{:S(2)}, u32[]{:S(2)}) collective-permute-start(bf16[32,512]{1,0:T(8,128)(2,1)S(1)} %add_convert_fusion.1), channel_id=1, source_target_pairs={{0,3},{1,2},{2,1},{3,0},{4,7},{5,6},{6,5},{7,4},{8,11},{9,10},{10,... | collective-permute-start | bytes 98312 | tf_op jit(solution)/shard_map/ppermute | solution.py:201
  36.0 1.6 %collective-permute-done.3 = bf16[32,512]{1,0:T(8,128)(2,1)S(1)} collective-permute-done((bf16[32,512]{1,0:T(8,128)(2,1)S(1)}, bf16[32,512]{1,0:T(8,128)(2,1)S(1)}, u32[]{:S(2)}, u32[]{:S(2)}) %collective-permute-start.3) | collective-permute-done | bytes 32800 | tf_op jit(solution)/shard_map/ppermute | solution.py:201
  37.6 1.1 %collective-permute-done.2 = bf16[32,512]{1,0:T(8,128)(2,1)S(1)} collective-permute-done((bf16[32,512]{1,0:T(8,128)(2,1)S(1)}, bf16[32,512]{1,0:T(8,128)(2,1)S(1)}, u32[]{:S(2)}, u32[]{:S(2)}) %collective-permute-start.2) | collective-permute-done | bytes 32800 | tf_op jit(solution)/shard_map/ppermute | solution.py:201
  38.7 0.0 collective-permute-done.1
  38.7 1.5 %collective-permute-start.6 = (bf16[32,512]{1,0:T(8,128)(2,1)S(1)}, bf16[32,512]{1,0:T(8,128)(2,1)S(1)}, u32[]{:S(2)}, u32[]{:S(2)}) collective-permute-start(bf16[32,512]{1,0:T(8,128)(2,1)S(1)} %add_convert_fusion.a), channel_id=1, source_target_pairs={{0,24},{1,25},{2,26},{3,27},{4,28},{5,29},{6,30},{7,31},{8,16},{9,... | collective-permute-start | bytes 98312 | tf_op jit(solution)/shard_map/ppermute | solution.py:201
  40.2 0.4 collective-permute-start.5
  40.7 2.2 %collective-permute-start.4 = (bf16[32,512]{1,0:T(8,128)(2,1)S(1)}, bf16[32,512]{1,0:T(8,128)(2,1)S(1)}, u32[]{:S(2)}, u32[]{:S(2)}) collective-permute-start(bf16[32,512]{1,0:T(8,128)(2,1)S(1)} %add_convert_fusion.a), channel_id=1, source_target_pairs={{0,9},{1,8},{2,11},{3,10},{4,13},{5,12},{6,15},{7,14},{8,1},{9,0},... | collective-permute-start | bytes 98312 | tf_op jit(solution)/shard_map/ppermute | solution.py:201
  42.9 1.8 %collective-permute-done.6.d = bf16[32,512]{1,0:T(8,128)(2,1)S(1)} collective-permute-done((bf16[32,512]{1,0:T(8,128)(2,1)S(1)}, bf16[32,512]{1,0:T(8,128)(2,1)S(1)}, u32[]{:S(2)}, u32[]{:S(2)}) %collective-permute-start.6) | collective-permute-done | bytes 32800 | tf_op jit(solution)/shard_map/ppermute | solution.py:201
  44.7 1.0 %collective-permute-done.5.c = bf16[32,512]{1,0:T(8,128)(2,1)S(1)} collective-permute-done((bf16[32,512]{1,0:T(8,128)(2,1)S(1)}, bf16[32,512]{1,0:T(8,128)(2,1)S(1)}, u32[]{:S(2)}, u32[]{:S(2)}) %collective-permute-start.5) | collective-permute-done | bytes 32800 | tf_op jit(solution)/shard_map/ppermute | solution.py:201
  45.7 0.1 collective-permute-done.4.b
  45.8 0.0 copy-done
  45.8 0.0 copy-done.1
  45.8 2.3 %final.1 = (f32[32,64]{1,0:T(8,128)}, bf16[2,2048]{1,0:T(2,128)(2,1)}) custom-call(s32[2]{0:T(128)S(1)} %copy-done, s32[8]{0:T(128)S(1)} %copy-done.1, bf16[32,512]{1,0:T(8,128)(2,1)S(1)} %add_convert_fusion.a, bf16[32,512]{1,0:T(8,128)(2,1)S(1)} %collective-permute-done.4.b, bf16[32,512]{1,0:T(8,128)(2,1)S(1)} %collective-permute-done.5.c, ...), custom_call_target="tpu_custom_call" | custom-call | tf_op jit(solution)/shard_map/final/pallas_call | solution.py:255
  (2 shorter events, 0.0 us)
Async XLA Ops:
  31.4 1.2 %collective-permute-start = (bf16[32,512]{1,0:T(8,128)(2,1)S(1)}, bf16[32,512]{1,0:T(8,128)(2,1)S(1)}, u32[]{:S(2)}, u32[]{:S(2)}) collective-permute-start(bf16[32,512]{1,0:T(8,128)(2,1)S(1)} %rows_part.1), channel_id=1, source_target_pairs={{0,1},{1,0},{2,3},{3,2},{4,5},{5,4},{6,7},{7,6},{8,9},{9,8},{10,11... | collective-permute-start | bytes 98312 | tf_op jit(solution)/shard_map/ppermute | solution.py:201
  32.7 13.1 %copy-start = (s32[2]{0:T(128)S(1)}, s32[2]{0:T(128)}, u32[]{:S(2)}) copy-start(s32[2]{0:T(128)} %one.1) | copy-start | bytes 28
  32.7 13.1 %copy-start.1 = (s32[8]{0:T(128)S(1)}, s32[8]{0:T(128)}, u32[]{:S(2)}) copy-start(s32[8]{0:T(128)} %owner.1) | copy-start | bytes 100
  32.7 4.9 %collective-permute-start.3 = (bf16[32,512]{1,0:T(8,128)(2,1)S(1)}, bf16[32,512]{1,0:T(8,128)(2,1)S(1)}, u32[]{:S(2)}, u32[]{:S(2)}) collective-permute-start(bf16[32,512]{1,0:T(8,128)(2,1)S(1)} %add_convert_fusion.1), channel_id=1, source_target_pairs={{0,6},{1,7},{2,4},{3,5},{4,2},{5,3},{6,0},{7,1},{8,14},{9,15},{10,... | collective-permute-start | bytes 98312 | tf_op jit(solution)/shard_map/ppermute | solution.py:201
  35.1 3.6 %collective-permute-start.2 = (bf16[32,512]{1,0:T(8,128)(2,1)S(1)}, bf16[32,512]{1,0:T(8,128)(2,1)S(1)}, u32[]{:S(2)}, u32[]{:S(2)}) collective-permute-start(bf16[32,512]{1,0:T(8,128)(2,1)S(1)} %add_convert_fusion.1), channel_id=1, source_target_pairs={{0,5},{1,4},{2,7},{3,6},{4,1},{5,0},{6,3},{7,2},{8,13},{9,12},{10,... | collective-permute-start | bytes 98312 | tf_op jit(solution)/shard_map/ppermute | solution.py:201
  35.2 3.5 %collective-permute-start.1 = (bf16[32,512]{1,0:T(8,128)(2,1)S(1)}, bf16[32,512]{1,0:T(8,128)(2,1)S(1)}, u32[]{:S(2)}, u32[]{:S(2)}) collective-permute-start(bf16[32,512]{1,0:T(8,128)(2,1)S(1)} %add_convert_fusion.1), channel_id=1, source_target_pairs={{0,3},{1,2},{2,1},{3,0},{4,7},{5,6},{6,5},{7,4},{8,11},{9,10},{10,... | collective-permute-start | bytes 98312 | tf_op jit(solution)/shard_map/ppermute | solution.py:201
  38.7 6.0 %collective-permute-start.6 = (bf16[32,512]{1,0:T(8,128)(2,1)S(1)}, bf16[32,512]{1,0:T(8,128)(2,1)S(1)}, u32[]{:S(2)}, u32[]{:S(2)}) collective-permute-start(bf16[32,512]{1,0:T(8,128)(2,1)S(1)} %add_convert_fusion.a), channel_id=1, source_target_pairs={{0,24},{1,25},{2,26},{3,27},{4,28},{5,29},{6,30},{7,31},{8,16},{9,... | collective-permute-start | bytes 98312 | tf_op jit(solution)/shard_map/ppermute | solution.py:201
  40.2 5.4 %collective-permute-start.5 = (bf16[32,512]{1,0:T(8,128)(2,1)S(1)}, bf16[32,512]{1,0:T(8,128)(2,1)S(1)}, u32[]{:S(2)}, u32[]{:S(2)}) collective-permute-start(bf16[32,512]{1,0:T(8,128)(2,1)S(1)} %add_convert_fusion.a), channel_id=1, source_target_pairs={{0,17},{1,16},{2,19},{3,18},{4,21},{5,20},{6,23},{7,22},{8,25},{9,... | collective-permute-start | bytes 98312 | tf_op jit(solution)/shard_map/ppermute | solution.py:201
  40.7 5.1 %collective-permute-start.4 = (bf16[32,512]{1,0:T(8,128)(2,1)S(1)}, bf16[32,512]{1,0:T(8,128)(2,1)S(1)}, u32[]{:S(2)}, u32[]{:S(2)}) collective-permute-start(bf16[32,512]{1,0:T(8,128)(2,1)S(1)} %add_convert_fusion.a), channel_id=1, source_target_pairs={{0,9},{1,8},{2,11},{3,10},{4,13},{5,12},{6,15},{7,14},{8,1},{9,0},... | collective-permute-start | bytes 98312 | tf_op jit(solution)/shard_map/ppermute | solution.py:201

commit v3 on v2

--- a/solution.py
+++ b/solution.py
@@ -10,7 +10,6 @@
 NS_STEPS = 2
 HI = lax.Precision.HIGHEST
 LANES = 128
-WIDE = 60 * 1024 * 1024
 NARROW = 16 * 1024 * 1024
 META = 16
 F32 = jnp.float32
@@ -65,6 +64,18 @@
     return (factor, tile_factor)
 
 
+def split(a):
+    high = a.astype(BF16)
+    return high, (a - high.astype(F32)).astype(BF16)
+
+
+def dot3(a, b, axis=0):
+    (ah, al), (bh, bl) = split(a), split(b)
+    left = jnp.concatenate([ah, al, ah], axis=1)
+    right = jnp.concatenate([bh, bh, bl], axis=axis)
+    return lax.dot_general(left, right, (((1,), (axis,)), ((), ())), preferred_element_type=F32)
+
+
 def lane_iota(shape):
     return lax.broadcasted_iota(jnp.int32, shape, len(shape) - 1)
 
@@ -81,19 +92,21 @@
 
 def first_kernel(
     one_hbm, two_hbm, three_hbm, owner_hbm, tiles_hbm, u_three_hbm, u_two_hbm, u_one_hbm, out,
-    one, two, three, owner, tiles, u_three, u_two, u_one, scratch, two_f32, sems,
+    one, two, three, owner, tiles, u_three, u_two, u_one, two_f32, in_sems, tile_sems,
 ):
     count, width = tiles.shape[:2]
     rank = u_three.shape[0]
     half = LANES // 2
-    group = LANES // rank
-    span = group * width
-    moves = [(three_hbm, three), (u_three_hbm, u_three)]
-    moves += [(tiles_hbm.at[t], tiles.at[t]) for t in range(count)]
-    moves += [(u_two_hbm, u_two), (u_one_hbm, u_one)]
-    moves += [(two_hbm, two), (one_hbm, one), (owner_hbm, owner)]
-    copies = [pltpu.make_async_copy(a, b, sems.at[i]) for i, (a, b) in enumerate(moves)]
-    for copy in copies:
+    share = META // 2
+    span = share * width
+    pieces = tiles.shape[2] // (2 * span)
+    moves = [(three_hbm, three), (u_three_hbm, u_three), (two_hbm, two), (one_hbm, one)]
+    moves += [(owner_hbm, owner), (u_two_hbm, u_two), (u_one_hbm, u_one)]
+    copies = [pltpu.make_async_copy(a, b, in_sems.at[i]) for i, (a, b) in enumerate(moves)]
+    loads = [
+        pltpu.make_async_copy(tiles_hbm.at[t], tiles.at[t], tile_sems.at[t]) for t in range(count)
+    ]
+    for copy in copies[:2] + loads + copies[2:]:
         copy.start()
     copies[0].wait()
     copies[1].wait()
@@ -104,16 +117,25 @@
         window = u_three[:, pl.ds(start, LANES)].astype(F32)
         same = (lane_iota(window.shape) // half) == (block % 2)
         both = jnp.where(same, window, pltpu.roll(window, half, 1))
-        full = jnp.concatenate([jnp.concatenate([both] * (span // LANES), axis=1)] * group, axis=0)
-        keep = (row_iota(full.shape) // rank) == (lane_iota(full.shape) // width)
+        tall = jnp.broadcast_to(both[:, None, :], (rank, share, LANES)).reshape(rank * share, LANES)
+        full = jnp.concatenate([tall] * (span // LANES), axis=1)
+        keep = (row_iota(full.shape) % share) == (lane_iota(full.shape) // width)
         weights.append(jnp.where(keep, full, 0.0).astype(BF16))
+    for copy in loads:
+        copy.wait()
+    for n in range(pieces):
+        pair = []
+        for g in (2 * n, 2 * n + 1):
+            columns = slice(g * span, (g + 1) * span)
+            pair.append([nt(weights[t], tiles[t, :, columns]) for t in range(count)])
+        rows = slice(2 * n * share, 2 * (n + 1) * share)
+        for s in range(rank):
+            at = slice(s * share, (s + 1) * share)
+            block = [jnp.concatenate([part[at] for part in parts], axis=1) for parts in pair]
+            out[s, rows, :] = jnp.concatenate(block, axis=0).astype(BF16)
+
     for copy in copies[2:]:
         copy.wait()
-    for g in range(tiles.shape[2] // span):
-        parts = [nt(weights[t], tiles[t, :, g * span : (g + 1) * span]) for t in range(count)]
-        scratch[g * LANES : (g + 1) * LANES, :] = jnp.concatenate(parts, axis=1)
-
-    share = META // 2
     q = lax.axis_index("rep")
     two_f32[...] = u_two[...].astype(F32)
     top = two_f32[pl.ds(pl.multiple_of(q * share, share), share), :]
@@ -124,12 +146,12 @@
         ints = jnp.where(lane == t, two[t].astype(F32), ints)
         ints = jnp.where(lane == count + t, owner[one[t]].astype(F32), ints)
     meta = jnp.concatenate([top, jnp.concatenate([low, ints], axis=1)], axis=0).astype(BF16)
+    rows = slice(width, width + META)
     for s in range(rank):
-        out[s, 0:width, :] = scratch[pl.ds(s, width, stride=rank), :].astype(BF16)
-        out[s, width : width + META, :] = meta
-
-
-def rows_kernel(reps, got, out, two, one, ints, ints_smem, total):
+        out[s, rows, :] = meta
+
+
+def rows_kernel(reps, got, out, two, one, total):
     sources, depth = got.shape[:2]
     width = depth - META
     half = LANES // 2
@@ -137,61 +159,76 @@
     rank = share * reps
     count = LANES // width
     owners = sources // reps
+    blocks = 2 * owners
+    lines = []
     for src in range(sources):
         t, q = divmod(src, reps)
         meta = got[src, width:depth, :].astype(F32)
         two[t, q * share : (q + 1) * share, :] = meta[:share]
         one[t, q * share : (q + 1) * share, :] = meta[share:]
-        ints[src : src + 1, :] = meta[share : share + 1].astype(jnp.int32)
-    pltpu.sync_copy(ints, ints_smem)
+        lines.append(meta[share : share + 1])
+    lines = jnp.concatenate(lines, axis=0)
+    lane = lane_iota(lines.shape)
+    scale = jnp.zeros(lines.shape, F32)
+    for k in range(2 * count):
+        scale = jnp.where(lane == half + k, float(blocks**k), scale)
+    code = jnp.sum(lines * scale, axis=1, keepdims=True).astype(jnp.int32)
     total[...] = jnp.zeros_like(total)
     lane = lane_iota((rank, LANES))
     for src in range(sources):
         block = got[src, 0:width, :]
         moving = jnp.concatenate([block, block], axis=0)
+        left = code[src, 0]
+        digits = []
+        for _ in range(2 * count):
+            digits.append(left % blocks)
+            left = left // blocks
         picks = []
-        for t in range(count):
-            b = ints_smem[src, half + t]
+        for b in digits[:count]:
             picks.append(jnp.where((lane // half) == (b % 2), two[b // 2], 0.0))
         stacked = jnp.concatenate(picks, axis=0).astype(BF16)
-        product = jnp.dot(stacked, moving, preferred_element_type=F32)
-        for t in range(count):
-            p = ints_smem[src, half + count + t]
-            mine = product[t * rank : (t + 1) * rank].astype(BF16).astype(F32)
-            total[p] += jnp.where((lane // width) == t, mine, 0.0)
+        product = jnp.dot(stacked, moving, preferred_element_type=F32).astype(BF16).astype(F32)
+        for t, p in enumerate(digits[count:]):
+            total[t, src % 2, p] += product[t * rank : (t + 1) * rank]
     sums = []
     for p in range(owners):
-        value = total[p]
-        sums.append((value + pltpu.roll(value, half, 1))[:, :half])
+        low = (total[0, 0, p] + total[0, 1, p])[:, :half]
+        high = pltpu.roll(total[1, 0, p] + total[1, 1, p], half, 1)[:, :half]
+        sums.append(low + high)
     table = jnp.concatenate(sums, axis=1)
-    readers = jnp.concatenate([one[p][:, :half] for p in range(owners)], axis=1)
-    project = nt(readers, table, HI).astype(BF16).astype(F32)
-    out[...] = jnp.dot(project, table, precision=HI, preferred_element_type=F32).astype(BF16)
+    high = table.astype(BF16)
+    low = (table - high.astype(F32)).astype(BF16)
+    readers = jnp.concatenate([one[p][:, :half] for p in range(owners)], axis=1).astype(BF16)
+    project = (nt(readers, high) + nt(readers, low)).astype(BF16)
+    part = jnp.dot(project, high, preferred_element_type=F32)
+    part += jnp.dot(project, low, preferred_element_type=F32)
+    out[...] = part.astype(BF16)
 
 
 def final_kernel(one, owner, a, b, c, d, factor, tile_factor, table):
     rank, rows_total = a.shape
     half = LANES // 2
     rows = (a[...].astype(F32) + b[...].astype(F32)) + (c[...].astype(F32) + d[...].astype(F32))
-    g0 = nt(rows, rows, HI)
+    table[...] = rows
+    g0 = dot3(rows, rows, 1)
     eye = (row_iota(g0.shape) == lane_iota(g0.shape)).astype(F32)
     msq = jnp.sum(g0 * eye, keepdims=True) / rows_total
     inv = 1.0 / jnp.sqrt(msq + 1e-06)
-    x = rows * inv
     g = g0 * (inv * inv) / rows_total
-    for step in range(NS_STEPS):
-        if step > 0:
-            g = nt(x, x, HI) / rows_total
-        x = jnp.dot(1.5 * eye - 0.5 * g, x, precision=HI, preferred_element_type=F32)
-    table[...] = x
+    square = dot3(g, g)
+    outer = dot3(square, 0.0625 * square - 0.5625 * g)
+    step = (outer + (1.6875 * square - 2.4375 * g + 2.25 * eye)) * inv
 
     def block(p):
         window = table[:, pl.ds(pl.multiple_of((p // 2) * LANES, LANES), LANES)]
         return jnp.where(p % 2 == 1, pltpu.roll(window, half, 1), window)[:, :half]
 
-    factor[...] = block(lax.axis_index("tiles"))
+    places = [lax.axis_index("tiles")] + [owner[one[t]] for t in range(tile_factor.shape[0])]
+    picked = jnp.concatenate([block(p) for p in places], axis=1)
+    x = dot3(step, picked)
+    factor[...] = x[:, :half]
     for t in range(tile_factor.shape[0]):
-        value = block(owner[one[t]])
+        value = x[:, (t + 1) * half : (t + 2) * half]
         for r in range(0, rank, 2):
             line = jnp.concatenate([value[r : r + 1], value[r + 1 : r + 2]], axis=1)
             tile_factor[t : t + 1, r * half : (r + 2) * half] = line.astype(BF16)
@@ -210,7 +247,6 @@
     rows_total = owner_map.shape[0] * width
     smem = pl.BlockSpec(memory_space=pltpu.SMEM)
     vmem = pl.BlockSpec(memory_space=pltpu.VMEM)
-    wide = pltpu.CompilerParams(vmem_limit_bytes=WIDE)
     narrow = pltpu.CompilerParams(vmem_limit_bytes=NARROW)
     ints = (block_one, block_two, block_three, owner_map)
     arrays = (tiles, u_three, u_two, u_one)
@@ -222,13 +258,13 @@
         scratch_shapes=[pltpu.SMEM(x.shape, x.dtype) for x in ints]
         + [pltpu.VMEM(x.shape, x.dtype) for x in arrays]
         + [
-            pltpu.VMEM((width * rank, LANES), F32),
             pltpu.VMEM(u_two.shape, F32),
-            pltpu.SemaphoreType.DMA((len(ints) + len(arrays) + count - 1,)),
+            pltpu.SemaphoreType.DMA((7,)),
+            pltpu.SemaphoreType.DMA((count,)),
         ],
-        compiler_params=wide,
+        compiler_params=narrow,
         name="first",
-    )(*ints, *arrays)
+    )(*[pltpu.with_memory_space_constraint(x, pltpu.HBM) for x in ints + arrays])
     got = lax.all_to_all(sends, ("tiles", "rep"), 0, 0, tiled=True)
     part = pl.pallas_call(
         functools.partial(rows_kernel, reps),
@@ -238,9 +274,7 @@
         scratch_shapes=[
             pltpu.VMEM((owners, rank, LANES), F32),
             pltpu.VMEM((owners, rank, LANES), F32),
-            pltpu.VMEM((size, LANES), jnp.int32),
-            pltpu.SMEM((size, LANES), jnp.int32),
-            pltpu.VMEM((owners, rank, LANES), F32),
+            pltpu.VMEM((count, 2, owners, rank, LANES), F32),
         ],
         compiler_params=narrow,
         name="rows_part",
@@ -250,7 +284,7 @@
     pair = part.astype(F32) + swap(part, size, m | 1).astype(F32)
     other = swap(part, size, n | 1).astype(F32) + swap(part, size, m ^ n).astype(F32)
     part = (pair + other).astype(BF16)
-    m, n = 8, 16
+    m, n = 16, 8
     parts = [part, swap(part, size, m | 1), swap(part, size, n | 1), swap(part, size, m ^ n)]
     return pl.pallas_call(
         final_kernel,

time: 48.3 us -> 46.1 us (0.954)
  Pallas kernels: 7.83 us -> 6.48 us
  waiting for transfers between devices: 6.72 us -> 6.08 us
    pallas_call x1, Pallas kernels: 3.53 us -> 2.76 us  [sliced(): pl.pallas_call(first_kernel, out_shape=jax.ShapeDtypeStruct((rank, width...]
    ppermute x7, waiting for transfers between devices: 6.72 us -> 6.08 us  [swap(): lax.ppermute(x, ('tiles', 'rep'), [(i, i ^ mask) for i in range(size)])]
  transfers between devices with their start and end apart: 7 -> 7, of which waited for: 6 -> 5; matrix products, arithmetic and copies ran while one was open for 0% -> 0% of each run, Pallas kernels for 0% -> 0%
where the time goes in v3:
time: 46.1 us; the launch traced here: 45.9 us
  blocking collectives  25 us (54%)
  starting transfers between devices  7.6 us (16%)
  Pallas kernels  6.48 us (14%)
  waiting for transfers between devices  6.08 us (13%)
  between operations  0.68 us (1%)
    all_to_all x1, blocking collectives, sliced(): got = lax.all_to_all(sends, ('tiles', 'rep'), 0, 0, tiled=True)  25 us
    ppermute x7, starting transfers between devices, swap(): lax.ppermute(x, ('tiles', 'rep'), [(i, i ^ mask) for i in range(size)])  7.6 us
    ppermute x7, waiting for transfers between devices, swap(): lax.ppermute(x, ('tiles', 'rep'), [(i, i ^ mask) for i in range(size)])  6.08 us
    pallas_call x1, Pallas kernels, sliced(): pl.pallas_call(first_kernel, out_shape=jax.ShapeDtypeStruct((rank, width...  2.76 us
    pallas_call x1, Pallas kernels, sliced(): pl.pallas_call(final_kernel, out_shape=(jax.ShapeDtypeStruct(u_one.shape,...  2.12 us
    pallas_call x1, Pallas kernels, sliced(): pl.pallas_call(functools.partial(rows_kernel, reps), out_shape=jax.ShapeD...  1.59 us
  transfers between devices with their start and end apart: 7, of which 5 were waited for; matrix products, arithmetic and copies ran while one was open for 0% of the time, Pallas kernels for 0%

profile of v3, /device:TPU:0, one launch (start us, length us, event | category | flops | bytes accessed | tf_op | source)
XLA Modules:
  0.0 45.9 jit_solution(8719981422150981033)
XLA Ops:
  0.6 2.8 %first.1 = bf16[32,80,128]{2,1,0:T(8,128)(2,1)S(1)} custom-call(s32[2]{0:T(128)} %one.1, s32[2]{0:T(128)} %two_hbm.1, s32[2]{0:T(128)} %three_hbm.1, s32[8]{0:T(128)} %owner.1, bf16[2,64,4096]{2,1,0:T(8,128)(2,1)} %tiles_hbm.1, bf16[32,1024]{1,0:T(8,128)(2,1)} %u_three_hbm.1, bf16[32,128]{1,0:T(8,128)(2,1)} %u_two_hbm.1, f32[32,64]{1,0:T(8,128)} %u_one_hbm.1), custom_call_target="tpu_custom_call" | custom-call | tf_op jit(solution)/shard_map/first/pallas_call | solution.py:253
  3.4 25.0 %all_to_all.5.got = bf16[32,80,128]{2,1,0:T(8,128)(2,1)S(1)} all-to-all(bf16[32,80,128]{2,1,0:T(8,128)(2,1)S(1)} %first.1), channel_id=1, replica_groups=mesh['tiles'=8,'rep'=4] {'tiles','rep'}, dimensions={0} | all-to-all | bytes 1310720 | tf_op jit(solution)/shard_map/all_to_all | solution.py:268
  28.4 1.6 %rows_part.1 = bf16[32,512]{1,0:T(8,128)(2,1)S(1)} custom-call(bf16[32,80,128]{2,1,0:T(8,128)(2,1)S(1)} %all_to_all.5.got), custom_call_target="tpu_custom_call" | custom-call | tf_op jit(solution)/shard_map/rows_part/pallas_call | solution.py:269
  30.0 0.1 collective-permute-start
  30.2 1.1 %collective-permute-done = bf16[32,512]{1,0:T(8,128)(2,1)S(1)} collective-permute-done((bf16[32,512]{1,0:T(8,128)(2,1)S(1)}, bf16[32,512]{1,0:T(8,128)(2,1)S(1)}, u32[]{:S(2)}, u32[]{:S(2)}) %collective-permute-start) | collective-permute-done | bytes 32800 | tf_op jit(solution)/shard_map/ppermute | solution.py:238
  31.3 0.0 copy-start
  31.3 0.0 copy-start.1
  31.3 2.4 %collective-permute-start.3 = (bf16[32,512]{1,0:T(8,128)(2,1)S(1)}, bf16[32,512]{1,0:T(8,128)(2,1)S(1)}, u32[]{:S(2)}, u32[]{:S(2)}) collective-permute-start(bf16[32,512]{1,0:T(8,128)(2,1)S(1)} %add_convert_fusion.1), channel_id=1, source_target_pairs={{0,6},{1,7},{2,4},{3,5},{4,2},{5,3},{6,0},{7,1},{8,14},{9,15},{10,... | collective-permute-start | bytes 98312 | tf_op jit(solution)/shard_map/ppermute | solution.py:238
  33.7 0.2 collective-permute-start.2
  33.9 0.8 %collective-permute-start.1 = (bf16[32,512]{1,0:T(8,128)(2,1)S(1)}, bf16[32,512]{1,0:T(8,128)(2,1)S(1)}, u32[]{:S(2)}, u32[]{:S(2)}) collective-permute-start(bf16[32,512]{1,0:T(8,128)(2,1)S(1)} %add_convert_fusion.1), channel_id=1, source_target_pairs={{0,3},{1,2},{2,1},{3,0},{4,7},{5,6},{6,5},{7,4},{8,11},{9,10},{10,... | collective-permute-start | bytes 98312 | tf_op jit(solution)/shard_map/ppermute | solution.py:238
  34.6 1.6 %collective-permute-done.3 = bf16[32,512]{1,0:T(8,128)(2,1)S(1)} collective-permute-done((bf16[32,512]{1,0:T(8,128)(2,1)S(1)}, bf16[32,512]{1,0:T(8,128)(2,1)S(1)}, u32[]{:S(2)}, u32[]{:S(2)}) %collective-permute-start.3) | collective-permute-done | bytes 32800 | tf_op jit(solution)/shard_map/ppermute | solution.py:238
  36.2 1.1 %collective-permute-done.2 = bf16[32,512]{1,0:T(8,128)(2,1)S(1)} collective-permute-done((bf16[32,512]{1,0:T(8,128)(2,1)S(1)}, bf16[32,512]{1,0:T(8,128)(2,1)S(1)}, u32[]{:S(2)}, u32[]{:S(2)}) %collective-permute-start.2) | collective-permute-done | bytes 32800 | tf_op jit(solution)/shard_map/ppermute | solution.py:238
  37.3 0.0 collective-permute-done.1
  37.3 1.5 %collective-permute-start.6 = (bf16[32,512]{1,0:T(8,128)(2,1)S(1)}, bf16[32,512]{1,0:T(8,128)(2,1)S(1)}, u32[]{:S(2)}, u32[]{:S(2)}) collective-permute-start(bf16[32,512]{1,0:T(8,128)(2,1)S(1)} %add_convert_fusion.a), channel_id=1, source_target_pairs={{0,24},{1,25},{2,26},{3,27},{4,28},{5,29},{6,30},{7,31},{8,16},{9,... | collective-permute-start | bytes 98312 | tf_op jit(solution)/shard_map/ppermute | solution.py:238
  38.9 0.0 collective-permute-start.5
  38.9 2.7 %collective-permute-start.4 = (bf16[32,512]{1,0:T(8,128)(2,1)S(1)}, bf16[32,512]{1,0:T(8,128)(2,1)S(1)}, u32[]{:S(2)}, u32[]{:S(2)}) collective-permute-start(bf16[32,512]{1,0:T(8,128)(2,1)S(1)} %add_convert_fusion.a), channel_id=1, source_target_pairs={{0,17},{1,16},{2,19},{3,18},{4,21},{5,20},{6,23},{7,22},{8,25},{9,... | collective-permute-start | bytes 98312 | tf_op jit(solution)/shard_map/ppermute | solution.py:238
  41.5 1.8 %collective-permute-done.6.d = bf16[32,512]{1,0:T(8,128)(2,1)S(1)} collective-permute-done((bf16[32,512]{1,0:T(8,128)(2,1)S(1)}, bf16[32,512]{1,0:T(8,128)(2,1)S(1)}, u32[]{:S(2)}, u32[]{:S(2)}) %collective-permute-start.6) | collective-permute-done | bytes 32800 | tf_op jit(solution)/shard_map/ppermute | solution.py:238
  43.3 0.0 collective-permute-done.5.c
  43.3 0.5 %collective-permute-done.4.b = bf16[32,512]{1,0:T(8,128)(2,1)S(1)} collective-permute-done((bf16[32,512]{1,0:T(8,128)(2,1)S(1)}, bf16[32,512]{1,0:T(8,128)(2,1)S(1)}, u32[]{:S(2)}, u32[]{:S(2)}) %collective-permute-start.4) | collective-permute-done | bytes 32800 | tf_op jit(solution)/shard_map/ppermute | solution.py:238
  43.8 0.0 copy-done
  43.8 0.0 copy-done.1
  43.8 2.1 %final.1 = (f32[32,64]{1,0:T(8,128)}, bf16[2,2048]{1,0:T(2,128)(2,1)}) custom-call(s32[2]{0:T(128)S(1)} %copy-done, s32[8]{0:T(128)S(1)} %copy-done.1, bf16[32,512]{1,0:T(8,128)(2,1)S(1)} %add_convert_fusion.a, bf16[32,512]{1,0:T(8,128)(2,1)S(1)} %collective-permute-done.4.b, bf16[32,512]{1,0:T(8,128)(2,1)S(1)} %collective-permute-done.5.c, ...), custom_call_target="tpu_custom_call" | custom-call | tf_op jit(solution)/shard_map/final/pallas_call | solution.py:289
  (2 shorter events, 0.0 us)
Async XLA Ops:
  30.0 1.3 %collective-permute-start = (bf16[32,512]{1,0:T(8,128)(2,1)S(1)}, bf16[32,512]{1,0:T(8,128)(2,1)S(1)}, u32[]{:S(2)}, u32[]{:S(2)}) collective-permute-start(bf16[32,512]{1,0:T(8,128)(2,1)S(1)} %rows_part.1), channel_id=1, source_target_pairs={{0,1},{1,0},{2,3},{3,2},{4,5},{5,4},{6,7},{7,6},{8,9},{9,8},{10,11... | collective-permute-start | bytes 98312 | tf_op jit(solution)/shard_map/ppermute | solution.py:238
  31.3 12.5 %copy-start = (s32[2]{0:T(128)S(1)}, s32[2]{0:T(128)}, u32[]{:S(2)}) copy-start(s32[2]{0:T(128)} %one.1) | copy-start | bytes 28
  31.3 12.5 %copy-start.1 = (s32[8]{0:T(128)S(1)}, s32[8]{0:T(128)}, u32[]{:S(2)}) copy-start(s32[8]{0:T(128)} %owner.1) | copy-start | bytes 100
  31.3 4.9 %collective-permute-start.3 = (bf16[32,512]{1,0:T(8,128)(2,1)S(1)}, bf16[32,512]{1,0:T(8,128)(2,1)S(1)}, u32[]{:S(2)}, u32[]{:S(2)}) collective-permute-start(bf16[32,512]{1,0:T(8,128)(2,1)S(1)} %add_convert_fusion.1), channel_id=1, source_target_pairs={{0,6},{1,7},{2,4},{3,5},{4,2},{5,3},{6,0},{7,1},{8,14},{9,15},{10,... | collective-permute-start | bytes 98312 | tf_op jit(solution)/shard_map/ppermute | solution.py:238
  33.7 3.6 %collective-permute-start.2 = (bf16[32,512]{1,0:T(8,128)(2,1)S(1)}, bf16[32,512]{1,0:T(8,128)(2,1)S(1)}, u32[]{:S(2)}, u32[]{:S(2)}) collective-permute-start(bf16[32,512]{1,0:T(8,128)(2,1)S(1)} %add_convert_fusion.1), channel_id=1, source_target_pairs={{0,5},{1,4},{2,7},{3,6},{4,1},{5,0},{6,3},{7,2},{8,13},{9,12},{10,... | collective-permute-start | bytes 98312 | tf_op jit(solution)/shard_map/ppermute | solution.py:238
  33.9 3.5 %collective-permute-start.1 = (bf16[32,512]{1,0:T(8,128)(2,1)S(1)}, bf16[32,512]{1,0:T(8,128)(2,1)S(1)}, u32[]{:S(2)}, u32[]{:S(2)}) collective-permute-start(bf16[32,512]{1,0:T(8,128)(2,1)S(1)} %add_convert_fusion.1), channel_id=1, source_target_pairs={{0,3},{1,2},{2,1},{3,0},{4,7},{5,6},{6,5},{7,4},{8,11},{9,10},{10,... | collective-permute-start | bytes 98312 | tf_op jit(solution)/shard_map/ppermute | solution.py:238
  37.3 5.9 %collective-permute-start.6 = (bf16[32,512]{1,0:T(8,128)(2,1)S(1)}, bf16[32,512]{1,0:T(8,128)(2,1)S(1)}, u32[]{:S(2)}, u32[]{:S(2)}) collective-permute-start(bf16[32,512]{1,0:T(8,128)(2,1)S(1)} %add_convert_fusion.a), channel_id=1, source_target_pairs={{0,24},{1,25},{2,26},{3,27},{4,28},{5,29},{6,30},{7,31},{8,16},{9,... | collective-permute-start | bytes 98312 | tf_op jit(solution)/shard_map/ppermute | solution.py:238
  38.9 4.4 %collective-permute-start.5 = (bf16[32,512]{1,0:T(8,128)(2,1)S(1)}, bf16[32,512]{1,0:T(8,128)(2,1)S(1)}, u32[]{:S(2)}, u32[]{:S(2)}) collective-permute-start(bf16[32,512]{1,0:T(8,128)(2,1)S(1)} %add_convert_fusion.a), channel_id=1, source_target_pairs={{0,9},{1,8},{2,11},{3,10},{4,13},{5,12},{6,15},{7,14},{8,1},{9,0},... | collective-permute-start | bytes 98312 | tf_op jit(solution)/shard_map/ppermute | solution.py:238
  38.9 4.9 %collective-permute-start.4 = (bf16[32,512]{1,0:T(8,128)(2,1)S(1)}, bf16[32,512]{1,0:T(8,128)(2,1)S(1)}, u32[]{:S(2)}, u32[]{:S(2)}) collective-permute-start(bf16[32,512]{1,0:T(8,128)(2,1)S(1)} %add_convert_fusion.a), channel_id=1, source_target_pairs={{0,17},{1,16},{2,19},{3,18},{4,21},{5,20},{6,23},{7,22},{8,25},{9,... | collective-permute-start | bytes 98312 | tf_op jit(solution)/shard_map/ppermute | solution.py:238

commit v4 on v3

--- a/solution.py
+++ b/solution.py
@@ -106,7 +106,7 @@
     loads = [
         pltpu.make_async_copy(tiles_hbm.at[t], tiles.at[t], tile_sems.at[t]) for t in range(count)
     ]
-    for copy in copies[:2] + loads + copies[2:]:
+    for copy in copies + loads:
         copy.start()
     copies[0].wait()
     copies[1].wait()
@@ -121,19 +121,6 @@
         full = jnp.concatenate([tall] * (span // LANES), axis=1)
         keep = (row_iota(full.shape) % share) == (lane_iota(full.shape) // width)
         weights.append(jnp.where(keep, full, 0.0).astype(BF16))
-    for copy in loads:
-        copy.wait()
-    for n in range(pieces):
-        pair = []
-        for g in (2 * n, 2 * n + 1):
-            columns = slice(g * span, (g + 1) * span)
-            pair.append([nt(weights[t], tiles[t, :, columns]) for t in range(count)])
-        rows = slice(2 * n * share, 2 * (n + 1) * share)
-        for s in range(rank):
-            at = slice(s * share, (s + 1) * share)
-            block = [jnp.concatenate([part[at] for part in parts], axis=1) for parts in pair]
-            out[s, rows, :] = jnp.concatenate(block, axis=0).astype(BF16)
-
     for copy in copies[2:]:
         copy.wait()
     q = lax.axis_index("rep")
@@ -149,6 +136,22 @@
     rows = slice(width, width + META)
     for s in range(rank):
         out[s, rows, :] = meta
+    for copy in loads:
+        copy.wait()
+    for n in range(pieces // 2):
+        wide = []
+        for t in range(count):
+            groups = [tiles[t, :, (4 * n + g) * span : (4 * n + g + 1) * span] for g in range(4)]
+            wide.append(nt(weights[t], jnp.concatenate(groups, axis=0)))
+        for s in range(rank):
+            at = slice(s * share, (s + 1) * share)
+            for h in range(2):
+                block = []
+                for g in (2 * h, 2 * h + 1):
+                    lanes = slice(g * width, (g + 1) * width)
+                    block.append(jnp.concatenate([part[at, lanes] for part in wide], axis=1))
+                rows = slice((2 * n + h) * META, (2 * n + h + 1) * META)
+                out[s, rows, :] = jnp.concatenate(block, axis=0).astype(BF16)
 
 
 def rows_kernel(reps, got, out, two, one, total):
@@ -212,7 +215,7 @@
     table[...] = rows
     g0 = dot3(rows, rows, 1)
     eye = (row_iota(g0.shape) == lane_iota(g0.shape)).astype(F32)
-    msq = jnp.sum(g0 * eye, keepdims=True) / rows_total
+    msq = jnp.sum(rows * rows, keepdims=True) / rows_total
     inv = 1.0 / jnp.sqrt(msq + 1e-06)
     g = g0 * (inv * inv) / rows_total
     square = dot3(g, g)

time: 46.1 us -> 45.1 us (0.978)
  Pallas kernels: 6.48 us -> 5.49 us
    pallas_call x1, Pallas kernels: 2.76 us -> 1.9 us  [sliced(): pl.pallas_call(first_kernel, out_shape=jax.ShapeDtypeStruct((rank, width...]
where the time goes in v4:
time: 45.1 us; the launch traced here: 44.9 us
  blocking collectives  25 us (55%)
  starting transfers between devices  7.6 us (17%)
  waiting for transfers between devices  6.08 us (13%)
  Pallas kernels  5.49 us (12%)
  between operations  0.68 us (2%)
    all_to_all x1, blocking collectives, sliced(): got = lax.all_to_all(sends, ('tiles', 'rep'), 0, 0, tiled=True)  25 us
    ppermute x7, starting transfers between devices, swap(): lax.ppermute(x, ('tiles', 'rep'), [(i, i ^ mask) for i in range(size)])  7.6 us
    ppermute x7, waiting for transfers between devices, swap(): lax.ppermute(x, ('tiles', 'rep'), [(i, i ^ mask) for i in range(size)])  6.08 us
    pallas_call x1, Pallas kernels, sliced(): pl.pallas_call(final_kernel, out_shape=(jax.ShapeDtypeStruct(u_one.shape,...  1.99 us
    pallas_call x1, Pallas kernels, sliced(): pl.pallas_call(first_kernel, out_shape=jax.ShapeDtypeStruct((rank, width...  1.9 us
    pallas_call x1, Pallas kernels, sliced(): pl.pallas_call(functools.partial(rows_kernel, reps), out_shape=jax.ShapeD...  1.6 us
  transfers between devices with their start and end apart: 7, of which 5 were waited for; matrix products, arithmetic and copies ran while one was open for 0% of the time, Pallas kernels for 0%

profile of v4, /device:TPU:0, one launch (start us, length us, event | category | flops | bytes accessed | tf_op | source)
XLA Modules:
  0.0 44.9 jit_solution(16233058474461306786)
XLA Ops:
  0.6 1.9 %first.1 = bf16[32,80,128]{2,1,0:T(8,128)(2,1)S(1)} custom-call(s32[2]{0:T(128)} %one.1, s32[2]{0:T(128)} %two_hbm.1, s32[2]{0:T(128)} %three_hbm.1, s32[8]{0:T(128)} %owner.1, bf16[2,64,4096]{2,1,0:T(8,128)(2,1)} %tiles_hbm.1, bf16[32,1024]{1,0:T(8,128)(2,1)} %u_three_hbm.1, bf16[32,128]{1,0:T(8,128)(2,1)} %u_two_hbm.1, f32[32,64]{1,0:T(8,128)} %u_one_hbm.1), custom_call_target="tpu_custom_call" | custom-call | tf_op jit(solution)/shard_map/first/pallas_call | solution.py:256
  2.5 25.0 %all_to_all.5.got = bf16[32,80,128]{2,1,0:T(8,128)(2,1)S(1)} all-to-all(bf16[32,80,128]{2,1,0:T(8,128)(2,1)S(1)} %first.1), channel_id=1, replica_groups=mesh['tiles'=8,'rep'=4] {'tiles','rep'}, dimensions={0} | all-to-all | bytes 1310720 | tf_op jit(solution)/shard_map/all_to_all | solution.py:271
  27.6 1.6 %rows_part.1 = bf16[32,512]{1,0:T(8,128)(2,1)S(1)} custom-call(bf16[32,80,128]{2,1,0:T(8,128)(2,1)S(1)} %all_to_all.5.got), custom_call_target="tpu_custom_call" | custom-call | tf_op jit(solution)/shard_map/rows_part/pallas_call | solution.py:272
  29.2 0.1 collective-permute-start
  29.3 1.1 %collective-permute-done = bf16[32,512]{1,0:T(8,128)(2,1)S(1)} collective-permute-done((bf16[32,512]{1,0:T(8,128)(2,1)S(1)}, bf16[32,512]{1,0:T(8,128)(2,1)S(1)}, u32[]{:S(2)}, u32[]{:S(2)}) %collective-permute-start) | collective-permute-done | bytes 32800 | tf_op jit(solution)/shard_map/ppermute | solution.py:241
  30.4 0.0 copy-start
  30.5 0.0 copy-start.1
  30.5 2.4 %collective-permute-start.3 = (bf16[32,512]{1,0:T(8,128)(2,1)S(1)}, bf16[32,512]{1,0:T(8,128)(2,1)S(1)}, u32[]{:S(2)}, u32[]{:S(2)}) collective-permute-start(bf16[32,512]{1,0:T(8,128)(2,1)S(1)} %add_convert_fusion.1), channel_id=1, source_target_pairs={{0,6},{1,7},{2,4},{3,5},{4,2},{5,3},{6,0},{7,1},{8,14},{9,15},{10,... | collective-permute-start | bytes 98312 | tf_op jit(solution)/shard_map/ppermute | solution.py:241
  32.8 0.2 collective-permute-start.2
  33.0 0.8 %collective-permute-start.1 = (bf16[32,512]{1,0:T(8,128)(2,1)S(1)}, bf16[32,512]{1,0:T(8,128)(2,1)S(1)}, u32[]{:S(2)}, u32[]{:S(2)}) collective-permute-start(bf16[32,512]{1,0:T(8,128)(2,1)S(1)} %add_convert_fusion.1), channel_id=1, source_target_pairs={{0,3},{1,2},{2,1},{3,0},{4,7},{5,6},{6,5},{7,4},{8,11},{9,10},{10,... | collective-permute-start | bytes 98312 | tf_op jit(solution)/shard_map/ppermute | solution.py:241
  33.7 1.6 %collective-permute-done.3 = bf16[32,512]{1,0:T(8,128)(2,1)S(1)} collective-permute-done((bf16[32,512]{1,0:T(8,128)(2,1)S(1)}, bf16[32,512]{1,0:T(8,128)(2,1)S(1)}, u32[]{:S(2)}, u32[]{:S(2)}) %collective-permute-start.3) | collective-permute-done | bytes 32800 | tf_op jit(solution)/shard_map/ppermute | solution.py:241
  35.4 1.1 %collective-permute-done.2 = bf16[32,512]{1,0:T(8,128)(2,1)S(1)} collective-permute-done((bf16[32,512]{1,0:T(8,128)(2,1)S(1)}, bf16[32,512]{1,0:T(8,128)(2,1)S(1)}, u32[]{:S(2)}, u32[]{:S(2)}) %collective-permute-start.2) | collective-permute-done | bytes 32800 | tf_op jit(solution)/shard_map/ppermute | solution.py:241
  36.5 0.0 collective-permute-done.1
  36.5 1.5 %collective-permute-start.6 = (bf16[32,512]{1,0:T(8,128)(2,1)S(1)}, bf16[32,512]{1,0:T(8,128)(2,1)S(1)}, u32[]{:S(2)}, u32[]{:S(2)}) collective-permute-start(bf16[32,512]{1,0:T(8,128)(2,1)S(1)} %add_convert_fusion.a), channel_id=1, source_target_pairs={{0,24},{1,25},{2,26},{3,27},{4,28},{5,29},{6,30},{7,31},{8,16},{9,... | collective-permute-start | bytes 98312 | tf_op jit(solution)/shard_map/ppermute | solution.py:241
  38.0 0.0 collective-permute-start.5
  38.0 2.7 %collective-permute-start.4 = (bf16[32,512]{1,0:T(8,128)(2,1)S(1)}, bf16[32,512]{1,0:T(8,128)(2,1)S(1)}, u32[]{:S(2)}, u32[]{:S(2)}) collective-permute-start(bf16[32,512]{1,0:T(8,128)(2,1)S(1)} %add_convert_fusion.a), channel_id=1, source_target_pairs={{0,17},{1,16},{2,19},{3,18},{4,21},{5,20},{6,23},{7,22},{8,25},{9,... | collective-permute-start | bytes 98312 | tf_op jit(solution)/shard_map/ppermute | solution.py:241
  40.7 1.8 %collective-permute-done.6.d = bf16[32,512]{1,0:T(8,128)(2,1)S(1)} collective-permute-done((bf16[32,512]{1,0:T(8,128)(2,1)S(1)}, bf16[32,512]{1,0:T(8,128)(2,1)S(1)}, u32[]{:S(2)}, u32[]{:S(2)}) %collective-permute-start.6) | collective-permute-done | bytes 32800 | tf_op jit(solution)/shard_map/ppermute | solution.py:241
  42.4 0.0 collective-permute-done.5.c
  42.4 0.5 %collective-permute-done.4.b = bf16[32,512]{1,0:T(8,128)(2,1)S(1)} collective-permute-done((bf16[32,512]{1,0:T(8,128)(2,1)S(1)}, bf16[32,512]{1,0:T(8,128)(2,1)S(1)}, u32[]{:S(2)}, u32[]{:S(2)}) %collective-permute-start.4) | collective-permute-done | bytes 32800 | tf_op jit(solution)/shard_map/ppermute | solution.py:241
  42.9 0.0 copy-done
  42.9 0.0 copy-done.1
  42.9 2.0 %final.1 = (f32[32,64]{1,0:T(8,128)}, bf16[2,2048]{1,0:T(2,128)(2,1)}) custom-call(s32[2]{0:T(128)S(1)} %copy-done, s32[8]{0:T(128)S(1)} %copy-done.1, bf16[32,512]{1,0:T(8,128)(2,1)S(1)} %add_convert_fusion.a, bf16[32,512]{1,0:T(8,128)(2,1)S(1)} %collective-permute-done.4.b, bf16[32,512]{1,0:T(8,128)(2,1)S(1)} %collective-permute-done.5.c, ...), custom_call_target="tpu_custom_call" | custom-call | tf_op jit(solution)/shard_map/final/pallas_call | solution.py:292
  (2 shorter events, 0.0 us)
Async XLA Ops:
  29.2 1.3 %collective-permute-start = (bf16[32,512]{1,0:T(8,128)(2,1)S(1)}, bf16[32,512]{1,0:T(8,128)(2,1)S(1)}, u32[]{:S(2)}, u32[]{:S(2)}) collective-permute-start(bf16[32,512]{1,0:T(8,128)(2,1)S(1)} %rows_part.1), channel_id=1, source_target_pairs={{0,1},{1,0},{2,3},{3,2},{4,5},{5,4},{6,7},{7,6},{8,9},{9,8},{10,11... | collective-permute-start | bytes 98312 | tf_op jit(solution)/shard_map/ppermute | solution.py:241
  30.4 12.5 %copy-start = (s32[2]{0:T(128)S(1)}, s32[2]{0:T(128)}, u32[]{:S(2)}) copy-start(s32[2]{0:T(128)} %one.1) | copy-start | bytes 28
  30.5 12.5 %copy-start.1 = (s32[8]{0:T(128)S(1)}, s32[8]{0:T(128)}, u32[]{:S(2)}) copy-start(s32[8]{0:T(128)} %owner.1) | copy-start | bytes 100
  30.5 4.9 %collective-permute-start.3 = (bf16[32,512]{1,0:T(8,128)(2,1)S(1)}, bf16[32,512]{1,0:T(8,128)(2,1)S(1)}, u32[]{:S(2)}, u32[]{:S(2)}) collective-permute-start(bf16[32,512]{1,0:T(8,128)(2,1)S(1)} %add_convert_fusion.1), channel_id=1, source_target_pairs={{0,6},{1,7},{2,4},{3,5},{4,2},{5,3},{6,0},{7,1},{8,14},{9,15},{10,... | collective-permute-start | bytes 98312 | tf_op jit(solution)/shard_map/ppermute | solution.py:241
  32.8 3.6 %collective-permute-start.2 = (bf16[32,512]{1,0:T(8,128)(2,1)S(1)}, bf16[32,512]{1,0:T(8,128)(2,1)S(1)}, u32[]{:S(2)}, u32[]{:S(2)}) collective-permute-start(bf16[32,512]{1,0:T(8,128)(2,1)S(1)} %add_convert_fusion.1), channel_id=1, source_target_pairs={{0,5},{1,4},{2,7},{3,6},{4,1},{5,0},{6,3},{7,2},{8,13},{9,12},{10,... | collective-permute-start | bytes 98312 | tf_op jit(solution)/shard_map/ppermute | solution.py:241
  33.0 3.5 %collective-permute-start.1 = (bf16[32,512]{1,0:T(8,128)(2,1)S(1)}, bf16[32,512]{1,0:T(8,128)(2,1)S(1)}, u32[]{:S(2)}, u32[]{:S(2)}) collective-permute-start(bf16[32,512]{1,0:T(8,128)(2,1)S(1)} %add_convert_fusion.1), channel_id=1, source_target_pairs={{0,3},{1,2},{2,1},{3,0},{4,7},{5,6},{6,5},{7,4},{8,11},{9,10},{10,... | collective-permute-start | bytes 98312 | tf_op jit(solution)/shard_map/ppermute | solution.py:241
  36.5 5.9 %collective-permute-start.6 = (bf16[32,512]{1,0:T(8,128)(2,1)S(1)}, bf16[32,512]{1,0:T(8,128)(2,1)S(1)}, u32[]{:S(2)}, u32[]{:S(2)}) collective-permute-start(bf16[32,512]{1,0:T(8,128)(2,1)S(1)} %add_convert_fusion.a), channel_id=1, source_target_pairs={{0,24},{1,25},{2,26},{3,27},{4,28},{5,29},{6,30},{7,31},{8,16},{9,... | collective-permute-start | bytes 98312 | tf_op jit(solution)/shard_map/ppermute | solution.py:241
  38.0 4.4 %collective-permute-start.5 = (bf16[32,512]{1,0:T(8,128)(2,1)S(1)}, bf16[32,512]{1,0:T(8,128)(2,1)S(1)}, u32[]{:S(2)}, u32[]{:S(2)}) collective-permute-start(bf16[32,512]{1,0:T(8,128)(2,1)S(1)} %add_convert_fusion.a), channel_id=1, source_target_pairs={{0,9},{1,8},{2,11},{3,10},{4,13},{5,12},{6,15},{7,14},{8,1},{9,0},... | collective-permute-start | bytes 98312 | tf_op jit(solution)/shard_map/ppermute | solution.py:241
  38.0 4.9 %collective-permute-start.4 = (bf16[32,512]{1,0:T(8,128)(2,1)S(1)}, bf16[32,512]{1,0:T(8,128)(2,1)S(1)}, u32[]{:S(2)}, u32[]{:S(2)}) collective-permute-start(bf16[32,512]{1,0:T(8,128)(2,1)S(1)} %add_convert_fusion.a), channel_id=1, source_target_pairs={{0,17},{1,16},{2,19},{3,18},{4,21},{5,20},{6,23},{7,22},{8,25},{9,... | collective-permute-start | bytes 98312 | tf_op jit(solution)/shard_map/ppermute | solution.py:241

commit v5 on v4

--- a/solution.py
+++ b/solution.py
@@ -91,7 +91,7 @@
 
 
 def first_kernel(
-    one_hbm, two_hbm, three_hbm, owner_hbm, tiles_hbm, u_three_hbm, u_two_hbm, u_one_hbm, out,
+    one_hbm, two_hbm, three_hbm, owner_hbm, tiles_hbm, u_three_hbm, u_two_hbm, u_one_hbm, out, places,
     one, two, three, owner, tiles, u_three, u_two, u_one, two_f32, in_sems, tile_sems,
 ):
     count, width = tiles.shape[:2]
@@ -129,9 +129,14 @@
     low = u_one[pl.ds(pl.multiple_of(q * share, share), share), :]
     lane = lane_iota((share, half))
     ints = jnp.zeros((share, half), F32)
+    spot = lane_iota(places.shape)
+    place = jnp.zeros(places.shape, jnp.int32)
     for t in range(count):
+        position = owner[one[t]]
         ints = jnp.where(lane == t, two[t].astype(F32), ints)
-        ints = jnp.where(lane == count + t, owner[one[t]].astype(F32), ints)
+        ints = jnp.where(lane == count + t, position.astype(F32), ints)
+        place = jnp.where(spot == t, position, place)
+    places[...] = place
     meta = jnp.concatenate([top, jnp.concatenate([low, ints], axis=1)], axis=0).astype(BF16)
     rows = slice(width, width + META)
     for s in range(rank):
@@ -164,12 +169,16 @@
     owners = sources // reps
     blocks = 2 * owners
     lines = []
-    for src in range(sources):
+    halves = lane_iota((META, LANES)) // half
+    for src in range(0, sources, 2):
         t, q = divmod(src, reps)
-        meta = got[src, width:depth, :].astype(F32)
-        two[t, q * share : (q + 1) * share, :] = meta[:share]
-        one[t, q * share : (q + 1) * share, :] = meta[share:]
-        lines.append(meta[share : share + 1])
+        pair = [got[src + k, width:depth, :].astype(F32) for k in range(2)]
+        rows = slice(q * share, (q + 2) * share)
+        both = jnp.concatenate([meta[:share] for meta in pair], axis=0)
+        for k in range(2):
+            two[2 * t + k, rows, :] = jnp.where(halves == k, both, 0.0).astype(BF16)
+        one[t, rows, :] = jnp.concatenate([meta[share:] for meta in pair], axis=0)
+        lines += [meta[share : share + 1] for meta in pair]
     lines = jnp.concatenate(lines, axis=0)
     lane = lane_iota(lines.shape)
     scale = jnp.zeros(lines.shape, F32)
@@ -177,7 +186,6 @@
         scale = jnp.where(lane == half + k, float(blocks**k), scale)
     code = jnp.sum(lines * scale, axis=1, keepdims=True).astype(jnp.int32)
     total[...] = jnp.zeros_like(total)
-    lane = lane_iota((rank, LANES))
     for src in range(sources):
         block = got[src, 0:width, :]
         moving = jnp.concatenate([block, block], axis=0)
@@ -186,10 +194,7 @@
         for _ in range(2 * count):
             digits.append(left % blocks)
             left = left // blocks
-        picks = []
-        for b in digits[:count]:
-            picks.append(jnp.where((lane // half) == (b % 2), two[b // 2], 0.0))
-        stacked = jnp.concatenate(picks, axis=0).astype(BF16)
+        stacked = jnp.concatenate([two[b] for b in digits[:count]], axis=0)
         product = jnp.dot(stacked, moving, preferred_element_type=F32).astype(BF16).astype(F32)
         for t, p in enumerate(digits[count:]):
             total[t, src % 2, p] += product[t * rank : (t + 1) * rank]
@@ -208,7 +213,7 @@
     out[...] = part.astype(BF16)
 
 
-def final_kernel(one, owner, a, b, c, d, factor, tile_factor, table):
+def final_kernel(places, a, b, c, d, factor, tile_factor, table):
     rank, rows_total = a.shape
     half = LANES // 2
     rows = (a[...].astype(F32) + b[...].astype(F32)) + (c[...].astype(F32) + d[...].astype(F32))
@@ -226,8 +231,9 @@
         window = table[:, pl.ds(pl.multiple_of((p // 2) * LANES, LANES), LANES)]
         return jnp.where(p % 2 == 1, pltpu.roll(window, half, 1), window)[:, :half]
 
-    places = [lax.axis_index("tiles")] + [owner[one[t]] for t in range(tile_factor.shape[0])]
-    picked = jnp.concatenate([block(p) for p in places], axis=1)
+    place = places[...]
+    picks = [lax.axis_index("tiles")] + [place[0, t] for t in range(tile_factor.shape[0])]
+    picked = jnp.concatenate([block(p) for p in picks], axis=1)
     x = dot3(step, picked)
     factor[...] = x[:, :half]
     for t in range(tile_factor.shape[0]):
@@ -248,16 +254,18 @@
     reps = lax.axis_size("rep")
     size = owners * reps
     rows_total = owner_map.shape[0] * width
-    smem = pl.BlockSpec(memory_space=pltpu.SMEM)
     vmem = pl.BlockSpec(memory_space=pltpu.VMEM)
     narrow = pltpu.CompilerParams(vmem_limit_bytes=NARROW)
     ints = (block_one, block_two, block_three, owner_map)
     arrays = (tiles, u_three, u_two, u_one)
-    sends = pl.pallas_call(
+    sends, places = pl.pallas_call(
         first_kernel,
-        out_shape=jax.ShapeDtypeStruct((rank, width + META, LANES), BF16),
+        out_shape=(
+            jax.ShapeDtypeStruct((rank, width + META, LANES), BF16),
+            jax.ShapeDtypeStruct((META // 2, LANES), jnp.int32),
+        ),
         in_specs=[pl.BlockSpec(memory_space=pltpu.HBM)] * 8,
-        out_specs=vmem,
+        out_specs=(vmem, vmem),
         scratch_shapes=[pltpu.SMEM(x.shape, x.dtype) for x in ints]
         + [pltpu.VMEM(x.shape, x.dtype) for x in arrays]
         + [
@@ -275,7 +283,7 @@
         in_specs=[vmem],
         out_specs=vmem,
         scratch_shapes=[
-            pltpu.VMEM((owners, rank, LANES), F32),
+            pltpu.VMEM((2 * owners, rank, LANES), BF16),
             pltpu.VMEM((owners, rank, LANES), F32),
             pltpu.VMEM((count, 2, owners, rank, LANES), F32),
         ],
@@ -295,12 +303,12 @@
             jax.ShapeDtypeStruct(u_one.shape, F32),
             jax.ShapeDtypeStruct((count, rank * width), BF16),
         ),
-        in_specs=[smem] * 2 + [vmem] * 4,
+        in_specs=[vmem] * 5,
         out_specs=(vmem, vmem),
         scratch_shapes=[pltpu.VMEM((rank, rows_total), F32)],
         compiler_params=narrow,
         name="final",
-    )(block_one, owner_map, *parts)
+    )(places, *parts)
 
 
 def per_device(*args):
@@ -312,6 +320,7 @@
     fits = (
         owners * reps == rank == 32
         and reps * META // 2 == rank
+        and reps % 2 == 0
         and width * 2 == LANES
         and count == 2
         and owner_map.shape[0] == owners

time: 45.1 us -> 44.2 us (0.980)
  Pallas kernels: 5.49 us -> 4.61 us
    pallas_call x1, Pallas kernels: 1.99 us -> 1.45 us  [sliced(): pl.pallas_call(final_kernel, out_shape=(jax.ShapeDtypeStruct(u_one.shape,...]
where the time goes in v5:
time: 44.2 us; the launch traced here: 44 us
  blocking collectives  25 us (57%)
  starting transfers between devices  7.6 us (17%)
  waiting for transfers between devices  6.08 us (14%)
  Pallas kernels  4.61 us (10%)
  between operations  0.66 us (1%)
    all_to_all x1, blocking collectives, sliced(): got = lax.all_to_all(sends, ('tiles', 'rep'), 0, 0, tiled=True)  25 us
    ppermute x7, starting transfers between devices, swap(): lax.ppermute(x, ('tiles', 'rep'), [(i, i ^ mask) for i in range(size)])  7.6 us
    ppermute x7, waiting for transfers between devices, swap(): lax.ppermute(x, ('tiles', 'rep'), [(i, i ^ mask) for i in range(size)])  6.08 us
    pallas_call x1, Pallas kernels, sliced(): pl.pallas_call(first_kernel, out_shape=(jax.ShapeDtypeStruct((rank, width...  1.9 us
    pallas_call x1, Pallas kernels, sliced(): pl.pallas_call(final_kernel, out_shape=(jax.ShapeDtypeStruct(u_one.shape,...  1.45 us
    pallas_call x1, Pallas kernels, sliced(): pl.pallas_call(functools.partial(rows_kernel, reps), out_shape=jax.ShapeD...  1.26 us
  transfers between devices with their start and end apart: 7, of which 5 were waited for; matrix products, arithmetic and copies ran while one was open for 0% of the time, Pallas kernels for 0%

profile of v5, /device:TPU:0, one launch (start us, length us, event | category | flops | bytes accessed | tf_op | source)
XLA Modules:
  0.0 44.0 jit_solution(6432589576642732911)
XLA Ops:
  0.6 1.9 %first.1 = (bf16[32,80,128]{2,1,0:T(8,128)(2,1)S(1)}, s32[8,128]{1,0:T(8,128)S(1)}) custom-call(s32[2]{0:T(128)} %one_hbm.1, s32[2]{0:T(128)} %two_hbm.1, s32[2]{0:T(128)} %three_hbm.1, s32[8]{0:T(128)} %owner_hbm.1, bf16[2,64,4096]{2,1,0:T(8,128)(2,1)} %tiles_hbm.1, bf16[32,1024]{1,0:T(8,128)(2,1)} %u_three_hbm.1, bf16[32,128]{1,0:T(8,128)(2,1)} %u_two_hbm.1, ...), custom_call_target="tpu_custom_call" | custom-call | tf_op jit(solution)/shard_map/first/pallas_call | solution.py:261
  2.5 25.0 %all_to_all.5.got = bf16[32,80,128]{2,1,0:T(8,128)(2,1)S(1)} all-to-all(bf16[32,80,128]{2,1,0:T(8,128)(2,1)S(1)} %get-tuple-element.5), channel_id=1, replica_groups=mesh['tiles'=8,'rep'=4] {'tiles','rep'}, dimensions={0} | all-to-all | bytes 1310720 | tf_op jit(solution)/shard_map/all_to_all | solution.py:279
  27.6 1.3 %rows_part.1 = bf16[32,512]{1,0:T(8,128)(2,1)S(1)} custom-call(bf16[32,80,128]{2,1,0:T(8,128)(2,1)S(1)} %all_to_all.5.got), custom_call_target="tpu_custom_call" | custom-call | tf_op jit(solution)/shard_map/rows_part/pallas_call | solution.py:280
  28.8 0.1 collective-permute-start
  29.0 1.1 %collective-permute-done = bf16[32,512]{1,0:T(8,128)(2,1)S(1)} collective-permute-done((bf16[32,512]{1,0:T(8,128)(2,1)S(1)}, bf16[32,512]{1,0:T(8,128)(2,1)S(1)}, u32[]{:S(2)}, u32[]{:S(2)}) %collective-permute-start) | collective-permute-done | bytes 32800 | tf_op jit(solution)/shard_map/ppermute | solution.py:247
  30.1 2.4 %collective-permute-start.3 = (bf16[32,512]{1,0:T(8,128)(2,1)S(1)}, bf16[32,512]{1,0:T(8,128)(2,1)S(1)}, u32[]{:S(2)}, u32[]{:S(2)}) collective-permute-start(bf16[32,512]{1,0:T(8,128)(2,1)S(1)} %add_convert_fusion.1), channel_id=1, source_target_pairs={{0,6},{1,7},{2,4},{3,5},{4,2},{5,3},{6,0},{7,1},{8,14},{9,15},{10,... | collective-permute-start | bytes 98312 | tf_op jit(solution)/shard_map/ppermute | solution.py:247
  32.5 0.2 collective-permute-start.2
  32.6 0.8 %collective-permute-start.1 = (bf16[32,512]{1,0:T(8,128)(2,1)S(1)}, bf16[32,512]{1,0:T(8,128)(2,1)S(1)}, u32[]{:S(2)}, u32[]{:S(2)}) collective-permute-start(bf16[32,512]{1,0:T(8,128)(2,1)S(1)} %add_convert_fusion.1), channel_id=1, source_target_pairs={{0,3},{1,2},{2,1},{3,0},{4,7},{5,6},{6,5},{7,4},{8,11},{9,10},{10,... | collective-permute-start | bytes 98312 | tf_op jit(solution)/shard_map/ppermute | solution.py:247
  33.4 1.6 %collective-permute-done.3 = bf16[32,512]{1,0:T(8,128)(2,1)S(1)} collective-permute-done((bf16[32,512]{1,0:T(8,128)(2,1)S(1)}, bf16[32,512]{1,0:T(8,128)(2,1)S(1)}, u32[]{:S(2)}, u32[]{:S(2)}) %collective-permute-start.3) | collective-permute-done | bytes 32800 | tf_op jit(solution)/shard_map/ppermute | solution.py:247
  35.0 1.1 %collective-permute-done.2 = bf16[32,512]{1,0:T(8,128)(2,1)S(1)} collective-permute-done((bf16[32,512]{1,0:T(8,128)(2,1)S(1)}, bf16[32,512]{1,0:T(8,128)(2,1)S(1)}, u32[]{:S(2)}, u32[]{:S(2)}) %collective-permute-start.2) | collective-permute-done | bytes 32800 | tf_op jit(solution)/shard_map/ppermute | solution.py:247
  36.1 0.0 collective-permute-done.1
  36.1 1.5 %collective-permute-start.6 = (bf16[32,512]{1,0:T(8,128)(2,1)S(1)}, bf16[32,512]{1,0:T(8,128)(2,1)S(1)}, u32[]{:S(2)}, u32[]{:S(2)}) collective-permute-start(bf16[32,512]{1,0:T(8,128)(2,1)S(1)} %add_convert_fusion.a), channel_id=1, source_target_pairs={{0,24},{1,25},{2,26},{3,27},{4,28},{5,29},{6,30},{7,31},{8,16},{9,... | collective-permute-start | bytes 98312 | tf_op jit(solution)/shard_map/ppermute | solution.py:247
  37.6 0.0 collective-permute-start.5
  37.6 2.7 %collective-permute-start.4 = (bf16[32,512]{1,0:T(8,128)(2,1)S(1)}, bf16[32,512]{1,0:T(8,128)(2,1)S(1)}, u32[]{:S(2)}, u32[]{:S(2)}) collective-permute-start(bf16[32,512]{1,0:T(8,128)(2,1)S(1)} %add_convert_fusion.a), channel_id=1, source_target_pairs={{0,17},{1,16},{2,19},{3,18},{4,21},{5,20},{6,23},{7,22},{8,25},{9,... | collective-permute-start | bytes 98312 | tf_op jit(solution)/shard_map/ppermute | solution.py:247
  40.3 1.8 %collective-permute-done.6.d = bf16[32,512]{1,0:T(8,128)(2,1)S(1)} collective-permute-done((bf16[32,512]{1,0:T(8,128)(2,1)S(1)}, bf16[32,512]{1,0:T(8,128)(2,1)S(1)}, u32[]{:S(2)}, u32[]{:S(2)}) %collective-permute-start.6) | collective-permute-done | bytes 32800 | tf_op jit(solution)/shard_map/ppermute | solution.py:247
  42.1 0.0 collective-permute-done.5.c
  42.1 0.5 %collective-permute-done.4.b = bf16[32,512]{1,0:T(8,128)(2,1)S(1)} collective-permute-done((bf16[32,512]{1,0:T(8,128)(2,1)S(1)}, bf16[32,512]{1,0:T(8,128)(2,1)S(1)}, u32[]{:S(2)}, u32[]{:S(2)}) %collective-permute-start.4) | collective-permute-done | bytes 32800 | tf_op jit(solution)/shard_map/ppermute | solution.py:247
  42.6 1.4 %final.1 = (f32[32,64]{1,0:T(8,128)}, bf16[2,2048]{1,0:T(2,128)(2,1)}) custom-call(s32[8,128]{1,0:T(8,128)S(1)} %get-tuple-element.4.places, bf16[32,512]{1,0:T(8,128)(2,1)S(1)} %add_convert_fusion.a, bf16[32,512]{1,0:T(8,128)(2,1)S(1)} %collective-permute-done.4.b, bf16[32,512]{1,0:T(8,128)(2,1)S(1)} %collective-permute-done.5.c, ...), custom_call_target="tpu_custom_call" | custom-call | tf_op jit(solution)/shard_map/final/pallas_call | solution.py:300
  (2 shorter events, 0.0 us)
Async XLA Ops:
  28.8 1.3 %collective-permute-start = (bf16[32,512]{1,0:T(8,128)(2,1)S(1)}, bf16[32,512]{1,0:T(8,128)(2,1)S(1)}, u32[]{:S(2)}, u32[]{:S(2)}) collective-permute-start(bf16[32,512]{1,0:T(8,128)(2,1)S(1)} %rows_part.1), channel_id=1, source_target_pairs={{0,1},{1,0},{2,3},{3,2},{4,5},{5,4},{6,7},{7,6},{8,9},{9,8},{10,11... | collective-permute-start | bytes 98312 | tf_op jit(solution)/shard_map/ppermute | solution.py:247
  30.1 4.9 %collective-permute-start.3 = (bf16[32,512]{1,0:T(8,128)(2,1)S(1)}, bf16[32,512]{1,0:T(8,128)(2,1)S(1)}, u32[]{:S(2)}, u32[]{:S(2)}) collective-permute-start(bf16[32,512]{1,0:T(8,128)(2,1)S(1)} %add_convert_fusion.1), channel_id=1, source_target_pairs={{0,6},{1,7},{2,4},{3,5},{4,2},{5,3},{6,0},{7,1},{8,14},{9,15},{10,... | collective-permute-start | bytes 98312 | tf_op jit(solution)/shard_map/ppermute | solution.py:247
  32.5 3.6 %collective-permute-start.2 = (bf16[32,512]{1,0:T(8,128)(2,1)S(1)}, bf16[32,512]{1,0:T(8,128)(2,1)S(1)}, u32[]{:S(2)}, u32[]{:S(2)}) collective-permute-start(bf16[32,512]{1,0:T(8,128)(2,1)S(1)} %add_convert_fusion.1), channel_id=1, source_target_pairs={{0,5},{1,4},{2,7},{3,6},{4,1},{5,0},{6,3},{7,2},{8,13},{9,12},{10,... | collective-permute-start | bytes 98312 | tf_op jit(solution)/shard_map/ppermute | solution.py:247
  32.6 3.5 %collective-permute-start.1 = (bf16[32,512]{1,0:T(8,128)(2,1)S(1)}, bf16[32,512]{1,0:T(8,128)(2,1)S(1)}, u32[]{:S(2)}, u32[]{:S(2)}) collective-permute-start(bf16[32,512]{1,0:T(8,128)(2,1)S(1)} %add_convert_fusion.1), channel_id=1, source_target_pairs={{0,3},{1,2},{2,1},{3,0},{4,7},{5,6},{6,5},{7,4},{8,11},{9,10},{10,... | collective-permute-start | bytes 98312 | tf_op jit(solution)/shard_map/ppermute | solution.py:247
  36.1 5.9 %collective-permute-start.6 = (bf16[32,512]{1,0:T(8,128)(2,1)S(1)}, bf16[32,512]{1,0:T(8,128)(2,1)S(1)}, u32[]{:S(2)}, u32[]{:S(2)}) collective-permute-start(bf16[32,512]{1,0:T(8,128)(2,1)S(1)} %add_convert_fusion.a), channel_id=1, source_target_pairs={{0,24},{1,25},{2,26},{3,27},{4,28},{5,29},{6,30},{7,31},{8,16},{9,... | collective-permute-start | bytes 98312 | tf_op jit(solution)/shard_map/ppermute | solution.py:247
  37.6 4.4 %collective-permute-start.5 = (bf16[32,512]{1,0:T(8,128)(2,1)S(1)}, bf16[32,512]{1,0:T(8,128)(2,1)S(1)}, u32[]{:S(2)}, u32[]{:S(2)}) collective-permute-start(bf16[32,512]{1,0:T(8,128)(2,1)S(1)} %add_convert_fusion.a), channel_id=1, source_target_pairs={{0,9},{1,8},{2,11},{3,10},{4,13},{5,12},{6,15},{7,14},{8,1},{9,0},... | collective-permute-start | bytes 98312 | tf_op jit(solution)/shard_map/ppermute | solution.py:247
  37.6 4.9 %collective-permute-start.4 = (bf16[32,512]{1,0:T(8,128)(2,1)S(1)}, bf16[32,512]{1,0:T(8,128)(2,1)S(1)}, u32[]{:S(2)}, u32[]{:S(2)}) collective-permute-start(bf16[32,512]{1,0:T(8,128)(2,1)S(1)} %add_convert_fusion.a), channel_id=1, source_target_pairs={{0,17},{1,16},{2,19},{3,18},{4,21},{5,20},{6,23},{7,22},{8,25},{9,... | collective-permute-start | bytes 98312 | tf_op jit(solution)/shard_map/ppermute | solution.py:247

commit v6 on v5

--- a/solution.py
+++ b/solution.py
@@ -94,6 +94,7 @@
     one_hbm, two_hbm, three_hbm, owner_hbm, tiles_hbm, u_three_hbm, u_two_hbm, u_one_hbm, out, places,
     one, two, three, owner, tiles, u_three, u_two, u_one, two_f32, in_sems, tile_sems,
 ):
+    side = lax.axis_index("half")
     count, width = tiles.shape[:2]
     rank = u_three.shape[0]
     half = LANES // 2
@@ -138,9 +139,9 @@
         place = jnp.where(spot == t, position, place)
     places[...] = place
     meta = jnp.concatenate([top, jnp.concatenate([low, ints], axis=1)], axis=0).astype(BF16)
-    rows = slice(width, width + META)
-    for s in range(rank):
-        out[s, rows, :] = meta
+    rows = slice(2 * width, 2 * width + META)
+    for k in range(out.shape[0]):
+        out[k, rows, :] = meta
     for copy in loads:
         copy.wait()
     for n in range(pieces // 2):
@@ -155,28 +156,44 @@
                 for g in (2 * h, 2 * h + 1):
                     lanes = slice(g * width, (g + 1) * width)
                     block.append(jnp.concatenate([part[at, lanes] for part in wide], axis=1))
-                rows = slice((2 * n + h) * META, (2 * n + h + 1) * META)
-                out[s, rows, :] = jnp.concatenate(block, axis=0).astype(BF16)
-
-
-def rows_kernel(reps, got, out, two, one, total):
+                start = (s % 2) * width + (2 * n + h) * META
+                rows = slice(start, start + META)
+                out[(s // 2) ^ side, rows, :] = jnp.concatenate(block, axis=0).astype(BF16)
+
+
+def share_kernel(sends, u_two, out, two_f32):
+    share = META // 2
+    two_f32[...] = u_two[...].astype(F32)
+    start = pl.multiple_of(lax.axis_index("rep") * share, share)
+    line = two_f32[pl.ds(start, share), :].astype(BF16)
+    depth = out.shape[1]
+    for k in range(out.shape[0]):
+        out[k, depth - share : depth, :] = line
+
+
+def table_kernel(reps, got, out, two, one, total):
     sources, depth = got.shape[:2]
-    width = depth - META
     half = LANES // 2
     share = META // 2
+    width = (depth - META - share) // 2
     rank = share * reps
     count = LANES // width
-    owners = sources // reps
+    owners = 2 * sources // reps
     blocks = 2 * owners
+    side = lax.axis_index("half")
     lines = []
     halves = lane_iota((META, LANES)) // half
     for src in range(0, sources, 2):
         t, q = divmod(src, reps)
-        pair = [got[src + k, width:depth, :].astype(F32) for k in range(2)]
         rows = slice(q * share, (q + 2) * share)
-        both = jnp.concatenate([meta[:share] for meta in pair], axis=0)
-        for k in range(2):
-            two[2 * t + k, rows, :] = jnp.where(halves == k, both, 0.0).astype(BF16)
+        pair = [got[src + k, 2 * width : 2 * width + META, :].astype(F32) for k in range(2)]
+        last = [got[src + k, depth - share : depth, :].astype(F32) for k in range(2)]
+        mine = jnp.concatenate([meta[:share] for meta in pair], axis=0)
+        theirs = jnp.concatenate(last, axis=0)
+        for at, both in ((side, mine), (1 - side, theirs)):
+            shard = at * (owners // 2) + t
+            for k in range(2):
+                two[2 * shard + k, rows, :] = jnp.where(halves == k, both, 0.0).astype(BF16)
         one[t, rows, :] = jnp.concatenate([meta[share:] for meta in pair], axis=0)
         lines += [meta[share : share + 1] for meta in pair]
     lines = jnp.concatenate(lines, axis=0)
@@ -187,8 +204,11 @@
     code = jnp.sum(lines * scale, axis=1, keepdims=True).astype(jnp.int32)
     total[...] = jnp.zeros_like(total)
     for src in range(sources):
-        block = got[src, 0:width, :]
-        moving = jnp.concatenate([block, block], axis=0)
+        moving = []
+        for s in range(2):
+            block = got[src, s * width : (s + 1) * width, :]
+            moving.append(jnp.concatenate([block, block], axis=0))
+        moving = jnp.concatenate(moving, axis=1)
         left = code[src, 0]
         digits = []
         for _ in range(2 * count):
@@ -198,25 +218,43 @@
         product = jnp.dot(stacked, moving, preferred_element_type=F32).astype(BF16).astype(F32)
         for t, p in enumerate(digits[count:]):
             total[t, src % 2, p] += product[t * rank : (t + 1) * rank]
-    sums = []
-    for p in range(owners):
-        low = (total[0, 0, p] + total[0, 1, p])[:, :half]
-        high = pltpu.roll(total[1, 0, p] + total[1, 1, p], half, 1)[:, :half]
-        sums.append(low + high)
-    table = jnp.concatenate(sums, axis=1)
-    high = table.astype(BF16)
-    low = (table - high.astype(F32)).astype(BF16)
-    readers = jnp.concatenate([one[p][:, :half] for p in range(owners)], axis=1).astype(BF16)
+    for s in range(2):
+        sums = []
+        lanes = slice(s * LANES, (s + 1) * LANES)
+        for p in range(owners):
+            low = (total[0, 0, p, :, lanes] + total[0, 1, p, :, lanes])[:, :half]
+            high = total[1, 0, p, :, lanes] + total[1, 1, p, :, lanes]
+            sums.append(low + pltpu.roll(high, half, 1)[:, :half])
+        out[s * rank : (s + 1) * rank, :] = jnp.concatenate(sums, axis=1).astype(BF16)
+    known = jnp.concatenate([one[p][:, :half] for p in range(owners // 2)], axis=1)
+    known = jnp.concatenate([known[: rank // 2], known[rank // 2 :]], axis=1)
+    out[2 * rank :, :] = known.astype(BF16)
+
+
+def rows_kernel(mine, theirs, out):
+    rank, rows_total = out.shape
+    table = mine[: 2 * rank, :].astype(F32) + theirs[: 2 * rank, :].astype(F32)
+    known = []
+    for ref in (mine, theirs):
+        lines = ref[2 * rank :, :].astype(F32)
+        known.append(
+            jnp.concatenate([lines[:, : rows_total // 2], lines[:, rows_total // 2 :]], axis=0)
+        )
+    first = lax.axis_index("half") == 0
+    readers = jnp.concatenate(
+        [jnp.where(first, known[0], known[1]), jnp.where(first, known[1], known[0])], axis=1
+    ).astype(BF16)
+    high, low = split(table)
     project = (nt(readers, high) + nt(readers, low)).astype(BF16)
     part = jnp.dot(project, high, preferred_element_type=F32)
     part += jnp.dot(project, low, preferred_element_type=F32)
     out[...] = part.astype(BF16)
 
 
-def final_kernel(places, a, b, c, d, factor, tile_factor, table):
+def final_kernel(places, a, b, factor, tile_factor, table):
     rank, rows_total = a.shape
     half = LANES // 2
-    rows = (a[...].astype(F32) + b[...].astype(F32)) + (c[...].astype(F32) + d[...].astype(F32))
+    rows = a[...].astype(F32) + b[...].astype(F32)
     table[...] = rows
     g0 = dot3(rows, rows, 1)
     eye = (row_iota(g0.shape) == lane_iota(g0.shape)).astype(F32)
@@ -232,7 +270,7 @@
         return jnp.where(p % 2 == 1, pltpu.roll(window, half, 1), window)[:, :half]
 
     place = places[...]
-    picks = [lax.axis_index("tiles")] + [place[0, t] for t in range(tile_factor.shape[0])]
+    picks = [lax.axis_index(("half", "rest"))] + [place[0, t] for t in range(tile_factor.shape[0])]
     picked = jnp.concatenate([block(p) for p in picks], axis=1)
     x = dot3(step, picked)
     factor[...] = x[:, :half]
@@ -244,30 +282,34 @@
 
 
 def swap(x, size, mask):
-    return lax.ppermute(x, ("tiles", "rep"), [(i, i ^ mask) for i in range(size)])
+    return lax.ppermute(x, ("half", "rest", "rep"), [(i, i ^ mask) for i in range(size)])
 
 
 def sliced(tiles, block_one, block_two, block_three, owner_map, u_one, u_two, u_three):
     count, width = tiles.shape[:2]
     rank = u_three.shape[0]
-    owners = lax.axis_size("tiles")
+    owners = 2 * lax.axis_size("rest")
     reps = lax.axis_size("rep")
     size = owners * reps
+    sources = size // 2
     rows_total = owner_map.shape[0] * width
+    depth = 2 * width + META + META // 2
     vmem = pl.BlockSpec(memory_space=pltpu.VMEM)
     narrow = pltpu.CompilerParams(vmem_limit_bytes=NARROW)
+    core, x, y, near, far = 1, 2, 4, 8, 16
+    their_two = swap(u_two, size, far | core)
     ints = (block_one, block_two, block_three, owner_map)
     arrays = (tiles, u_three, u_two, u_one)
     sends, places = pl.pallas_call(
         first_kernel,
         out_shape=(
-            jax.ShapeDtypeStruct((rank, width + META, LANES), BF16),
+            jax.ShapeDtypeStruct((sources, depth, LANES), BF16),
             jax.ShapeDtypeStruct((META // 2, LANES), jnp.int32),
         ),
         in_specs=[pl.BlockSpec(memory_space=pltpu.HBM)] * 8,
         out_specs=(vmem, vmem),
-        scratch_shapes=[pltpu.SMEM(x.shape, x.dtype) for x in ints]
-        + [pltpu.VMEM(x.shape, x.dtype) for x in arrays]
+        scratch_shapes=[pltpu.SMEM(a.shape, a.dtype) for a in ints]
+        + [pltpu.VMEM(a.shape, a.dtype) for a in arrays]
         + [
             pltpu.VMEM(u_two.shape, F32),
             pltpu.SemaphoreType.DMA((7,)),
@@ -275,73 +317,91 @@
         ],
         compiler_params=narrow,
         name="first",
-    )(*[pltpu.with_memory_space_constraint(x, pltpu.HBM) for x in ints + arrays])
-    got = lax.all_to_all(sends, ("tiles", "rep"), 0, 0, tiled=True)
-    part = pl.pallas_call(
-        functools.partial(rows_kernel, reps),
-        out_shape=jax.ShapeDtypeStruct((rank, rows_total), BF16),
+    )(*[pltpu.with_memory_space_constraint(a, pltpu.HBM) for a in ints + arrays])
+    sends = pl.pallas_call(
+        share_kernel,
+        out_shape=jax.ShapeDtypeStruct(sends.shape, sends.dtype),
+        in_specs=[vmem] * 2,
+        out_specs=vmem,
+        scratch_shapes=[pltpu.VMEM(u_two.shape, F32)],
+        input_output_aliases={0: 0},
+        compiler_params=narrow,
+        name="share",
+    )(sends, their_two)
+    got = lax.all_to_all(sends, ("rest", "rep"), 0, 0, tiled=True)
+    table = pl.pallas_call(
+        functools.partial(table_kernel, reps),
+        out_shape=jax.ShapeDtypeStruct((2 * rank + rank // 2, rows_total), BF16),
         in_specs=[vmem],
         out_specs=vmem,
         scratch_shapes=[
             pltpu.VMEM((2 * owners, rank, LANES), BF16),
-            pltpu.VMEM((owners, rank, LANES), F32),
-            pltpu.VMEM((count, 2, owners, rank, LANES), F32),
+            pltpu.VMEM((owners // 2, rank, LANES), F32),
+            pltpu.VMEM((count, 2, owners, rank, 2 * LANES), F32),
         ],
         compiler_params=narrow,
+        name="table",
+    )(got)
+    part = pl.pallas_call(
+        rows_kernel,
+        out_shape=jax.ShapeDtypeStruct((rank, rows_total), BF16),
+        in_specs=[vmem] * 2,
+        out_specs=vmem,
+        compiler_params=narrow,
         name="rows_part",
-    )(got)
-    part = (part.astype(F32) + swap(part, size, 1).astype(F32)).astype(BF16)
-    m, n = 2, 4
-    pair = part.astype(F32) + swap(part, size, m | 1).astype(F32)
-    other = swap(part, size, n | 1).astype(F32) + swap(part, size, m ^ n).astype(F32)
+    )(table, swap(table, size, far | core))
+    part = (part.astype(F32) + swap(part, size, core).astype(F32)).astype(BF16)
+    pair = part.astype(F32) + swap(part, size, x | core).astype(F32)
+    other = swap(part, size, y | core).astype(F32) + swap(part, size, x ^ y).astype(F32)
     part = (pair + other).astype(BF16)
-    m, n = 16, 8
-    parts = [part, swap(part, size, m | 1), swap(part, size, n | 1), swap(part, size, m ^ n)]
     return pl.pallas_call(
         final_kernel,
         out_shape=(
             jax.ShapeDtypeStruct(u_one.shape, F32),
             jax.ShapeDtypeStruct((count, rank * width), BF16),
         ),
-        in_specs=[vmem] * 5,
+        in_specs=[vmem] * 3,
         out_specs=(vmem, vmem),
         scratch_shapes=[pltpu.VMEM((rank, rows_total), F32)],
         compiler_params=narrow,
         name="final",
-    )(places, *parts)
-
-
-def per_device(*args):
-    tiles, _, _, _, owner_map, u_one, u_two, u_three = args
-    count, width = tiles.shape[:2]
+    )(places, part, swap(part, size, near | core))
+
+
+def fits(mesh, tiles, block_one, block_two, block_three, owner_map, u_one, u_two, u_three):
+    owners, reps = mesh.shape["tiles"], mesh.shape["rep"]
     rank = u_three.shape[0]
-    owners = lax.axis_size("tiles")
-    reps = lax.axis_size("rep")
-    fits = (
-        owners * reps == rank == 32
-        and reps * META // 2 == rank
-        and reps % 2 == 0
-        and width * 2 == LANES
-        and count == 2
+    width = tiles.shape[1]
+    return (
+        owners == 8
+        and reps == 4
+        and rank == owners * reps == reps * META // 2
+        and tiles.shape[0] == 2 * owners * reps
+        and 2 * width == LANES
         and owner_map.shape[0] == owners
-        and u_one.shape[1] == width
-        and u_two.shape[1] == LANES
+        and u_one.shape[1] == owners * width
+        and u_two.shape[1] == owners * LANES
+        and u_three.shape[1] % LANES == 0
     )
-    return (sliced if fits else general)(*args)
+
+
+def specs(tiles, rep):
+    both = tiles + rep
+    ins = (P(both, None, None), P(both), P(both), P(both), P(), P(None, tiles), P(None, tiles), P())
+    return ins, (P(None, tiles), P(both, None))
 
 
 def solution(mesh):
-    in_specs = (
-        P(("tiles", "rep"), None, None),
-        P(("tiles", "rep")),
-        P(("tiles", "rep")),
-        P(("tiles", "rep")),
-        P(),
-        P(None, "tiles"),
-        P(None, "tiles"),
-        P(),
-    )
-    out_specs = (P(None, "tiles"), P(("tiles", "rep"), None))
-    return jax.shard_map(
-        per_device, mesh=mesh, in_specs=in_specs, out_specs=out_specs, check_vma=False
-    )
+    def run(*args):
+        if fits(mesh, *args):
+            axes = ("half", "rest", "rep")
+            grid = mesh.devices.reshape(2, -1, mesh.shape["rep"])
+            halves = jax.sharding.Mesh(grid, axes)
+            ins, outs = specs(axes[:2], axes[2:])
+            body, where = sliced, halves
+        else:
+            ins, outs = specs(("tiles",), ("rep",))
+            body, where = general, mesh
+        return jax.shard_map(body, mesh=where, in_specs=ins, out_specs=outs, check_vma=False)(*args)
+
+    return run

time: 44.2 us -> 42.6 us (0.964)
  blocking collectives: 25 us -> 16.5 us
  waiting for transfers between devices: 6.08 us -> 11.7 us
  starting transfers between devices: 7.6 us -> 8.99 us
    all_to_all x1, blocking collectives: 25 us -> 16.5 us  [sliced(): got = lax.all_to_all(sends, ('rest', 'rep'), 0, 0, tiled=True)]
    ppermute x7, waiting for transfers between devices: 6.08 us -> 11.7 us  [swap(): lax.ppermute(x, ('half', 'rest', 'rep'), [(i, i ^ mask) for i in range(si...]
    ppermute x7, starting transfers between devices: 7.6 us -> 8.99 us  [swap(): lax.ppermute(x, ('half', 'rest', 'rep'), [(i, i ^ mask) for i in range(si...]
    pallas_call x2 -> x4, Pallas kernels: 3.16 us -> 2.99 us  [the longest x1 1.9 us: sliced(): pl.pallas_call(first_kernel, out_shape=(jax.ShapeDtypeStruct((sources, de...]
  transfers between devices with their start and end apart: 7 -> 7, of which waited for: 5 -> 4; matrix products, arithmetic and copies ran while one was open for 0% -> 0% of each run, Pallas kernels for 0% -> 4%
where the time goes in v6:
time: 42.6 us; the launch traced here: 42.4 us
  blocking collectives  16.5 us (39%)
  waiting for transfers between devices  11.7 us (27%)
  starting transfers between devices  8.99 us (21%)
  Pallas kernels  4.43 us (10%)
  between operations  0.69 us (2%)
    all_to_all x1, blocking collectives, sliced(): got = lax.all_to_all(sends, ('rest', 'rep'), 0, 0, tiled=True)  16.5 us
    ppermute x7, waiting for transfers between devices, swap(): lax.ppermute(x, ('half', 'rest', 'rep'), [(i, i ^ mask) for i in range(si...  11.7 us
    ppermute x7, starting transfers between devices, swap(): lax.ppermute(x, ('half', 'rest', 'rep'), [(i, i ^ mask) for i in range(si...  8.99 us
    pallas_call x1, Pallas kernels, sliced(): pl.pallas_call(first_kernel, out_shape=(jax.ShapeDtypeStruct((sources, de...  1.9 us
    pallas_call x1, Pallas kernels, sliced(): pl.pallas_call(final_kernel, out_shape=(jax.ShapeDtypeStruct(u_one.shape,...  1.44 us
  transfers between devices with their start and end apart: 7, of which 4 were waited for; matrix products, arithmetic and copies ran while one was open for 0% of the time, Pallas kernels for 4%

profile of v6, /device:TPU:0, one launch (start us, length us, event | category | flops | bytes accessed | tf_op | source)
XLA Modules:
  0.0 42.4 jit_solution(14361044787577393441)
XLA Ops:
  0.6 3.5 %collective-permute-start = (bf16[32,128]{1,0:T(8,128)(2,1)}, bf16[32,128]{1,0:T(8,128)(2,1)S(1)}, u32[]{:S(2)}, u32[]{:S(2)}) collective-permute-start(bf16[32,128]{1,0:T(8,128)(2,1)} %u_two_hbm.1), channel_id=1, source_target_pairs={{0,17},{1,16},{2,19},{3,18},{4,21},{5,20},{6,23},{7,22},{8,25},{9,... | collective-permute-start | bytes 24584 | tf_op jit(solution)/shard_map/ppermute | solution.py:285
  4.2 1.9 %first.1 = (bf16[16,152,128]{2,1,0:T(8,128)(2,1)S(1)}, s32[8,128]{1,0:T(8,128)S(1)}) custom-call(s32[2]{0:T(128)} %one_hbm.1, s32[2]{0:T(128)} %two_hbm.1, s32[2]{0:T(128)} %three_hbm.1, s32[8]{0:T(128)} %owner_hbm.1, bf16[2,64,4096]{2,1,0:T(8,128)(2,1)} %tiles_hbm.1, bf16[32,1024]{1,0:T(8,128)(2,1)} %u_three_hbm.1, bf16[32,128]{1,0:T(8,128)(2,1)} %u_two_hbm.1, ...), custom_call_target="tpu_custom_call" | custom-call | tf_op jit(solution)/shard_map/first/pallas_call | solution.py:303
  6.1 0.0 collective-permute-done.u_two
  6.1 16.5 %all_to_all.5.got = bf16[16,152,128]{2,1,0:T(8,128)(2,1)S(1)} all-to-all(bf16[16,152,128]{2,1,0:T(8,128)(2,1)S(1)} %share.1), channel_id=1, replica_groups=mesh['half'=2,'rest'=4,'rep'=4] {'rest','rep'}, dimensions={0} | all-to-all | bytes 1245184 | tf_op jit(solution)/shard_map/all_to_all | solution.py:331
  22.6 0.8 %table.1.mine = bf16[80,512]{1,0:T(8,128)(2,1)S(1)} custom-call(bf16[16,152,128]{2,1,0:T(8,128)(2,1)S(1)} %all_to_all.5.got), custom_call_target="tpu_custom_call" | custom-call | tf_op jit(solution)/shard_map/table/pallas_call | solution.py:332
  23.4 1.9 %collective-permute-start.1 = (bf16[80,512]{1,0:T(8,128)(2,1)S(1)}, bf16[80,512]{1,0:T(8,128)(2,1)S(1)}, u32[]{:S(2)}, u32[]{:S(2)}) collective-permute-start(bf16[80,512]{1,0:T(8,128)(2,1)S(1)} %table.1.mine), channel_id=1, source_target_pairs={{0,17},{1,16},{2,19},{3,18},{4,21},{5,20},{6,23},{7,22},{8,25},{9,... | collective-permute-start | bytes 245768 | tf_op jit(solution)/shard_map/ppermute | solution.py:285
  25.3 5.4 %collective-permute-done.1.theirs = bf16[80,512]{1,0:T(8,128)(2,1)S(1)} collective-permute-done((bf16[80,512]{1,0:T(8,128)(2,1)S(1)}, bf16[80,512]{1,0:T(8,128)(2,1)S(1)}, u32[]{:S(2)}, u32[]{:S(2)}) %collective-permute-start.1) | collective-permute-done | bytes 81952 | tf_op jit(solution)/shard_map/ppermute | solution.py:285
  30.8 0.3 rows_part.1
  31.1 0.2 collective-permute-start.2
  31.3 1.1 %collective-permute-done.2 = bf16[32,512]{1,0:T(8,128)(2,1)S(1)} collective-permute-done((bf16[32,512]{1,0:T(8,128)(2,1)S(1)}, bf16[32,512]{1,0:T(8,128)(2,1)S(1)}, u32[]{:S(2)}, u32[]{:S(2)}) %collective-permute-start.2) | collective-permute-done | bytes 32800 | tf_op jit(solution)/shard_map/ppermute | solution.py:285
  32.4 0.3 collective-permute-start.5
  32.7 0.7 %collective-permute-start.4 = (bf16[32,512]{1,0:T(8,128)(2,1)S(1)}, bf16[32,512]{1,0:T(8,128)(2,1)S(1)}, u32[]{:S(2)}, u32[]{:S(2)}) collective-permute-start(bf16[32,512]{1,0:T(8,128)(2,1)S(1)} %add_convert_fusion.1), channel_id=1, source_target_pairs={{0,5},{1,4},{2,7},{3,6},{4,1},{5,0},{6,3},{7,2},{8,13},{9,12},{10,... | collective-permute-start | bytes 98312 | tf_op jit(solution)/shard_map/ppermute | solution.py:285
  33.3 2.3 %collective-permute-start.3 = (bf16[32,512]{1,0:T(8,128)(2,1)S(1)}, bf16[32,512]{1,0:T(8,128)(2,1)S(1)}, u32[]{:S(2)}, u32[]{:S(2)}) collective-permute-start(bf16[32,512]{1,0:T(8,128)(2,1)S(1)} %add_convert_fusion.1), channel_id=1, source_target_pairs={{0,3},{1,2},{2,1},{3,0},{4,7},{5,6},{6,5},{7,4},{8,11},{9,10},{10,... | collective-permute-start | bytes 98312 | tf_op jit(solution)/shard_map/ppermute | solution.py:285
  35.6 1.8 %collective-permute-done.5 = bf16[32,512]{1,0:T(8,128)(2,1)S(1)} collective-permute-done((bf16[32,512]{1,0:T(8,128)(2,1)S(1)}, bf16[32,512]{1,0:T(8,128)(2,1)S(1)}, u32[]{:S(2)}, u32[]{:S(2)}) %collective-permute-start.5) | collective-permute-done | bytes 32800 | tf_op jit(solution)/shard_map/ppermute | solution.py:285
  37.4 0.0 collective-permute-done.4
  37.4 0.0 collective-permute-done.3
  37.5 0.1 collective-permute-start.6
  37.5 3.4 %collective-permute-done.6.b = bf16[32,512]{1,0:T(8,128)(2,1)S(1)} collective-permute-done((bf16[32,512]{1,0:T(8,128)(2,1)S(1)}, bf16[32,512]{1,0:T(8,128)(2,1)S(1)}, u32[]{:S(2)}, u32[]{:S(2)}) %collective-permute-start.6) | collective-permute-done | bytes 32800 | tf_op jit(solution)/shard_map/ppermute | solution.py:285
  40.9 1.4 %final.1 = (f32[32,64]{1,0:T(8,128)}, bf16[2,2048]{1,0:T(2,128)(2,1)}) custom-call(s32[8,128]{1,0:T(8,128)S(1)} %get-tuple-element.4.places, bf16[32,512]{1,0:T(8,128)(2,1)S(1)} %add_convert_fusion.a, bf16[32,512]{1,0:T(8,128)(2,1)S(1)} %collective-permute-done.6.b), custom_call_target="tpu_custom_call" | custom-call | tf_op jit(solution)/shard_map/final/pallas_call | solution.py:357
  (3 shorter events, 0.0 us)
Async XLA Ops:
  0.6 5.4 %collective-permute-start = (bf16[32,128]{1,0:T(8,128)(2,1)}, bf16[32,128]{1,0:T(8,128)(2,1)S(1)}, u32[]{:S(2)}, u32[]{:S(2)}) collective-permute-start(bf16[32,128]{1,0:T(8,128)(2,1)} %u_two_hbm.1), channel_id=1, source_target_pairs={{0,17},{1,16},{2,19},{3,18},{4,21},{5,20},{6,23},{7,22},{8,25},{9,... | collective-permute-start | bytes 24584 | tf_op jit(solution)/shard_map/ppermute | solution.py:285
  23.4 7.4 %collective-permute-start.1 = (bf16[80,512]{1,0:T(8,128)(2,1)S(1)}, bf16[80,512]{1,0:T(8,128)(2,1)S(1)}, u32[]{:S(2)}, u32[]{:S(2)}) collective-permute-start(bf16[80,512]{1,0:T(8,128)(2,1)S(1)} %table.1.mine), channel_id=1, source_target_pairs={{0,17},{1,16},{2,19},{3,18},{4,21},{5,20},{6,23},{7,22},{8,25},{9,... | collective-permute-start | bytes 245768 | tf_op jit(solution)/shard_map/ppermute | solution.py:285
  31.1 1.3 %collective-permute-start.2 = (bf16[32,512]{1,0:T(8,128)(2,1)S(1)}, bf16[32,512]{1,0:T(8,128)(2,1)S(1)}, u32[]{:S(2)}, u32[]{:S(2)}) collective-permute-start(bf16[32,512]{1,0:T(8,128)(2,1)S(1)} %rows_part.1), channel_id=1, source_target_pairs={{0,1},{1,0},{2,3},{3,2},{4,5},{5,4},{6,7},{7,6},{8,9},{9,8},{10,11... | collective-permute-start | bytes 98312 | tf_op jit(solution)/shard_map/ppermute | solution.py:285
  32.4 5.1 %collective-permute-start.5 = (bf16[32,512]{1,0:T(8,128)(2,1)S(1)}, bf16[32,512]{1,0:T(8,128)(2,1)S(1)}, u32[]{:S(2)}, u32[]{:S(2)}) collective-permute-start(bf16[32,512]{1,0:T(8,128)(2,1)S(1)} %add_convert_fusion.1), channel_id=1, source_target_pairs={{0,6},{1,7},{2,4},{3,5},{4,2},{5,3},{6,0},{7,1},{8,14},{9,15},{10,... | collective-permute-start | bytes 98312 | tf_op jit(solution)/shard_map/ppermute | solution.py:285
  32.7 4.8 %collective-permute-start.4 = (bf16[32,512]{1,0:T(8,128)(2,1)S(1)}, bf16[32,512]{1,0:T(8,128)(2,1)S(1)}, u32[]{:S(2)}, u32[]{:S(2)}) collective-permute-start(bf16[32,512]{1,0:T(8,128)(2,1)S(1)} %add_convert_fusion.1), channel_id=1, source_target_pairs={{0,5},{1,4},{2,7},{3,6},{4,1},{5,0},{6,3},{7,2},{8,13},{9,12},{10,... | collective-permute-start | bytes 98312 | tf_op jit(solution)/shard_map/ppermute | solution.py:285
  33.3 4.1 %collective-permute-start.3 = (bf16[32,512]{1,0:T(8,128)(2,1)S(1)}, bf16[32,512]{1,0:T(8,128)(2,1)S(1)}, u32[]{:S(2)}, u32[]{:S(2)}) collective-permute-start(bf16[32,512]{1,0:T(8,128)(2,1)S(1)} %add_convert_fusion.1), channel_id=1, source_target_pairs={{0,3},{1,2},{2,1},{3,0},{4,7},{5,6},{6,5},{7,4},{8,11},{9,10},{10,... | collective-permute-start | bytes 98312 | tf_op jit(solution)/shard_map/ppermute | solution.py:285
  37.5 3.5 %collective-permute-start.6 = (bf16[32,512]{1,0:T(8,128)(2,1)S(1)}, bf16[32,512]{1,0:T(8,128)(2,1)S(1)}, u32[]{:S(2)}, u32[]{:S(2)}) collective-permute-start(bf16[32,512]{1,0:T(8,128)(2,1)S(1)} %add_convert_fusion.a), channel_id=1, source_target_pairs={{0,9},{1,8},{2,11},{3,10},{4,13},{5,12},{6,15},{7,14},{8,1},{9,0},... | collective-permute-start | bytes 98312 | tf_op jit(solution)/shard_map/ppermute | solution.py:285

commit v7 on v6

--- a/solution.py
+++ b/solution.py
@@ -71,9 +71,9 @@
 
 def dot3(a, b, axis=0):
     (ah, al), (bh, bl) = split(a), split(b)
-    left = jnp.concatenate([ah, al, ah], axis=1)
-    right = jnp.concatenate([bh, bh, bl], axis=axis)
-    return lax.dot_general(left, right, (((1,), (axis,)), ((), ())), preferred_element_type=F32)
+    dims = (((1,), (axis,)), ((), ()))
+    parts = [lax.dot_general(p, q, dims, preferred_element_type=F32) for p, q in ((ah, bh), (ah, bl), (al, bh))]
+    return parts[0] + (parts[1] + parts[2])
 
 
 def lane_iota(shape):
@@ -91,7 +91,7 @@
 
 
 def first_kernel(
-    one_hbm, two_hbm, three_hbm, owner_hbm, tiles_hbm, u_three_hbm, u_two_hbm, u_one_hbm, out, places,
+    one_hbm, two_hbm, three_hbm, owner_hbm, tiles_hbm, u_three_hbm, u_two_hbm, u_one_hbm, out, places, pack,
     one, two, three, owner, tiles, u_three, u_two, u_one, two_f32, in_sems, tile_sems,
 ):
     side = lax.axis_index("half")
@@ -125,6 +125,9 @@
     for copy in copies[2:]:
         copy.wait()
     q = lax.axis_index("rep")
+    pack[:rank, :] = u_two[...]
+    pair = [u_one[: rank // 2, :], u_one[rank // 2 :, :]]
+    pack[rank:, :] = jnp.concatenate(pair, axis=1).astype(BF16)
     two_f32[...] = u_two[...].astype(F32)
     top = two_f32[pl.ds(pl.multiple_of(q * share, share), share), :]
     low = u_one[pl.ds(pl.multiple_of(q * share, share), share), :]
@@ -161,21 +164,11 @@
                 out[(s // 2) ^ side, rows, :] = jnp.concatenate(block, axis=0).astype(BF16)
 
 
-def share_kernel(sends, u_two, out, two_f32):
-    share = META // 2
-    two_f32[...] = u_two[...].astype(F32)
-    start = pl.multiple_of(lax.axis_index("rep") * share, share)
-    line = two_f32[pl.ds(start, share), :].astype(BF16)
-    depth = out.shape[1]
-    for k in range(out.shape[0]):
-        out[k, depth - share : depth, :] = line
-
-
-def table_kernel(reps, got, out, two, one, total):
+def table_kernel(reps, got, far0, far1, far2, far3, out, readers, two, one, total):
     sources, depth = got.shape[:2]
     half = LANES // 2
     share = META // 2
-    width = (depth - META - share) // 2
+    width = (depth - META) // 2
     rank = share * reps
     count = LANES // width
     owners = 2 * sources // reps
@@ -187,15 +180,21 @@
         t, q = divmod(src, reps)
         rows = slice(q * share, (q + 2) * share)
         pair = [got[src + k, 2 * width : 2 * width + META, :].astype(F32) for k in range(2)]
-        last = [got[src + k, depth - share : depth, :].astype(F32) for k in range(2)]
         mine = jnp.concatenate([meta[:share] for meta in pair], axis=0)
-        theirs = jnp.concatenate(last, axis=0)
-        for at, both in ((side, mine), (1 - side, theirs)):
-            shard = at * (owners // 2) + t
-            for k in range(2):
-                two[2 * shard + k, rows, :] = jnp.where(halves == k, both, 0.0).astype(BF16)
-        one[t, rows, :] = jnp.concatenate([meta[share:] for meta in pair], axis=0)
+        shard = side * (owners // 2) + t
+        for k in range(2):
+            two[2 * shard + k, rows, :] = jnp.where(halves == k, mine, 0.0).astype(BF16)
+        one[shard, rows, :] = jnp.concatenate([meta[share:] for meta in pair], axis=0)
         lines += [meta[share : share + 1] for meta in pair]
+    halves = lane_iota((rank, LANES)) // half
+    for k, ref in enumerate((far0, far1, far2, far3)):
+        shard = (1 - side) * (owners // 2) + (lax.axis_index("rest") ^ k)
+        theirs = ref[:rank, :].astype(F32)
+        for k in range(2):
+            two[2 * shard + k] = jnp.where(halves == k, theirs, 0.0).astype(BF16)
+        theirs = ref[rank:, :].astype(F32)
+        one[shard, : rank // 2, :] = theirs
+        one[shard, rank // 2 :, :] = pltpu.roll(theirs, half, 1)
     lines = jnp.concatenate(lines, axis=0)
     lane = lane_iota(lines.shape)
     scale = jnp.zeros(lines.shape, F32)
@@ -226,26 +225,12 @@
             high = total[1, 0, p, :, lanes] + total[1, 1, p, :, lanes]
             sums.append(low + pltpu.roll(high, half, 1)[:, :half])
         out[s * rank : (s + 1) * rank, :] = jnp.concatenate(sums, axis=1).astype(BF16)
-    known = jnp.concatenate([one[p][:, :half] for p in range(owners // 2)], axis=1)
-    known = jnp.concatenate([known[: rank // 2], known[rank // 2 :]], axis=1)
-    out[2 * rank :, :] = known.astype(BF16)
-
-
-def rows_kernel(mine, theirs, out):
-    rank, rows_total = out.shape
-    table = mine[: 2 * rank, :].astype(F32) + theirs[: 2 * rank, :].astype(F32)
-    known = []
-    for ref in (mine, theirs):
-        lines = ref[2 * rank :, :].astype(F32)
-        known.append(
-            jnp.concatenate([lines[:, : rows_total // 2], lines[:, rows_total // 2 :]], axis=0)
-        )
-    first = lax.axis_index("half") == 0
-    readers = jnp.concatenate(
-        [jnp.where(first, known[0], known[1]), jnp.where(first, known[1], known[0])], axis=1
-    ).astype(BF16)
-    high, low = split(table)
-    project = (nt(readers, high) + nt(readers, low)).astype(BF16)
+    readers[...] = jnp.concatenate([one[p][:, :half] for p in range(owners)], axis=1).astype(BF16)
+
+
+def rows_kernel(mine, theirs, readers, out):
+    high, low = split(mine[...].astype(F32) + theirs[...].astype(F32))
+    project = (nt(readers[...], high) + nt(readers[...], low)).astype(BF16)
     part = jnp.dot(project, high, preferred_element_type=F32)
     part += jnp.dot(project, low, preferred_element_type=F32)
     out[...] = part.astype(BF16)
@@ -293,21 +278,21 @@
     size = owners * reps
     sources = size // 2
     rows_total = owner_map.shape[0] * width
-    depth = 2 * width + META + META // 2
+    depth = 2 * width + META
     vmem = pl.BlockSpec(memory_space=pltpu.VMEM)
     narrow = pltpu.CompilerParams(vmem_limit_bytes=NARROW)
     core, x, y, near, far = 1, 2, 4, 8, 16
-    their_two = swap(u_two, size, far | core)
     ints = (block_one, block_two, block_three, owner_map)
     arrays = (tiles, u_three, u_two, u_one)
-    sends, places = pl.pallas_call(
+    sends, places, pack = pl.pallas_call(
         first_kernel,
         out_shape=(
             jax.ShapeDtypeStruct((sources, depth, LANES), BF16),
             jax.ShapeDtypeStruct((META // 2, LANES), jnp.int32),
+            jax.ShapeDtypeStruct((rank + rank // 2, LANES), BF16),
         ),
         in_specs=[pl.BlockSpec(memory_space=pltpu.HBM)] * 8,
-        out_specs=(vmem, vmem),
+        out_specs=(vmem, vmem, vmem),
         scratch_shapes=[pltpu.SMEM(a.shape, a.dtype) for a in ints]
         + [pltpu.VMEM(a.shape, a.dtype) for a in arrays]
         + [
@@ -318,38 +303,32 @@
         compiler_params=narrow,
         name="first",
     )(*[pltpu.with_memory_space_constraint(a, pltpu.HBM) for a in ints + arrays])
-    sends = pl.pallas_call(
-        share_kernel,
-        out_shape=jax.ShapeDtypeStruct(sends.shape, sends.dtype),
-        in_specs=[vmem] * 2,
-        out_specs=vmem,
-        scratch_shapes=[pltpu.VMEM(u_two.shape, F32)],
-        input_output_aliases={0: 0},
-        compiler_params=narrow,
-        name="share",
-    )(sends, their_two)
+    theirs = [swap(pack, size, far | core | k * y) for k in range(4)]
     got = lax.all_to_all(sends, ("rest", "rep"), 0, 0, tiled=True)
-    table = pl.pallas_call(
+    table, readers = pl.pallas_call(
         functools.partial(table_kernel, reps),
-        out_shape=jax.ShapeDtypeStruct((2 * rank + rank // 2, rows_total), BF16),
-        in_specs=[vmem],
-        out_specs=vmem,
+        out_shape=(
+            jax.ShapeDtypeStruct((2 * rank, rows_total), BF16),
+            jax.ShapeDtypeStruct((rank, rows_total), BF16),
+        ),
+        in_specs=[vmem] * 5,
+        out_specs=(vmem, vmem),
         scratch_shapes=[
             pltpu.VMEM((2 * owners, rank, LANES), BF16),
-            pltpu.VMEM((owners // 2, rank, LANES), F32),
+            pltpu.VMEM((owners, rank, LANES), F32),
             pltpu.VMEM((count, 2, owners, rank, 2 * LANES), F32),
         ],
         compiler_params=narrow,
         name="table",
-    )(got)
+    )(got, *theirs)
     part = pl.pallas_call(
         rows_kernel,
         out_shape=jax.ShapeDtypeStruct((rank, rows_total), BF16),
-        in_specs=[vmem] * 2,
+        in_specs=[vmem] * 3,
         out_specs=vmem,
         compiler_params=narrow,
         name="rows_part",
-    )(table, swap(table, size, far | core))
+    )(table, swap(table, size, far | core), readers)
     part = (part.astype(F32) + swap(part, size, core).astype(F32)).astype(BF16)
     pair = part.astype(F32) + swap(part, size, x | core).astype(F32)
     other = swap(part, size, y | core).astype(F32) + swap(part, size, x ^ y).astype(F32)

time: 42.6 us -> 41.4 us (0.972)
  blocking collectives: 16.5 us -> 0 us
  starting transfers between devices: 8.99 us -> 18.1 us
  waiting for transfers between devices: 11.7 us -> 17.3 us
  Pallas kernels: 4.43 us -> 5.06 us
    all_to_all x1 -> x0, blocking collectives: 16.5 us -> none  [sliced(): got = lax.all_to_all(sends, ('rest', 'rep'), 0, 0, tiled=True)]
    all_to_all x0 -> x1, starting transfers between devices: none -> 6.3 us  [sliced(): got = lax.all_to_all(sends, ('rest', 'rep'), 0, 0, tiled=True)]
    ppermute x7 -> x10, waiting for transfers between devices: 11.7 us -> 17.3 us  [swap(): lax.ppermute(x, ('half', 'rest', 'rep'), [(i, i ^ mask) for i in range(si...]
    ppermute x7 -> x10, starting transfers between devices: 8.99 us -> 11.8 us  [swap(): lax.ppermute(x, ('half', 'rest', 'rep'), [(i, i ^ mask) for i in range(si...]
    pallas_call x1, Pallas kernels: 1.9 us -> 2.71 us  [sliced(): pl.pallas_call(first_kernel, out_shape=(jax.ShapeDtypeStruct((sources, de...]
  transfers between devices with their start and end apart: 7 -> 11, of which waited for: 4 -> 7; matrix products, arithmetic and copies ran while one was open for 0% -> 0% of each run, Pallas kernels for 4% -> 0%
where the time goes in v7:
time: 41.4 us; the launch traced here: 41.2 us
  starting transfers between devices  18.1 us (44%)
  waiting for transfers between devices  17.3 us (42%)
  Pallas kernels  5.06 us (12%)
  between operations  0.7 us (2%)
    ppermute x10, waiting for transfers between devices, swap(): lax.ppermute(x, ('half', 'rest', 'rep'), [(i, i ^ mask) for i in range(si...  17.3 us
    ppermute x10, starting transfers between devices, swap(): lax.ppermute(x, ('half', 'rest', 'rep'), [(i, i ^ mask) for i in range(si...  11.8 us
    all_to_all x1, starting transfers between devices, sliced(): got = lax.all_to_all(sends, ('rest', 'rep'), 0, 0, tiled=True)  6.3 us
    pallas_call x1, Pallas kernels, sliced(): pl.pallas_call(first_kernel, out_shape=(jax.ShapeDtypeStruct((sources, de...  2.71 us
    pallas_call x1, Pallas kernels, sliced(): pl.pallas_call(final_kernel, out_shape=(jax.ShapeDtypeStruct(u_one.shape,...  1.29 us
  transfers between devices with their start and end apart: 11, of which 7 were waited for; matrix products, arithmetic and copies ran while one was open for 0% of the time, Pallas kernels for 0%

profile of v7, /device:TPU:0, one launch (start us, length us, event | category | flops | bytes accessed | tf_op | source)
XLA Modules:
  0.0 41.2 jit_solution(13415759849867769874)
XLA Ops:
  0.6 2.7 %first.1 = (bf16[16,144,128]{2,1,0:T(8,128)(2,1)}, s32[8,128]{1,0:T(8,128)S(1)}, bf16[48,128]{1,0:T(8,128)(2,1)S(1)}) custom-call(s32[2]{0:T(128)} %one_hbm.1, s32[2]{0:T(128)} %two_hbm.1, s32[2]{0:T(128)} %three_hbm.1, s32[8]{0:T(128)} %owner_hbm.1, bf16[2,64,4096]{2,1,0:T(8,128)(2,1)} %tiles_hbm.1, bf16[32,1024]{1,0:T(8,128)(2,1)} %u_three_hbm.1, ...), custom_call_target="tpu_custom_call" | custom-call | tf_op jit(solution)/shard_map/first/pallas_call | solution.py:287
  3.3 6.3 %all-to-all-start = ((bf16[16,144,128]{2,1,0:T(8,128)(2,1)}), bf16[16,144,128]{2,1,0:T(8,128)(2,1)S(1)}, u32[]{:S(2)}, u32[]{:S(2)}) async-start(bf16[16,144,128]{2,1,0:T(8,128)(2,1)} %get-tuple-element.8), calls=%async_computation | async-start | bytes 1179648 | tf_op jit(solution)/shard_map/all_to_all | solution.py:307
  9.7 4.6 %collective-permute-start.3 = (bf16[48,128]{1,0:T(8,128)(2,1)S(1)}, bf16[48,128]{1,0:T(8,128)(2,1)S(1)}, u32[]{:S(2)}, u32[]{:S(2)}) collective-permute-start(bf16[48,128]{1,0:T(8,128)(2,1)S(1)} %get-tuple-element.9), channel_id=1, source_target_pairs={{0,29},{1,28},{2,31},{3,30},{4,25},{5,24},{6,27},{7,26},{8,21},{9,... | collective-permute-start | bytes 36872 | tf_op jit(solution)/shard_map/ppermute | solution.py:270
  14.3 0.3 collective-permute-start.2
  14.6 0.3 collective-permute-start.1
  14.9 2.1 %collective-permute-start = (bf16[48,128]{1,0:T(8,128)(2,1)S(1)}, bf16[48,128]{1,0:T(8,128)(2,1)S(1)}, u32[]{:S(2)}, u32[]{:S(2)}) collective-permute-start(bf16[48,128]{1,0:T(8,128)(2,1)S(1)} %get-tuple-element.9), channel_id=1, source_target_pairs={{0,17},{1,16},{2,19},{3,18},{4,21},{5,20},{6,23},{7,22},{8,25},{9,... | collective-permute-start | bytes 36872 | tf_op jit(solution)/shard_map/ppermute | solution.py:270
  17.0 4.8 %collective-permute-done.3.far3 = bf16[48,128]{1,0:T(8,128)(2,1)S(1)} collective-permute-done((bf16[48,128]{1,0:T(8,128)(2,1)S(1)}, bf16[48,128]{1,0:T(8,128)(2,1)S(1)}, u32[]{:S(2)}, u32[]{:S(2)}) %collective-permute-start.3) | collective-permute-done | bytes 12320 | tf_op jit(solution)/shard_map/ppermute | solution.py:270
  21.8 0.0 collective-permute-done.2.far2
  21.8 0.0 collective-permute-done.1.far1
  21.8 0.0 collective-permute-done.far0
  21.8 0.0 all-to-all-done.got
  21.8 0.7 %table.1 = (bf16[64,512]{1,0:T(8,128)(2,1)S(1)}, bf16[32,512]{1,0:T(8,128)(2,1)S(1)}) custom-call(bf16[16,144,128]{2,1,0:T(8,128)(2,1)S(1)} %all-to-all-done.got, bf16[48,128]{1,0:T(8,128)(2,1)S(1)} %collective-permute-done.far0, bf16[48,128]{1,0:T(8,128)(2,1)S(1)} %collective-permute-done.1.far1, bf16[48,128]{1,0:T(8,128)(2,1)S(1)} %collective-permute-done.2.far2, ...), custom_call_target="tpu_custom_call" | custom-call | tf_op jit(solution)/shard_map/table/pallas_call | solution.py:308
  22.6 0.7 %collective-permute-start.4 = (bf16[64,512]{1,0:T(8,128)(2,1)S(1)}, bf16[64,512]{1,0:T(8,128)(2,1)S(1)}, u32[]{:S(2)}, u32[]{:S(2)}) collective-permute-start(bf16[64,512]{1,0:T(8,128)(2,1)S(1)} %get-tuple-element.10.mine), channel_id=1, source_target_pairs={{0,17},{1,16},{2,19},{3,18},{4,21},{5,20},{6,23},{7,22},{8,25},{9,... | collective-permute-start | bytes 196616 | tf_op jit(solution)/shard_map/ppermute | solution.py:270
  23.3 5.5 %collective-permute-done.4.theirs = bf16[64,512]{1,0:T(8,128)(2,1)S(1)} collective-permute-done((bf16[64,512]{1,0:T(8,128)(2,1)S(1)}, bf16[64,512]{1,0:T(8,128)(2,1)S(1)}, u32[]{:S(2)}, u32[]{:S(2)}) %collective-permute-start.4) | collective-permute-done | bytes 65568 | tf_op jit(solution)/shard_map/ppermute | solution.py:270
  28.8 0.3 rows_part.1
  29.1 0.5 %collective-permute-start.5 = (bf16[32,512]{1,0:T(8,128)(2,1)S(1)}, bf16[32,512]{1,0:T(8,128)(2,1)S(1)}, u32[]{:S(2)}, u32[]{:S(2)}) collective-permute-start(bf16[32,512]{1,0:T(8,128)(2,1)S(1)} %rows_part.1), channel_id=1, source_target_pairs={{0,1},{1,0},{2,3},{3,2},{4,5},{5,4},{6,7},{7,6},{8,9},{9,8},{10,11... | collective-permute-start | bytes 98312 | tf_op jit(solution)/shard_map/ppermute | solution.py:270
  29.6 0.9 %collective-permute-done.5 = bf16[32,512]{1,0:T(8,128)(2,1)S(1)} collective-permute-done((bf16[32,512]{1,0:T(8,128)(2,1)S(1)}, bf16[32,512]{1,0:T(8,128)(2,1)S(1)}, u32[]{:S(2)}, u32[]{:S(2)}) %collective-permute-start.5) | collective-permute-done | bytes 32800 | tf_op jit(solution)/shard_map/ppermute | solution.py:270
  30.4 1.8 %collective-permute-start.8 = (bf16[32,512]{1,0:T(8,128)(2,1)S(1)}, bf16[32,512]{1,0:T(8,128)(2,1)S(1)}, u32[]{:S(2)}, u32[]{:S(2)}) collective-permute-start(bf16[32,512]{1,0:T(8,128)(2,1)S(1)} %add_convert_fusion.1), channel_id=1, source_target_pairs={{0,6},{1,7},{2,4},{3,5},{4,2},{5,3},{6,0},{7,1},{8,14},{9,15},{10,... | collective-permute-start | bytes 98312 | tf_op jit(solution)/shard_map/ppermute | solution.py:270
  32.2 0.9 %collective-permute-start.7 = (bf16[32,512]{1,0:T(8,128)(2,1)S(1)}, bf16[32,512]{1,0:T(8,128)(2,1)S(1)}, u32[]{:S(2)}, u32[]{:S(2)}) collective-permute-start(bf16[32,512]{1,0:T(8,128)(2,1)S(1)} %add_convert_fusion.1), channel_id=1, source_target_pairs={{0,5},{1,4},{2,7},{3,6},{4,1},{5,0},{6,3},{7,2},{8,13},{9,12},{10,... | collective-permute-start | bytes 98312 | tf_op jit(solution)/shard_map/ppermute | solution.py:270
  33.1 0.6 %collective-permute-start.6 = (bf16[32,512]{1,0:T(8,128)(2,1)S(1)}, bf16[32,512]{1,0:T(8,128)(2,1)S(1)}, u32[]{:S(2)}, u32[]{:S(2)}) collective-permute-start(bf16[32,512]{1,0:T(8,128)(2,1)S(1)} %add_convert_fusion.1), channel_id=1, source_target_pairs={{0,3},{1,2},{2,1},{3,0},{4,7},{5,6},{6,5},{7,4},{8,11},{9,10},{10,... | collective-permute-start | bytes 98312 | tf_op jit(solution)/shard_map/ppermute | solution.py:270
  33.7 1.6 %collective-permute-done.8 = bf16[32,512]{1,0:T(8,128)(2,1)S(1)} collective-permute-done((bf16[32,512]{1,0:T(8,128)(2,1)S(1)}, bf16[32,512]{1,0:T(8,128)(2,1)S(1)}, u32[]{:S(2)}, u32[]{:S(2)}) %collective-permute-start.8) | collective-permute-done | bytes 32800 | tf_op jit(solution)/shard_map/ppermute | solution.py:270
  35.3 0.6 %collective-permute-done.7 = bf16[32,512]{1,0:T(8,128)(2,1)S(1)} collective-permute-done((bf16[32,512]{1,0:T(8,128)(2,1)S(1)}, bf16[32,512]{1,0:T(8,128)(2,1)S(1)}, u32[]{:S(2)}, u32[]{:S(2)}) %collective-permute-start.7) | collective-permute-done | bytes 32800 | tf_op jit(solution)/shard_map/ppermute | solution.py:270
  35.9 0.6 %collective-permute-done.6 = bf16[32,512]{1,0:T(8,128)(2,1)S(1)} collective-permute-done((bf16[32,512]{1,0:T(8,128)(2,1)S(1)}, bf16[32,512]{1,0:T(8,128)(2,1)S(1)}, u32[]{:S(2)}, u32[]{:S(2)}) %collective-permute-start.6) | collective-permute-done | bytes 32800 | tf_op jit(solution)/shard_map/ppermute | solution.py:270
  36.5 0.1 collective-permute-start.9
  36.5 3.3 %collective-permute-done.9.b = bf16[32,512]{1,0:T(8,128)(2,1)S(1)} collective-permute-done((bf16[32,512]{1,0:T(8,128)(2,1)S(1)}, bf16[32,512]{1,0:T(8,128)(2,1)S(1)}, u32[]{:S(2)}, u32[]{:S(2)}) %collective-permute-start.9) | collective-permute-done | bytes 32800 | tf_op jit(solution)/shard_map/ppermute | solution.py:270
  39.9 1.3 %final.1 = (f32[32,64]{1,0:T(8,128)}, bf16[2,2048]{1,0:T(2,128)(2,1)}) custom-call(s32[8,128]{1,0:T(8,128)S(1)} %get-tuple-element.7.places, bf16[32,512]{1,0:T(8,128)(2,1)S(1)} %add_convert_fusion.a, bf16[32,512]{1,0:T(8,128)(2,1)S(1)} %collective-permute-done.9.b), custom_call_target="tpu_custom_call" | custom-call | tf_op jit(solution)/shard_map/final/pallas_call | solution.py:336
  (2 shorter events, 0.0 us)
Async XLA Ops:
  3.3 18.5 %all-to-all-start = ((bf16[16,144,128]{2,1,0:T(8,128)(2,1)}), bf16[16,144,128]{2,1,0:T(8,128)(2,1)S(1)}, u32[]{:S(2)}, u32[]{:S(2)}) async-start(bf16[16,144,128]{2,1,0:T(8,128)(2,1)} %get-tuple-element.8), calls=%async_computation | async-start | bytes 1179648 | tf_op jit(solution)/shard_map/all_to_all | solution.py:307
  9.7 12.2 %collective-permute-start.3 = (bf16[48,128]{1,0:T(8,128)(2,1)S(1)}, bf16[48,128]{1,0:T(8,128)(2,1)S(1)}, u32[]{:S(2)}, u32[]{:S(2)}) collective-permute-start(bf16[48,128]{1,0:T(8,128)(2,1)S(1)} %get-tuple-element.9), channel_id=1, source_target_pairs={{0,29},{1,28},{2,31},{3,30},{4,25},{5,24},{6,27},{7,26},{8,21},{9,... | collective-permute-start | bytes 36872 | tf_op jit(solution)/shard_map/ppermute | solution.py:270
  14.3 7.6 %collective-permute-start.2 = (bf16[48,128]{1,0:T(8,128)(2,1)S(1)}, bf16[48,128]{1,0:T(8,128)(2,1)S(1)}, u32[]{:S(2)}, u32[]{:S(2)}) collective-permute-start(bf16[48,128]{1,0:T(8,128)(2,1)S(1)} %get-tuple-element.9), channel_id=1, source_target_pairs={{0,25},{1,24},{2,27},{3,26},{4,29},{5,28},{6,31},{7,30},{8,17},{9,... | collective-permute-start | bytes 36872 | tf_op jit(solution)/shard_map/ppermute | solution.py:270
  14.6 7.3 %collective-permute-start.1 = (bf16[48,128]{1,0:T(8,128)(2,1)S(1)}, bf16[48,128]{1,0:T(8,128)(2,1)S(1)}, u32[]{:S(2)}, u32[]{:S(2)}) collective-permute-start(bf16[48,128]{1,0:T(8,128)(2,1)S(1)} %get-tuple-element.9), channel_id=1, source_target_pairs={{0,21},{1,20},{2,23},{3,22},{4,17},{5,16},{6,19},{7,18},{8,29},{9,... | collective-permute-start | bytes 36872 | tf_op jit(solution)/shard_map/ppermute | solution.py:270
  14.9 6.9 %collective-permute-start = (bf16[48,128]{1,0:T(8,128)(2,1)S(1)}, bf16[48,128]{1,0:T(8,128)(2,1)S(1)}, u32[]{:S(2)}, u32[]{:S(2)}) collective-permute-start(bf16[48,128]{1,0:T(8,128)(2,1)S(1)} %get-tuple-element.9), channel_id=1, source_target_pairs={{0,17},{1,16},{2,19},{3,18},{4,21},{5,20},{6,23},{7,22},{8,25},{9,... | collective-permute-start | bytes 36872 | tf_op jit(solution)/shard_map/ppermute | solution.py:270
  22.6 6.2 %collective-permute-start.4 = (bf16[64,512]{1,0:T(8,128)(2,1)S(1)}, bf16[64,512]{1,0:T(8,128)(2,1)S(1)}, u32[]{:S(2)}, u32[]{:S(2)}) collective-permute-start(bf16[64,512]{1,0:T(8,128)(2,1)S(1)} %get-tuple-element.10.mine), channel_id=1, source_target_pairs={{0,17},{1,16},{2,19},{3,18},{4,21},{5,20},{6,23},{7,22},{8,25},{9,... | collective-permute-start | bytes 196616 | tf_op jit(solution)/shard_map/ppermute | solution.py:270
  29.1 1.3 %collective-permute-start.5 = (bf16[32,512]{1,0:T(8,128)(2,1)S(1)}, bf16[32,512]{1,0:T(8,128)(2,1)S(1)}, u32[]{:S(2)}, u32[]{:S(2)}) collective-permute-start(bf16[32,512]{1,0:T(8,128)(2,1)S(1)} %rows_part.1), channel_id=1, source_target_pairs={{0,1},{1,0},{2,3},{3,2},{4,5},{5,4},{6,7},{7,6},{8,9},{9,8},{10,11... | collective-permute-start | bytes 98312 | tf_op jit(solution)/shard_map/ppermute | solution.py:270
  30.4 4.9 %collective-permute-start.8 = (bf16[32,512]{1,0:T(8,128)(2,1)S(1)}, bf16[32,512]{1,0:T(8,128)(2,1)S(1)}, u32[]{:S(2)}, u32[]{:S(2)}) collective-permute-start(bf16[32,512]{1,0:T(8,128)(2,1)S(1)} %add_convert_fusion.1), channel_id=1, source_target_pairs={{0,6},{1,7},{2,4},{3,5},{4,2},{5,3},{6,0},{7,1},{8,14},{9,15},{10,... | collective-permute-start | bytes 98312 | tf_op jit(solution)/shard_map/ppermute | solution.py:270
  32.2 3.7 %collective-permute-start.7 = (bf16[32,512]{1,0:T(8,128)(2,1)S(1)}, bf16[32,512]{1,0:T(8,128)(2,1)S(1)}, u32[]{:S(2)}, u32[]{:S(2)}) collective-permute-start(bf16[32,512]{1,0:T(8,128)(2,1)S(1)} %add_convert_fusion.1), channel_id=1, source_target_pairs={{0,5},{1,4},{2,7},{3,6},{4,1},{5,0},{6,3},{7,2},{8,13},{9,12},{10,... | collective-permute-start | bytes 98312 | tf_op jit(solution)/shard_map/ppermute | solution.py:270
  33.1 3.3 %collective-permute-start.6 = (bf16[32,512]{1,0:T(8,128)(2,1)S(1)}, bf16[32,512]{1,0:T(8,128)(2,1)S(1)}, u32[]{:S(2)}, u32[]{:S(2)}) collective-permute-start(bf16[32,512]{1,0:T(8,128)(2,1)S(1)} %add_convert_fusion.1), channel_id=1, source_target_pairs={{0,3},{1,2},{2,1},{3,0},{4,7},{5,6},{6,5},{7,4},{8,11},{9,10},{10,... | collective-permute-start | bytes 98312 | tf_op jit(solution)/shard_map/ppermute | solution.py:270
  36.5 3.4 %collective-permute-start.9 = (bf16[32,512]{1,0:T(8,128)(2,1)S(1)}, bf16[32,512]{1,0:T(8,128)(2,1)S(1)}, u32[]{:S(2)}, u32[]{:S(2)}) collective-permute-start(bf16[32,512]{1,0:T(8,128)(2,1)S(1)} %add_convert_fusion.a), channel_id=1, source_target_pairs={{0,9},{1,8},{2,11},{3,10},{4,13},{5,12},{6,15},{7,14},{8,1},{9,0},... | collective-permute-start | bytes 98312 | tf_op jit(solution)/shard_map/ppermute | solution.py:270

commit v8 on v7

--- a/solution.py
+++ b/solution.py
@@ -330,8 +330,8 @@
         name="rows_part",
     )(table, swap(table, size, far | core), readers)
     part = (part.astype(F32) + swap(part, size, core).astype(F32)).astype(BF16)
-    pair = part.astype(F32) + swap(part, size, x | core).astype(F32)
-    other = swap(part, size, y | core).astype(F32) + swap(part, size, x ^ y).astype(F32)
+    pair = part.astype(F32) + swap(part, size, y | core).astype(F32)
+    other = swap(part, size, x | core).astype(F32) + swap(part, size, x ^ y).astype(F32)
     part = (pair + other).astype(BF16)
     return pl.pallas_call(
         final_kernel,

time: 41.4 us -> 40.8 us (0.986)
  waiting for transfers between devices: 17.3 us -> 16.3 us
    ppermute x10, waiting for transfers between devices: 17.3 us -> 16.3 us  [swap(): lax.ppermute(x, ('half', 'rest', 'rep'), [(i, i ^ mask) for i in range(si...]
where the time goes in v8:
time: 40.8 us; the launch traced here: 40.5 us
  starting transfers between devices  18.5 us (45%)
  waiting for transfers between devices  16.3 us (40%)
  Pallas kernels  5.06 us (12%)
  between operations  0.69 us (2%)
    ppermute x10, waiting for transfers between devices, swap(): lax.ppermute(x, ('half', 'rest', 'rep'), [(i, i ^ mask) for i in range(si...  16.3 us
    ppermute x10, starting transfers between devices, swap(): lax.ppermute(x, ('half', 'rest', 'rep'), [(i, i ^ mask) for i in range(si...  12.2 us
    all_to_all x1, starting transfers between devices, sliced(): got = lax.all_to_all(sends, ('rest', 'rep'), 0, 0, tiled=True)  6.3 us
    pallas_call x1, Pallas kernels, sliced(): pl.pallas_call(first_kernel, out_shape=(jax.ShapeDtypeStruct((sources, de...  2.71 us
    pallas_call x1, Pallas kernels, sliced(): pl.pallas_call(final_kernel, out_shape=(jax.ShapeDtypeStruct(u_one.shape,...  1.29 us
  transfers between devices with their start and end apart: 11, of which 7 were waited for; matrix products, arithmetic and copies ran while one was open for 0% of the time, Pallas kernels for 0%

profile of v8, /device:TPU:0, one launch (start us, length us, event | category | flops | bytes accessed | tf_op | source)
XLA Modules:
  0.0 40.5 jit_solution(7955606854885531175)
XLA Ops:
  0.6 2.7 %first.1 = (bf16[16,144,128]{2,1,0:T(8,128)(2,1)}, s32[8,128]{1,0:T(8,128)S(1)}, bf16[48,128]{1,0:T(8,128)(2,1)S(1)}) custom-call(s32[2]{0:T(128)} %one_hbm.1, s32[2]{0:T(128)} %two_hbm.1, s32[2]{0:T(128)} %three_hbm.1, s32[8]{0:T(128)} %owner_hbm.1, bf16[2,64,4096]{2,1,0:T(8,128)(2,1)} %tiles_hbm.1, bf16[32,1024]{1,0:T(8,128)(2,1)} %u_three_hbm.1, ...), custom_call_target="tpu_custom_call" | custom-call | tf_op jit(solution)/shard_map/first/pallas_call | solution.py:287
  3.3 6.3 %all-to-all-start = ((bf16[16,144,128]{2,1,0:T(8,128)(2,1)}), bf16[16,144,128]{2,1,0:T(8,128)(2,1)S(1)}, u32[]{:S(2)}, u32[]{:S(2)}) async-start(bf16[16,144,128]{2,1,0:T(8,128)(2,1)} %get-tuple-element.8), calls=%async_computation | async-start | bytes 1179648 | tf_op jit(solution)/shard_map/all_to_all | solution.py:307
  9.7 4.6 %collective-permute-start.3 = (bf16[48,128]{1,0:T(8,128)(2,1)S(1)}, bf16[48,128]{1,0:T(8,128)(2,1)S(1)}, u32[]{:S(2)}, u32[]{:S(2)}) collective-permute-start(bf16[48,128]{1,0:T(8,128)(2,1)S(1)} %get-tuple-element.9), channel_id=1, source_target_pairs={{0,29},{1,28},{2,31},{3,30},{4,25},{5,24},{6,27},{7,26},{8,21},{9,... | collective-permute-start | bytes 36872 | tf_op jit(solution)/shard_map/ppermute | solution.py:270
  14.3 0.3 collective-permute-start.2
  14.6 0.3 collective-permute-start.1
  14.9 2.1 %collective-permute-start = (bf16[48,128]{1,0:T(8,128)(2,1)S(1)}, bf16[48,128]{1,0:T(8,128)(2,1)S(1)}, u32[]{:S(2)}, u32[]{:S(2)}) collective-permute-start(bf16[48,128]{1,0:T(8,128)(2,1)S(1)} %get-tuple-element.9), channel_id=1, source_target_pairs={{0,17},{1,16},{2,19},{3,18},{4,21},{5,20},{6,23},{7,22},{8,25},{9,... | collective-permute-start | bytes 36872 | tf_op jit(solution)/shard_map/ppermute | solution.py:270
  17.0 4.8 %collective-permute-done.3.far3 = bf16[48,128]{1,0:T(8,128)(2,1)S(1)} collective-permute-done((bf16[48,128]{1,0:T(8,128)(2,1)S(1)}, bf16[48,128]{1,0:T(8,128)(2,1)S(1)}, u32[]{:S(2)}, u32[]{:S(2)}) %collective-permute-start.3) | collective-permute-done | bytes 12320 | tf_op jit(solution)/shard_map/ppermute | solution.py:270
  21.8 0.0 collective-permute-done.2.far2
  21.8 0.0 collective-permute-done.1.far1
  21.8 0.0 collective-permute-done.far0
  21.8 0.0 all-to-all-done.got
  21.8 0.7 %table.1 = (bf16[64,512]{1,0:T(8,128)(2,1)S(1)}, bf16[32,512]{1,0:T(8,128)(2,1)S(1)}) custom-call(bf16[16,144,128]{2,1,0:T(8,128)(2,1)S(1)} %all-to-all-done.got, bf16[48,128]{1,0:T(8,128)(2,1)S(1)} %collective-permute-done.far0, bf16[48,128]{1,0:T(8,128)(2,1)S(1)} %collective-permute-done.1.far1, bf16[48,128]{1,0:T(8,128)(2,1)S(1)} %collective-permute-done.2.far2, ...), custom_call_target="tpu_custom_call" | custom-call | tf_op jit(solution)/shard_map/table/pallas_call | solution.py:308
  22.6 0.7 %collective-permute-start.4 = (bf16[64,512]{1,0:T(8,128)(2,1)S(1)}, bf16[64,512]{1,0:T(8,128)(2,1)S(1)}, u32[]{:S(2)}, u32[]{:S(2)}) collective-permute-start(bf16[64,512]{1,0:T(8,128)(2,1)S(1)} %get-tuple-element.10.mine), channel_id=1, source_target_pairs={{0,17},{1,16},{2,19},{3,18},{4,21},{5,20},{6,23},{7,22},{8,25},{9,... | collective-permute-start | bytes 196616 | tf_op jit(solution)/shard_map/ppermute | solution.py:270
  23.3 5.5 %collective-permute-done.4.theirs = bf16[64,512]{1,0:T(8,128)(2,1)S(1)} collective-permute-done((bf16[64,512]{1,0:T(8,128)(2,1)S(1)}, bf16[64,512]{1,0:T(8,128)(2,1)S(1)}, u32[]{:S(2)}, u32[]{:S(2)}) %collective-permute-start.4) | collective-permute-done | bytes 65568 | tf_op jit(solution)/shard_map/ppermute | solution.py:270
  28.8 0.3 rows_part.1
  29.1 0.5 %collective-permute-start.5 = (bf16[32,512]{1,0:T(8,128)(2,1)S(1)}, bf16[32,512]{1,0:T(8,128)(2,1)S(1)}, u32[]{:S(2)}, u32[]{:S(2)}) collective-permute-start(bf16[32,512]{1,0:T(8,128)(2,1)S(1)} %rows_part.1), channel_id=1, source_target_pairs={{0,1},{1,0},{2,3},{3,2},{4,5},{5,4},{6,7},{7,6},{8,9},{9,8},{10,11... | collective-permute-start | bytes 98312 | tf_op jit(solution)/shard_map/ppermute | solution.py:270
  29.6 0.9 %collective-permute-done.5 = bf16[32,512]{1,0:T(8,128)(2,1)S(1)} collective-permute-done((bf16[32,512]{1,0:T(8,128)(2,1)S(1)}, bf16[32,512]{1,0:T(8,128)(2,1)S(1)}, u32[]{:S(2)}, u32[]{:S(2)}) %collective-permute-start.5) | collective-permute-done | bytes 32800 | tf_op jit(solution)/shard_map/ppermute | solution.py:270
  30.4 1.8 %collective-permute-start.8 = (bf16[32,512]{1,0:T(8,128)(2,1)S(1)}, bf16[32,512]{1,0:T(8,128)(2,1)S(1)}, u32[]{:S(2)}, u32[]{:S(2)}) collective-permute-start(bf16[32,512]{1,0:T(8,128)(2,1)S(1)} %add_convert_fusion.1), channel_id=1, source_target_pairs={{0,6},{1,7},{2,4},{3,5},{4,2},{5,3},{6,0},{7,1},{8,14},{9,15},{10,... | collective-permute-start | bytes 98312 | tf_op jit(solution)/shard_map/ppermute | solution.py:270
  32.2 0.2 collective-permute-start.7
  32.5 1.3 %collective-permute-start.6 = (bf16[32,512]{1,0:T(8,128)(2,1)S(1)}, bf16[32,512]{1,0:T(8,128)(2,1)S(1)}, u32[]{:S(2)}, u32[]{:S(2)}) collective-permute-start(bf16[32,512]{1,0:T(8,128)(2,1)S(1)} %add_convert_fusion.1), channel_id=1, source_target_pairs={{0,5},{1,4},{2,7},{3,6},{4,1},{5,0},{6,3},{7,2},{8,13},{9,12},{10,... | collective-permute-start | bytes 98312 | tf_op jit(solution)/shard_map/ppermute | solution.py:270
  33.7 1.6 %collective-permute-done.8 = bf16[32,512]{1,0:T(8,128)(2,1)S(1)} collective-permute-done((bf16[32,512]{1,0:T(8,128)(2,1)S(1)}, bf16[32,512]{1,0:T(8,128)(2,1)S(1)}, u32[]{:S(2)}, u32[]{:S(2)}) %collective-permute-start.8) | collective-permute-done | bytes 32800 | tf_op jit(solution)/shard_map/ppermute | solution.py:270
  35.3 0.3 collective-permute-done.7
  35.7 0.1 collective-permute-done.6
  35.8 0.4 %collective-permute-start.9 = (bf16[32,512]{1,0:T(8,128)(2,1)S(1)}, bf16[32,512]{1,0:T(8,128)(2,1)S(1)}, u32[]{:S(2)}, u32[]{:S(2)}) collective-permute-start(bf16[32,512]{1,0:T(8,128)(2,1)S(1)} %add_convert_fusion.a), channel_id=1, source_target_pairs={{0,9},{1,8},{2,11},{3,10},{4,13},{5,12},{6,15},{7,14},{8,1},{9,0},... | collective-permute-start | bytes 98312 | tf_op jit(solution)/shard_map/ppermute | solution.py:270
  36.2 3.0 %collective-permute-done.9.b = bf16[32,512]{1,0:T(8,128)(2,1)S(1)} collective-permute-done((bf16[32,512]{1,0:T(8,128)(2,1)S(1)}, bf16[32,512]{1,0:T(8,128)(2,1)S(1)}, u32[]{:S(2)}, u32[]{:S(2)}) %collective-permute-start.9) | collective-permute-done | bytes 32800 | tf_op jit(solution)/shard_map/ppermute | solution.py:270
  39.2 1.3 %final.1 = (f32[32,64]{1,0:T(8,128)}, bf16[2,2048]{1,0:T(2,128)(2,1)}) custom-call(s32[8,128]{1,0:T(8,128)S(1)} %get-tuple-element.7.places, bf16[32,512]{1,0:T(8,128)(2,1)S(1)} %add_convert_fusion.a, bf16[32,512]{1,0:T(8,128)(2,1)S(1)} %collective-permute-done.9.b), custom_call_target="tpu_custom_call" | custom-call | tf_op jit(solution)/shard_map/final/pallas_call | solution.py:336
  (2 shorter events, 0.0 us)
Async XLA Ops:
  3.3 18.5 %all-to-all-start = ((bf16[16,144,128]{2,1,0:T(8,128)(2,1)}), bf16[16,144,128]{2,1,0:T(8,128)(2,1)S(1)}, u32[]{:S(2)}, u32[]{:S(2)}) async-start(bf16[16,144,128]{2,1,0:T(8,128)(2,1)} %get-tuple-element.8), calls=%async_computation | async-start | bytes 1179648 | tf_op jit(solution)/shard_map/all_to_all | solution.py:307
  9.7 12.2 %collective-permute-start.3 = (bf16[48,128]{1,0:T(8,128)(2,1)S(1)}, bf16[48,128]{1,0:T(8,128)(2,1)S(1)}, u32[]{:S(2)}, u32[]{:S(2)}) collective-permute-start(bf16[48,128]{1,0:T(8,128)(2,1)S(1)} %get-tuple-element.9), channel_id=1, source_target_pairs={{0,29},{1,28},{2,31},{3,30},{4,25},{5,24},{6,27},{7,26},{8,21},{9,... | collective-permute-start | bytes 36872 | tf_op jit(solution)/shard_map/ppermute | solution.py:270
  14.3 7.6 %collective-permute-start.2 = (bf16[48,128]{1,0:T(8,128)(2,1)S(1)}, bf16[48,128]{1,0:T(8,128)(2,1)S(1)}, u32[]{:S(2)}, u32[]{:S(2)}) collective-permute-start(bf16[48,128]{1,0:T(8,128)(2,1)S(1)} %get-tuple-element.9), channel_id=1, source_target_pairs={{0,25},{1,24},{2,27},{3,26},{4,29},{5,28},{6,31},{7,30},{8,17},{9,... | collective-permute-start | bytes 36872 | tf_op jit(solution)/shard_map/ppermute | solution.py:270
  14.6 7.3 %collective-permute-start.1 = (bf16[48,128]{1,0:T(8,128)(2,1)S(1)}, bf16[48,128]{1,0:T(8,128)(2,1)S(1)}, u32[]{:S(2)}, u32[]{:S(2)}) collective-permute-start(bf16[48,128]{1,0:T(8,128)(2,1)S(1)} %get-tuple-element.9), channel_id=1, source_target_pairs={{0,21},{1,20},{2,23},{3,22},{4,17},{5,16},{6,19},{7,18},{8,29},{9,... | collective-permute-start | bytes 36872 | tf_op jit(solution)/shard_map/ppermute | solution.py:270
  14.9 6.9 %collective-permute-start = (bf16[48,128]{1,0:T(8,128)(2,1)S(1)}, bf16[48,128]{1,0:T(8,128)(2,1)S(1)}, u32[]{:S(2)}, u32[]{:S(2)}) collective-permute-start(bf16[48,128]{1,0:T(8,128)(2,1)S(1)} %get-tuple-element.9), channel_id=1, source_target_pairs={{0,17},{1,16},{2,19},{3,18},{4,21},{5,20},{6,23},{7,22},{8,25},{9,... | collective-permute-start | bytes 36872 | tf_op jit(solution)/shard_map/ppermute | solution.py:270
  22.6 6.2 %collective-permute-start.4 = (bf16[64,512]{1,0:T(8,128)(2,1)S(1)}, bf16[64,512]{1,0:T(8,128)(2,1)S(1)}, u32[]{:S(2)}, u32[]{:S(2)}) collective-permute-start(bf16[64,512]{1,0:T(8,128)(2,1)S(1)} %get-tuple-element.10.mine), channel_id=1, source_target_pairs={{0,17},{1,16},{2,19},{3,18},{4,21},{5,20},{6,23},{7,22},{8,25},{9,... | collective-permute-start | bytes 196616 | tf_op jit(solution)/shard_map/ppermute | solution.py:270
  29.1 1.3 %collective-permute-start.5 = (bf16[32,512]{1,0:T(8,128)(2,1)S(1)}, bf16[32,512]{1,0:T(8,128)(2,1)S(1)}, u32[]{:S(2)}, u32[]{:S(2)}) collective-permute-start(bf16[32,512]{1,0:T(8,128)(2,1)S(1)} %rows_part.1), channel_id=1, source_target_pairs={{0,1},{1,0},{2,3},{3,2},{4,5},{5,4},{6,7},{7,6},{8,9},{9,8},{10,11... | collective-permute-start | bytes 98312 | tf_op jit(solution)/shard_map/ppermute | solution.py:270
  30.4 4.9 %collective-permute-start.8 = (bf16[32,512]{1,0:T(8,128)(2,1)S(1)}, bf16[32,512]{1,0:T(8,128)(2,1)S(1)}, u32[]{:S(2)}, u32[]{:S(2)}) collective-permute-start(bf16[32,512]{1,0:T(8,128)(2,1)S(1)} %add_convert_fusion.1), channel_id=1, source_target_pairs={{0,6},{1,7},{2,4},{3,5},{4,2},{5,3},{6,0},{7,1},{8,14},{9,15},{10,... | collective-permute-start | bytes 98312 | tf_op jit(solution)/shard_map/ppermute | solution.py:270
  32.2 3.4 %collective-permute-start.7 = (bf16[32,512]{1,0:T(8,128)(2,1)S(1)}, bf16[32,512]{1,0:T(8,128)(2,1)S(1)}, u32[]{:S(2)}, u32[]{:S(2)}) collective-permute-start(bf16[32,512]{1,0:T(8,128)(2,1)S(1)} %add_convert_fusion.1), channel_id=1, source_target_pairs={{0,3},{1,2},{2,1},{3,0},{4,7},{5,6},{6,5},{7,4},{8,11},{9,10},{10,... | collective-permute-start | bytes 98312 | tf_op jit(solution)/shard_map/ppermute | solution.py:270
  32.5 3.3 %collective-permute-start.6 = (bf16[32,512]{1,0:T(8,128)(2,1)S(1)}, bf16[32,512]{1,0:T(8,128)(2,1)S(1)}, u32[]{:S(2)}, u32[]{:S(2)}) collective-permute-start(bf16[32,512]{1,0:T(8,128)(2,1)S(1)} %add_convert_fusion.1), channel_id=1, source_target_pairs={{0,5},{1,4},{2,7},{3,6},{4,1},{5,0},{6,3},{7,2},{8,13},{9,12},{10,... | collective-permute-start | bytes 98312 | tf_op jit(solution)/shard_map/ppermute | solution.py:270
  35.8 3.4 %collective-permute-start.9 = (bf16[32,512]{1,0:T(8,128)(2,1)S(1)}, bf16[32,512]{1,0:T(8,128)(2,1)S(1)}, u32[]{:S(2)}, u32[]{:S(2)}) collective-permute-start(bf16[32,512]{1,0:T(8,128)(2,1)S(1)} %add_convert_fusion.a), channel_id=1, source_target_pairs={{0,9},{1,8},{2,11},{3,10},{4,13},{5,12},{6,15},{7,14},{8,1},{9,0},... | collective-permute-start | bytes 98312 | tf_op jit(solution)/shard_map/ppermute | solution.py:270

commit v9 on v8

--- a/solution.py
+++ b/solution.py
@@ -228,18 +228,21 @@
     readers[...] = jnp.concatenate([one[p][:, :half] for p in range(owners)], axis=1).astype(BF16)
 
 
-def rows_kernel(mine, theirs, readers, out):
-    high, low = split(mine[...].astype(F32) + theirs[...].astype(F32))
-    project = (nt(readers[...], high) + nt(readers[...], low)).astype(BF16)
-    part = jnp.dot(project, high, preferred_element_type=F32)
-    part += jnp.dot(project, low, preferred_element_type=F32)
+def known_kernel(mine, readers, out):
+    out[...] = nt(readers[...], mine[...])
+
+
+def rows_kernel(mine, theirs, readers, known, out):
+    project = (known[...] + nt(readers[...], theirs[...])).astype(BF16)
+    part = jnp.dot(project, mine[...], preferred_element_type=F32)
+    part += jnp.dot(project, theirs[...], preferred_element_type=F32)
     out[...] = part.astype(BF16)
 
 
-def final_kernel(places, a, b, factor, tile_factor, table):
+def final_kernel(places, a, b, c, d, factor, tile_factor, table):
     rank, rows_total = a.shape
     half = LANES // 2
-    rows = a[...].astype(F32) + b[...].astype(F32)
+    rows = (a[...].astype(F32) + b[...].astype(F32)) + (c[...].astype(F32) + d[...].astype(F32))
     table[...] = rows
     g0 = dot3(rows, rows, 1)
     eye = (row_iota(g0.shape) == lane_iota(g0.shape)).astype(F32)
@@ -321,30 +324,37 @@
         compiler_params=narrow,
         name="table",
     )(got, *theirs)
+    known = pl.pallas_call(
+        known_kernel,
+        out_shape=jax.ShapeDtypeStruct((rank, 2 * rank), F32),
+        in_specs=[vmem] * 2,
+        out_specs=vmem,
+        compiler_params=narrow,
+        name="known",
+    )(table, readers)
     part = pl.pallas_call(
         rows_kernel,
         out_shape=jax.ShapeDtypeStruct((rank, rows_total), BF16),
-        in_specs=[vmem] * 3,
+        in_specs=[vmem] * 4,
         out_specs=vmem,
         compiler_params=narrow,
         name="rows_part",
-    )(table, swap(table, size, far | core), readers)
+    )(table, swap(table, size, far | core), readers, known)
     part = (part.astype(F32) + swap(part, size, core).astype(F32)).astype(BF16)
-    pair = part.astype(F32) + swap(part, size, y | core).astype(F32)
-    other = swap(part, size, x | core).astype(F32) + swap(part, size, x ^ y).astype(F32)
-    part = (pair + other).astype(BF16)
+    part = (part.astype(F32) + swap(part, size, near | core).astype(F32)).astype(BF16)
+    rest = [swap(part, size, mask) for mask in (y | core, x | core, x ^ y)]
     return pl.pallas_call(
         final_kernel,
         out_shape=(
             jax.ShapeDtypeStruct(u_one.shape, F32),
             jax.ShapeDtypeStruct((count, rank * width), BF16),
         ),
-        in_specs=[vmem] * 3,
+        in_specs=[vmem] * 5,
         out_specs=(vmem, vmem),
         scratch_shapes=[pltpu.VMEM((rank, rows_total), F32)],
         compiler_params=narrow,
         name="final",
-    )(places, part, swap(part, size, near | core))
+    )(places, part, *rest)
 
 
 def fits(mesh, tiles, block_one, block_two, block_three, owner_map, u_one, u_two, u_three):

time: 40.8 us -> 40.6 us (level)
  no operation moved by 1% of the time
where the time goes in v9:
time: 40.6 us; the launch traced here: 40.4 us
  starting transfers between devices  18.1 us (45%)
  waiting for transfers between devices  16.5 us (41%)
  Pallas kernels  5.11 us (13%)
  between operations  0.69 us (2%)
    ppermute x10, waiting for transfers between devices, swap(): lax.ppermute(x, ('half', 'rest', 'rep'), [(i, i ^ mask) for i in range(si...  16.5 us
    ppermute x10, starting transfers between devices, swap(): lax.ppermute(x, ('half', 'rest', 'rep'), [(i, i ^ mask) for i in range(si...  11.8 us
    all_to_all x1, starting transfers between devices, sliced(): got = lax.all_to_all(sends, ('rest', 'rep'), 0, 0, tiled=True)  6.3 us
    pallas_call x1, Pallas kernels, sliced(): pl.pallas_call(first_kernel, out_shape=(jax.ShapeDtypeStruct((sources, de...  2.71 us
    pallas_call x1, Pallas kernels, sliced(): pl.pallas_call(final_kernel, out_shape=(jax.ShapeDtypeStruct(u_one.shape,...  1.29 us
  transfers between devices with their start and end apart: 11, of which 7 were waited for; matrix products, arithmetic and copies ran while one was open for 0% of the time, Pallas kernels for 0%

profile of v9, /device:TPU:0, one launch (start us, length us, event | category | flops | bytes accessed | tf_op | source)
XLA Modules:
  0.0 40.4 jit_solution(18241970305461698572)
XLA Ops:
  0.6 2.7 %first.1 = (bf16[16,144,128]{2,1,0:T(8,128)(2,1)}, s32[8,128]{1,0:T(8,128)S(1)}, bf16[48,128]{1,0:T(8,128)(2,1)S(1)}) custom-call(s32[2]{0:T(128)} %one_hbm.1, s32[2]{0:T(128)} %two_hbm.1, s32[2]{0:T(128)} %three_hbm.1, s32[8]{0:T(128)} %owner_hbm.1, bf16[2,64,4096]{2,1,0:T(8,128)(2,1)} %tiles_hbm.1, bf16[32,1024]{1,0:T(8,128)(2,1)} %u_three_hbm.1, ...), custom_call_target="tpu_custom_call" | custom-call | tf_op jit(solution)/shard_map/first/pallas_call | solution.py:290
  3.4 6.3 %all-to-all-start = ((bf16[16,144,128]{2,1,0:T(8,128)(2,1)}), bf16[16,144,128]{2,1,0:T(8,128)(2,1)S(1)}, u32[]{:S(2)}, u32[]{:S(2)}) async-start(bf16[16,144,128]{2,1,0:T(8,128)(2,1)} %get-tuple-element.8), calls=%async_computation | async-start | bytes 1179648 | tf_op jit(solution)/shard_map/all_to_all | solution.py:310
  9.7 4.6 %collective-permute-start.3 = (bf16[48,128]{1,0:T(8,128)(2,1)S(1)}, bf16[48,128]{1,0:T(8,128)(2,1)S(1)}, u32[]{:S(2)}, u32[]{:S(2)}) collective-permute-start(bf16[48,128]{1,0:T(8,128)(2,1)S(1)} %get-tuple-element.9), channel_id=1, source_target_pairs={{0,29},{1,28},{2,31},{3,30},{4,25},{5,24},{6,27},{7,26},{8,21},{9,... | collective-permute-start | bytes 36872 | tf_op jit(solution)/shard_map/ppermute | solution.py:273
  14.3 0.3 collective-permute-start.2
  14.6 0.3 collective-permute-start.1
  14.9 2.1 %collective-permute-start = (bf16[48,128]{1,0:T(8,128)(2,1)S(1)}, bf16[48,128]{1,0:T(8,128)(2,1)S(1)}, u32[]{:S(2)}, u32[]{:S(2)}) collective-permute-start(bf16[48,128]{1,0:T(8,128)(2,1)S(1)} %get-tuple-element.9), channel_id=1, source_target_pairs={{0,17},{1,16},{2,19},{3,18},{4,21},{5,20},{6,23},{7,22},{8,25},{9,... | collective-permute-start | bytes 36872 | tf_op jit(solution)/shard_map/ppermute | solution.py:273
  17.0 4.8 %collective-permute-done.3.far3 = bf16[48,128]{1,0:T(8,128)(2,1)S(1)} collective-permute-done((bf16[48,128]{1,0:T(8,128)(2,1)S(1)}, bf16[48,128]{1,0:T(8,128)(2,1)S(1)}, u32[]{:S(2)}, u32[]{:S(2)}) %collective-permute-start.3) | collective-permute-done | bytes 12320 | tf_op jit(solution)/shard_map/ppermute | solution.py:273
  21.8 0.0 collective-permute-done.2.far2
  21.8 0.0 collective-permute-done.1.far1
  21.8 0.0 collective-permute-done.far0
  21.8 0.0 all-to-all-done.got
  21.8 0.7 %table.1 = (bf16[64,512]{1,0:T(8,128)(2,1)S(1)}, bf16[32,512]{1,0:T(8,128)(2,1)S(1)}) custom-call(bf16[16,144,128]{2,1,0:T(8,128)(2,1)S(1)} %all-to-all-done.got, bf16[48,128]{1,0:T(8,128)(2,1)S(1)} %collective-permute-done.far0, bf16[48,128]{1,0:T(8,128)(2,1)S(1)} %collective-permute-done.1.far1, bf16[48,128]{1,0:T(8,128)(2,1)S(1)} %collective-permute-done.2.far2, ...), custom_call_target="tpu_custom_call" | custom-call | tf_op jit(solution)/shard_map/table/pallas_call | solution.py:311
  22.6 0.7 %collective-permute-start.4 = (bf16[64,512]{1,0:T(8,128)(2,1)S(1)}, bf16[64,512]{1,0:T(8,128)(2,1)S(1)}, u32[]{:S(2)}, u32[]{:S(2)}) collective-permute-start(bf16[64,512]{1,0:T(8,128)(2,1)S(1)} %get-tuple-element.10.mine), channel_id=1, source_target_pairs={{0,17},{1,16},{2,19},{3,18},{4,21},{5,20},{6,23},{7,22},{8,25},{9,... | collective-permute-start | bytes 196616 | tf_op jit(solution)/shard_map/ppermute | solution.py:273
  23.3 0.1 known.1
  23.4 5.4 %collective-permute-done.4.theirs = bf16[64,512]{1,0:T(8,128)(2,1)S(1)} collective-permute-done((bf16[64,512]{1,0:T(8,128)(2,1)S(1)}, bf16[64,512]{1,0:T(8,128)(2,1)S(1)}, u32[]{:S(2)}, u32[]{:S(2)}) %collective-permute-start.4) | collective-permute-done | bytes 65568 | tf_op jit(solution)/shard_map/ppermute | solution.py:273
  28.8 0.2 rows_part.1
  29.0 0.4 %collective-permute-start.5 = (bf16[32,512]{1,0:T(8,128)(2,1)S(1)}, bf16[32,512]{1,0:T(8,128)(2,1)S(1)}, u32[]{:S(2)}, u32[]{:S(2)}) collective-permute-start(bf16[32,512]{1,0:T(8,128)(2,1)S(1)} %rows_part.1), channel_id=1, source_target_pairs={{0,1},{1,0},{2,3},{3,2},{4,5},{5,4},{6,7},{7,6},{8,9},{9,8},{10,11... | collective-permute-start | bytes 98312 | tf_op jit(solution)/shard_map/ppermute | solution.py:273
  29.4 0.9 %collective-permute-done.5 = bf16[32,512]{1,0:T(8,128)(2,1)S(1)} collective-permute-done((bf16[32,512]{1,0:T(8,128)(2,1)S(1)}, bf16[32,512]{1,0:T(8,128)(2,1)S(1)}, u32[]{:S(2)}, u32[]{:S(2)}) %collective-permute-start.5) | collective-permute-done | bytes 32800 | tf_op jit(solution)/shard_map/ppermute | solution.py:273
  30.3 0.1 collective-permute-start.6
  30.4 3.3 %collective-permute-done.6 = bf16[32,512]{1,0:T(8,128)(2,1)S(1)} collective-permute-done((bf16[32,512]{1,0:T(8,128)(2,1)S(1)}, bf16[32,512]{1,0:T(8,128)(2,1)S(1)}, u32[]{:S(2)}, u32[]{:S(2)}) %collective-permute-start.6) | collective-permute-done | bytes 32800 | tf_op jit(solution)/shard_map/ppermute | solution.py:273
  33.7 1.8 %collective-permute-start.9 = (bf16[32,512]{1,0:T(8,128)(2,1)S(1)}, bf16[32,512]{1,0:T(8,128)(2,1)S(1)}, u32[]{:S(2)}, u32[]{:S(2)}) collective-permute-start(bf16[32,512]{1,0:T(8,128)(2,1)S(1)} %add_convert_fusion.a), channel_id=1, source_target_pairs={{0,6},{1,7},{2,4},{3,5},{4,2},{5,3},{6,0},{7,1},{8,14},{9,15},{10,... | collective-permute-start | bytes 98312 | tf_op jit(solution)/shard_map/ppermute | solution.py:273
  35.5 0.2 collective-permute-start.8
  35.8 1.3 %collective-permute-start.7 = (bf16[32,512]{1,0:T(8,128)(2,1)S(1)}, bf16[32,512]{1,0:T(8,128)(2,1)S(1)}, u32[]{:S(2)}, u32[]{:S(2)}) collective-permute-start(bf16[32,512]{1,0:T(8,128)(2,1)S(1)} %add_convert_fusion.a), channel_id=1, source_target_pairs={{0,5},{1,4},{2,7},{3,6},{4,1},{5,0},{6,3},{7,2},{8,13},{9,12},{10,... | collective-permute-start | bytes 98312 | tf_op jit(solution)/shard_map/ppermute | solution.py:273
  37.0 1.6 %collective-permute-done.9.d = bf16[32,512]{1,0:T(8,128)(2,1)S(1)} collective-permute-done((bf16[32,512]{1,0:T(8,128)(2,1)S(1)}, bf16[32,512]{1,0:T(8,128)(2,1)S(1)}, u32[]{:S(2)}, u32[]{:S(2)}) %collective-permute-start.9) | collective-permute-done | bytes 32800 | tf_op jit(solution)/shard_map/ppermute | solution.py:273
  38.6 0.3 collective-permute-done.8.c
  39.0 0.1 collective-permute-done.7.b
  39.1 1.3 %final.1 = (f32[32,64]{1,0:T(8,128)}, bf16[2,2048]{1,0:T(2,128)(2,1)}) custom-call(s32[8,128]{1,0:T(8,128)S(1)} %get-tuple-element.7.places, bf16[32,512]{1,0:T(8,128)(2,1)S(1)} %add_convert_fusion.a, bf16[32,512]{1,0:T(8,128)(2,1)S(1)} %collective-permute-done.7.b, bf16[32,512]{1,0:T(8,128)(2,1)S(1)} %collective-permute-done.8.c, ...), custom_call_target="tpu_custom_call" | custom-call | tf_op jit(solution)/shard_map/final/pallas_call | solution.py:346
  (2 shorter events, 0.0 us)
Async XLA Ops:
  3.4 18.5 %all-to-all-start = ((bf16[16,144,128]{2,1,0:T(8,128)(2,1)}), bf16[16,144,128]{2,1,0:T(8,128)(2,1)S(1)}, u32[]{:S(2)}, u32[]{:S(2)}) async-start(bf16[16,144,128]{2,1,0:T(8,128)(2,1)} %get-tuple-element.8), calls=%async_computation | async-start | bytes 1179648 | tf_op jit(solution)/shard_map/all_to_all | solution.py:310
  9.7 12.2 %collective-permute-start.3 = (bf16[48,128]{1,0:T(8,128)(2,1)S(1)}, bf16[48,128]{1,0:T(8,128)(2,1)S(1)}, u32[]{:S(2)}, u32[]{:S(2)}) collective-permute-start(bf16[48,128]{1,0:T(8,128)(2,1)S(1)} %get-tuple-element.9), channel_id=1, source_target_pairs={{0,29},{1,28},{2,31},{3,30},{4,25},{5,24},{6,27},{7,26},{8,21},{9,... | collective-permute-start | bytes 36872 | tf_op jit(solution)/shard_map/ppermute | solution.py:273
  14.3 7.6 %collective-permute-start.2 = (bf16[48,128]{1,0:T(8,128)(2,1)S(1)}, bf16[48,128]{1,0:T(8,128)(2,1)S(1)}, u32[]{:S(2)}, u32[]{:S(2)}) collective-permute-start(bf16[48,128]{1,0:T(8,128)(2,1)S(1)} %get-tuple-element.9), channel_id=1, source_target_pairs={{0,25},{1,24},{2,27},{3,26},{4,29},{5,28},{6,31},{7,30},{8,17},{9,... | collective-permute-start | bytes 36872 | tf_op jit(solution)/shard_map/ppermute | solution.py:273
  14.6 7.3 %collective-permute-start.1 = (bf16[48,128]{1,0:T(8,128)(2,1)S(1)}, bf16[48,128]{1,0:T(8,128)(2,1)S(1)}, u32[]{:S(2)}, u32[]{:S(2)}) collective-permute-start(bf16[48,128]{1,0:T(8,128)(2,1)S(1)} %get-tuple-element.9), channel_id=1, source_target_pairs={{0,21},{1,20},{2,23},{3,22},{4,17},{5,16},{6,19},{7,18},{8,29},{9,... | collective-permute-start | bytes 36872 | tf_op jit(solution)/shard_map/ppermute | solution.py:273
  14.9 6.9 %collective-permute-start = (bf16[48,128]{1,0:T(8,128)(2,1)S(1)}, bf16[48,128]{1,0:T(8,128)(2,1)S(1)}, u32[]{:S(2)}, u32[]{:S(2)}) collective-permute-start(bf16[48,128]{1,0:T(8,128)(2,1)S(1)} %get-tuple-element.9), channel_id=1, source_target_pairs={{0,17},{1,16},{2,19},{3,18},{4,21},{5,20},{6,23},{7,22},{8,25},{9,... | collective-permute-start | bytes 36872 | tf_op jit(solution)/shard_map/ppermute | solution.py:273
  22.6 6.2 %collective-permute-start.4 = (bf16[64,512]{1,0:T(8,128)(2,1)S(1)}, bf16[64,512]{1,0:T(8,128)(2,1)S(1)}, u32[]{:S(2)}, u32[]{:S(2)}) collective-permute-start(bf16[64,512]{1,0:T(8,128)(2,1)S(1)} %get-tuple-element.10.mine), channel_id=1, source_target_pairs={{0,17},{1,16},{2,19},{3,18},{4,21},{5,20},{6,23},{7,22},{8,25},{9,... | collective-permute-start | bytes 196616 | tf_op jit(solution)/shard_map/ppermute | solution.py:273
  29.0 1.3 %collective-permute-start.5 = (bf16[32,512]{1,0:T(8,128)(2,1)S(1)}, bf16[32,512]{1,0:T(8,128)(2,1)S(1)}, u32[]{:S(2)}, u32[]{:S(2)}) collective-permute-start(bf16[32,512]{1,0:T(8,128)(2,1)S(1)} %rows_part.1), channel_id=1, source_target_pairs={{0,1},{1,0},{2,3},{3,2},{4,5},{5,4},{6,7},{7,6},{8,9},{9,8},{10,11... | collective-permute-start | bytes 98312 | tf_op jit(solution)/shard_map/ppermute | solution.py:273
  30.3 3.4 %collective-permute-start.6 = (bf16[32,512]{1,0:T(8,128)(2,1)S(1)}, bf16[32,512]{1,0:T(8,128)(2,1)S(1)}, u32[]{:S(2)}, u32[]{:S(2)}) collective-permute-start(bf16[32,512]{1,0:T(8,128)(2,1)S(1)} %add_convert_fusion.1), channel_id=1, source_target_pairs={{0,9},{1,8},{2,11},{3,10},{4,13},{5,12},{6,15},{7,14},{8,1},{9,0},... | collective-permute-start | bytes 98312 | tf_op jit(solution)/shard_map/ppermute | solution.py:273
  33.7 4.9 %collective-permute-start.9 = (bf16[32,512]{1,0:T(8,128)(2,1)S(1)}, bf16[32,512]{1,0:T(8,128)(2,1)S(1)}, u32[]{:S(2)}, u32[]{:S(2)}) collective-permute-start(bf16[32,512]{1,0:T(8,128)(2,1)S(1)} %add_convert_fusion.a), channel_id=1, source_target_pairs={{0,6},{1,7},{2,4},{3,5},{4,2},{5,3},{6,0},{7,1},{8,14},{9,15},{10,... | collective-permute-start | bytes 98312 | tf_op jit(solution)/shard_map/ppermute | solution.py:273
  35.5 3.4 %collective-permute-start.8 = (bf16[32,512]{1,0:T(8,128)(2,1)S(1)}, bf16[32,512]{1,0:T(8,128)(2,1)S(1)}, u32[]{:S(2)}, u32[]{:S(2)}) collective-permute-start(bf16[32,512]{1,0:T(8,128)(2,1)S(1)} %add_convert_fusion.a), channel_id=1, source_target_pairs={{0,3},{1,2},{2,1},{3,0},{4,7},{5,6},{6,5},{7,4},{8,11},{9,10},{10,... | collective-permute-start | bytes 98312 | tf_op jit(solution)/shard_map/ppermute | solution.py:273
  35.8 3.3 %collective-permute-start.7 = (bf16[32,512]{1,0:T(8,128)(2,1)S(1)}, bf16[32,512]{1,0:T(8,128)(2,1)S(1)}, u32[]{:S(2)}, u32[]{:S(2)}) collective-permute-start(bf16[32,512]{1,0:T(8,128)(2,1)S(1)} %add_convert_fusion.a), channel_id=1, source_target_pairs={{0,5},{1,4},{2,7},{3,6},{4,1},{5,0},{6,3},{7,2},{8,13},{9,12},{10,... | collective-permute-start | bytes 98312 | tf_op jit(solution)/shard_map/ppermute | solution.py:273

commit v10 on v9

--- a/solution.py
+++ b/solution.py
@@ -341,8 +341,8 @@
         name="rows_part",
     )(table, swap(table, size, far | core), readers, known)
     part = (part.astype(F32) + swap(part, size, core).astype(F32)).astype(BF16)
-    part = (part.astype(F32) + swap(part, size, near | core).astype(F32)).astype(BF16)
-    rest = [swap(part, size, mask) for mask in (y | core, x | core, x ^ y)]
+    part = (part.astype(F32) + swap(part, size, x | core).astype(F32)).astype(BF16)
+    rest = [swap(part, size, mask) for mask in (near | core, y | core, y ^ near)]
     return pl.pallas_call(
         final_kernel,
         out_shape=(

time: 40.6 us -> 40.3 us (level)
  waiting for transfers between devices: 16.5 us -> 14.7 us
  starting transfers between devices: 18.1 us -> 19.5 us
    ppermute x10, waiting for transfers between devices: 16.5 us -> 14.7 us  [swap(): lax.ppermute(x, ('half', 'rest', 'rep'), [(i, i ^ mask) for i in range(si...]
    ppermute x10, starting transfers between devices: 11.8 us -> 13.2 us  [swap(): lax.ppermute(x, ('half', 'rest', 'rep'), [(i, i ^ mask) for i in range(si...]
  transfers between devices with their start and end apart: 11 -> 11, of which waited for: 7 -> 5; matrix products, arithmetic and copies ran while one was open for 0% -> 0% of each run, Pallas kernels for 0% -> 0%
where the time goes in v10:
time: 40.3 us; the launch traced here: 40 us
  starting transfers between devices  19.5 us (48%)
  waiting for transfers between devices  14.7 us (36%)
  Pallas kernels  5.11 us (13%)
  between operations  0.69 us (2%)
    ppermute x10, waiting for transfers between devices, swap(): lax.ppermute(x, ('half', 'rest', 'rep'), [(i, i ^ mask) for i in range(si...  14.7 us
    ppermute x10, starting transfers between devices, swap(): lax.ppermute(x, ('half', 'rest', 'rep'), [(i, i ^ mask) for i in range(si...  13.2 us
    all_to_all x1, starting transfers between devices, sliced(): got = lax.all_to_all(sends, ('rest', 'rep'), 0, 0, tiled=True)  6.3 us
    pallas_call x1, Pallas kernels, sliced(): pl.pallas_call(first_kernel, out_shape=(jax.ShapeDtypeStruct((sources, de...  2.71 us
    pallas_call x1, Pallas kernels, sliced(): pl.pallas_call(final_kernel, out_shape=(jax.ShapeDtypeStruct(u_one.shape,...  1.29 us
  transfers between devices with their start and end apart: 11, of which 5 were waited for; matrix products, arithmetic and copies ran while one was open for 0% of the time, Pallas kernels for 0%

profile of v10, /device:TPU:0, one launch (start us, length us, event | category | flops | bytes accessed | tf_op | source)
XLA Modules:
  0.0 40.0 jit_solution(17267865508165529639)
XLA Ops:
  0.6 2.7 %first.1 = (bf16[16,144,128]{2,1,0:T(8,128)(2,1)}, s32[8,128]{1,0:T(8,128)S(1)}, bf16[48,128]{1,0:T(8,128)(2,1)S(1)}) custom-call(s32[2]{0:T(128)} %one_hbm.1, s32[2]{0:T(128)} %two_hbm.1, s32[2]{0:T(128)} %three_hbm.1, s32[8]{0:T(128)} %owner_hbm.1, bf16[2,64,4096]{2,1,0:T(8,128)(2,1)} %tiles_hbm.1, bf16[32,1024]{1,0:T(8,128)(2,1)} %u_three_hbm.1, ...), custom_call_target="tpu_custom_call" | custom-call | tf_op jit(solution)/shard_map/first/pallas_call | solution.py:290
  3.4 6.3 %all-to-all-start = ((bf16[16,144,128]{2,1,0:T(8,128)(2,1)}), bf16[16,144,128]{2,1,0:T(8,128)(2,1)S(1)}, u32[]{:S(2)}, u32[]{:S(2)}) async-start(bf16[16,144,128]{2,1,0:T(8,128)(2,1)} %get-tuple-element.8), calls=%async_computation | async-start | bytes 1179648 | tf_op jit(solution)/shard_map/all_to_all | solution.py:310
  9.7 4.6 %collective-permute-start.3 = (bf16[48,128]{1,0:T(8,128)(2,1)S(1)}, bf16[48,128]{1,0:T(8,128)(2,1)S(1)}, u32[]{:S(2)}, u32[]{:S(2)}) collective-permute-start(bf16[48,128]{1,0:T(8,128)(2,1)S(1)} %get-tuple-element.9), channel_id=1, source_target_pairs={{0,29},{1,28},{2,31},{3,30},{4,25},{5,24},{6,27},{7,26},{8,21},{9,... | collective-permute-start | bytes 36872 | tf_op jit(solution)/shard_map/ppermute | solution.py:273
  14.3 0.3 collective-permute-start.2
  14.6 0.3 collective-permute-start.1
  14.9 2.1 %collective-permute-start = (bf16[48,128]{1,0:T(8,128)(2,1)S(1)}, bf16[48,128]{1,0:T(8,128)(2,1)S(1)}, u32[]{:S(2)}, u32[]{:S(2)}) collective-permute-start(bf16[48,128]{1,0:T(8,128)(2,1)S(1)} %get-tuple-element.9), channel_id=1, source_target_pairs={{0,17},{1,16},{2,19},{3,18},{4,21},{5,20},{6,23},{7,22},{8,25},{9,... | collective-permute-start | bytes 36872 | tf_op jit(solution)/shard_map/ppermute | solution.py:273
  17.0 4.8 %collective-permute-done.3.far3 = bf16[48,128]{1,0:T(8,128)(2,1)S(1)} collective-permute-done((bf16[48,128]{1,0:T(8,128)(2,1)S(1)}, bf16[48,128]{1,0:T(8,128)(2,1)S(1)}, u32[]{:S(2)}, u32[]{:S(2)}) %collective-permute-start.3) | collective-permute-done | bytes 12320 | tf_op jit(solution)/shard_map/ppermute | solution.py:273
  21.8 0.0 collective-permute-done.2.far2
  21.8 0.0 collective-permute-done.1.far1
  21.8 0.0 collective-permute-done.far0
  21.8 0.0 all-to-all-done.got
  21.8 0.7 %table.1 = (bf16[64,512]{1,0:T(8,128)(2,1)S(1)}, bf16[32,512]{1,0:T(8,128)(2,1)S(1)}) custom-call(bf16[16,144,128]{2,1,0:T(8,128)(2,1)S(1)} %all-to-all-done.got, bf16[48,128]{1,0:T(8,128)(2,1)S(1)} %collective-permute-done.far0, bf16[48,128]{1,0:T(8,128)(2,1)S(1)} %collective-permute-done.1.far1, bf16[48,128]{1,0:T(8,128)(2,1)S(1)} %collective-permute-done.2.far2, ...), custom_call_target="tpu_custom_call" | custom-call | tf_op jit(solution)/shard_map/table/pallas_call | solution.py:311
  22.6 0.7 %collective-permute-start.4 = (bf16[64,512]{1,0:T(8,128)(2,1)S(1)}, bf16[64,512]{1,0:T(8,128)(2,1)S(1)}, u32[]{:S(2)}, u32[]{:S(2)}) collective-permute-start(bf16[64,512]{1,0:T(8,128)(2,1)S(1)} %get-tuple-element.10.mine), channel_id=1, source_target_pairs={{0,17},{1,16},{2,19},{3,18},{4,21},{5,20},{6,23},{7,22},{8,25},{9,... | collective-permute-start | bytes 196616 | tf_op jit(solution)/shard_map/ppermute | solution.py:273
  23.3 0.1 known.1
  23.4 5.4 %collective-permute-done.4.theirs = bf16[64,512]{1,0:T(8,128)(2,1)S(1)} collective-permute-done((bf16[64,512]{1,0:T(8,128)(2,1)S(1)}, bf16[64,512]{1,0:T(8,128)(2,1)S(1)}, u32[]{:S(2)}, u32[]{:S(2)}) %collective-permute-start.4) | collective-permute-done | bytes 65568 | tf_op jit(solution)/shard_map/ppermute | solution.py:273
  28.8 0.2 rows_part.1
  29.0 0.4 %collective-permute-start.5 = (bf16[32,512]{1,0:T(8,128)(2,1)S(1)}, bf16[32,512]{1,0:T(8,128)(2,1)S(1)}, u32[]{:S(2)}, u32[]{:S(2)}) collective-permute-start(bf16[32,512]{1,0:T(8,128)(2,1)S(1)} %rows_part.1), channel_id=1, source_target_pairs={{0,1},{1,0},{2,3},{3,2},{4,5},{5,4},{6,7},{7,6},{8,9},{9,8},{10,11... | collective-permute-start | bytes 98312 | tf_op jit(solution)/shard_map/ppermute | solution.py:273
  29.4 0.9 %collective-permute-done.5 = bf16[32,512]{1,0:T(8,128)(2,1)S(1)} collective-permute-done((bf16[32,512]{1,0:T(8,128)(2,1)S(1)}, bf16[32,512]{1,0:T(8,128)(2,1)S(1)}, u32[]{:S(2)}, u32[]{:S(2)}) %collective-permute-start.5) | collective-permute-done | bytes 32800 | tf_op jit(solution)/shard_map/ppermute | solution.py:273
  30.3 1.5 %collective-permute-start.6 = (bf16[32,512]{1,0:T(8,128)(2,1)S(1)}, bf16[32,512]{1,0:T(8,128)(2,1)S(1)}, u32[]{:S(2)}, u32[]{:S(2)}) collective-permute-start(bf16[32,512]{1,0:T(8,128)(2,1)S(1)} %add_convert_fusion.1), channel_id=1, source_target_pairs={{0,3},{1,2},{2,1},{3,0},{4,7},{5,6},{6,5},{7,4},{8,11},{9,10},{10,... | collective-permute-start | bytes 98312 | tf_op jit(solution)/shard_map/ppermute | solution.py:273
  31.8 1.9 %collective-permute-done.6 = bf16[32,512]{1,0:T(8,128)(2,1)S(1)} collective-permute-done((bf16[32,512]{1,0:T(8,128)(2,1)S(1)}, bf16[32,512]{1,0:T(8,128)(2,1)S(1)}, u32[]{:S(2)}, u32[]{:S(2)}) %collective-permute-start.6) | collective-permute-done | bytes 32800 | tf_op jit(solution)/shard_map/ppermute | solution.py:273
  33.7 0.6 %collective-permute-start.9 = (bf16[32,512]{1,0:T(8,128)(2,1)S(1)}, bf16[32,512]{1,0:T(8,128)(2,1)S(1)}, u32[]{:S(2)}, u32[]{:S(2)}) collective-permute-start(bf16[32,512]{1,0:T(8,128)(2,1)S(1)} %add_convert_fusion.a), channel_id=1, source_target_pairs={{0,12},{1,13},{2,14},{3,15},{4,8},{5,9},{6,10},{7,11},{8,4},{9,5},... | collective-permute-start | bytes 98312 | tf_op jit(solution)/shard_map/ppermute | solution.py:273
  34.4 0.3 collective-permute-start.8
  34.7 2.3 %collective-permute-start.7 = (bf16[32,512]{1,0:T(8,128)(2,1)S(1)}, bf16[32,512]{1,0:T(8,128)(2,1)S(1)}, u32[]{:S(2)}, u32[]{:S(2)}) collective-permute-start(bf16[32,512]{1,0:T(8,128)(2,1)S(1)} %add_convert_fusion.a), channel_id=1, source_target_pairs={{0,9},{1,8},{2,11},{3,10},{4,13},{5,12},{6,15},{7,14},{8,1},{9,0},... | collective-permute-start | bytes 98312 | tf_op jit(solution)/shard_map/ppermute | solution.py:273
  37.0 1.7 %collective-permute-done.9.d = bf16[32,512]{1,0:T(8,128)(2,1)S(1)} collective-permute-done((bf16[32,512]{1,0:T(8,128)(2,1)S(1)}, bf16[32,512]{1,0:T(8,128)(2,1)S(1)}, u32[]{:S(2)}, u32[]{:S(2)}) %collective-permute-start.9) | collective-permute-done | bytes 32800 | tf_op jit(solution)/shard_map/ppermute | solution.py:273
  38.7 0.0 collective-permute-done.8.c
  38.7 0.0 collective-permute-done.7.b
  38.7 1.3 %final.1 = (f32[32,64]{1,0:T(8,128)}, bf16[2,2048]{1,0:T(2,128)(2,1)}) custom-call(s32[8,128]{1,0:T(8,128)S(1)} %get-tuple-element.7.places, bf16[32,512]{1,0:T(8,128)(2,1)S(1)} %add_convert_fusion.a, bf16[32,512]{1,0:T(8,128)(2,1)S(1)} %collective-permute-done.7.b, bf16[32,512]{1,0:T(8,128)(2,1)S(1)} %collective-permute-done.8.c, ...), custom_call_target="tpu_custom_call" | custom-call | tf_op jit(solution)/shard_map/final/pallas_call | solution.py:346
  (2 shorter events, 0.0 us)
Async XLA Ops:
  3.4 18.5 %all-to-all-start = ((bf16[16,144,128]{2,1,0:T(8,128)(2,1)}), bf16[16,144,128]{2,1,0:T(8,128)(2,1)S(1)}, u32[]{:S(2)}, u32[]{:S(2)}) async-start(bf16[16,144,128]{2,1,0:T(8,128)(2,1)} %get-tuple-element.8), calls=%async_computation | async-start | bytes 1179648 | tf_op jit(solution)/shard_map/all_to_all | solution.py:310
  9.7 12.2 %collective-permute-start.3 = (bf16[48,128]{1,0:T(8,128)(2,1)S(1)}, bf16[48,128]{1,0:T(8,128)(2,1)S(1)}, u32[]{:S(2)}, u32[]{:S(2)}) collective-permute-start(bf16[48,128]{1,0:T(8,128)(2,1)S(1)} %get-tuple-element.9), channel_id=1, source_target_pairs={{0,29},{1,28},{2,31},{3,30},{4,25},{5,24},{6,27},{7,26},{8,21},{9,... | collective-permute-start | bytes 36872 | tf_op jit(solution)/shard_map/ppermute | solution.py:273
  14.3 7.6 %collective-permute-start.2 = (bf16[48,128]{1,0:T(8,128)(2,1)S(1)}, bf16[48,128]{1,0:T(8,128)(2,1)S(1)}, u32[]{:S(2)}, u32[]{:S(2)}) collective-permute-start(bf16[48,128]{1,0:T(8,128)(2,1)S(1)} %get-tuple-element.9), channel_id=1, source_target_pairs={{0,25},{1,24},{2,27},{3,26},{4,29},{5,28},{6,31},{7,30},{8,17},{9,... | collective-permute-start | bytes 36872 | tf_op jit(solution)/shard_map/ppermute | solution.py:273
  14.6 7.3 %collective-permute-start.1 = (bf16[48,128]{1,0:T(8,128)(2,1)S(1)}, bf16[48,128]{1,0:T(8,128)(2,1)S(1)}, u32[]{:S(2)}, u32[]{:S(2)}) collective-permute-start(bf16[48,128]{1,0:T(8,128)(2,1)S(1)} %get-tuple-element.9), channel_id=1, source_target_pairs={{0,21},{1,20},{2,23},{3,22},{4,17},{5,16},{6,19},{7,18},{8,29},{9,... | collective-permute-start | bytes 36872 | tf_op jit(solution)/shard_map/ppermute | solution.py:273
  14.9 6.9 %collective-permute-start = (bf16[48,128]{1,0:T(8,128)(2,1)S(1)}, bf16[48,128]{1,0:T(8,128)(2,1)S(1)}, u32[]{:S(2)}, u32[]{:S(2)}) collective-permute-start(bf16[48,128]{1,0:T(8,128)(2,1)S(1)} %get-tuple-element.9), channel_id=1, source_target_pairs={{0,17},{1,16},{2,19},{3,18},{4,21},{5,20},{6,23},{7,22},{8,25},{9,... | collective-permute-start | bytes 36872 | tf_op jit(solution)/shard_map/ppermute | solution.py:273
  22.6 6.2 %collective-permute-start.4 = (bf16[64,512]{1,0:T(8,128)(2,1)S(1)}, bf16[64,512]{1,0:T(8,128)(2,1)S(1)}, u32[]{:S(2)}, u32[]{:S(2)}) collective-permute-start(bf16[64,512]{1,0:T(8,128)(2,1)S(1)} %get-tuple-element.10.mine), channel_id=1, source_target_pairs={{0,17},{1,16},{2,19},{3,18},{4,21},{5,20},{6,23},{7,22},{8,25},{9,... | collective-permute-start | bytes 196616 | tf_op jit(solution)/shard_map/ppermute | solution.py:273
  29.0 1.3 %collective-permute-start.5 = (bf16[32,512]{1,0:T(8,128)(2,1)S(1)}, bf16[32,512]{1,0:T(8,128)(2,1)S(1)}, u32[]{:S(2)}, u32[]{:S(2)}) collective-permute-start(bf16[32,512]{1,0:T(8,128)(2,1)S(1)} %rows_part.1), channel_id=1, source_target_pairs={{0,1},{1,0},{2,3},{3,2},{4,5},{5,4},{6,7},{7,6},{8,9},{9,8},{10,11... | collective-permute-start | bytes 98312 | tf_op jit(solution)/shard_map/ppermute | solution.py:273
  30.3 3.4 %collective-permute-start.6 = (bf16[32,512]{1,0:T(8,128)(2,1)S(1)}, bf16[32,512]{1,0:T(8,128)(2,1)S(1)}, u32[]{:S(2)}, u32[]{:S(2)}) collective-permute-start(bf16[32,512]{1,0:T(8,128)(2,1)S(1)} %add_convert_fusion.1), channel_id=1, source_target_pairs={{0,3},{1,2},{2,1},{3,0},{4,7},{5,6},{6,5},{7,4},{8,11},{9,10},{10,... | collective-permute-start | bytes 98312 | tf_op jit(solution)/shard_map/ppermute | solution.py:273
  33.7 5.0 %collective-permute-start.9 = (bf16[32,512]{1,0:T(8,128)(2,1)S(1)}, bf16[32,512]{1,0:T(8,128)(2,1)S(1)}, u32[]{:S(2)}, u32[]{:S(2)}) collective-permute-start(bf16[32,512]{1,0:T(8,128)(2,1)S(1)} %add_convert_fusion.a), channel_id=1, source_target_pairs={{0,12},{1,13},{2,14},{3,15},{4,8},{5,9},{6,10},{7,11},{8,4},{9,5},... | collective-permute-start | bytes 98312 | tf_op jit(solution)/shard_map/ppermute | solution.py:273
  34.4 4.4 %collective-permute-start.8 = (bf16[32,512]{1,0:T(8,128)(2,1)S(1)}, bf16[32,512]{1,0:T(8,128)(2,1)S(1)}, u32[]{:S(2)}, u32[]{:S(2)}) collective-permute-start(bf16[32,512]{1,0:T(8,128)(2,1)S(1)} %add_convert_fusion.a), channel_id=1, source_target_pairs={{0,5},{1,4},{2,7},{3,6},{4,1},{5,0},{6,3},{7,2},{8,13},{9,12},{10,... | collective-permute-start | bytes 98312 | tf_op jit(solution)/shard_map/ppermute | solution.py:273
  34.7 4.0 %collective-permute-start.7 = (bf16[32,512]{1,0:T(8,128)(2,1)S(1)}, bf16[32,512]{1,0:T(8,128)(2,1)S(1)}, u32[]{:S(2)}, u32[]{:S(2)}) collective-permute-start(bf16[32,512]{1,0:T(8,128)(2,1)S(1)} %add_convert_fusion.a), channel_id=1, source_target_pairs={{0,9},{1,8},{2,11},{3,10},{4,13},{5,12},{6,15},{7,14},{8,1},{9,0},... | collective-permute-start | bytes 98312 | tf_op jit(solution)/shard_map/ppermute | solution.py:273

commit v11 on v10

--- a/solution.py
+++ b/solution.py
@@ -91,8 +91,8 @@
 
 
 def first_kernel(
-    one_hbm, two_hbm, three_hbm, owner_hbm, tiles_hbm, u_three_hbm, u_two_hbm, u_one_hbm, out, places, pack,
-    one, two, three, owner, tiles, u_three, u_two, u_one, two_f32, in_sems, tile_sems,
+    one_hbm, two_hbm, three_hbm, owner_hbm, tiles_hbm, u_three_hbm, u_two_hbm, u_one_hbm, out_hbm, places, pack,
+    one, two, three, owner, tiles, u_three, u_two, u_one, two_f32, out, in_sems, tile_sems, out_sems,
 ):
     side = lax.axis_index("half")
     count, width = tiles.shape[:2]
@@ -145,6 +145,16 @@
     rows = slice(2 * width, 2 * width + META)
     for k in range(out.shape[0]):
         out[k, rows, :] = meta
+    stores = []
+
+    def send(rows):
+        copy = pltpu.make_async_copy(
+            out.at[:, rows, :], out_hbm.at[:, rows, :], out_sems.at[len(stores)]
+        )
+        copy.start()
+        stores.append(copy)
+
+    send(rows)
     for copy in loads:
         copy.wait()
     for n in range(pieces // 2):
@@ -159,9 +169,12 @@
                 for g in (2 * h, 2 * h + 1):
                     lanes = slice(g * width, (g + 1) * width)
                     block.append(jnp.concatenate([part[at, lanes] for part in wide], axis=1))
-                start = (s % 2) * width + (2 * n + h) * META
+                start = n * width + (s % 2) * (width // 2) + h * META
                 rows = slice(start, start + META)
                 out[(s // 2) ^ side, rows, :] = jnp.concatenate(block, axis=0).astype(BF16)
+        send(slice(n * width, (n + 1) * width))
+    for copy in stores:
+        copy.wait()
 
 
 def table_kernel(reps, got, far0, far1, far2, far3, out, readers, two, one, total):
@@ -205,8 +218,8 @@
     for src in range(sources):
         moving = []
         for s in range(2):
-            block = got[src, s * width : (s + 1) * width, :]
-            moving.append(jnp.concatenate([block, block], axis=0))
+            lines = [got[src, at : at + width // 2, :] for at in (s * width // 2, (s + 2) * width // 2)]
+            moving.append(jnp.concatenate(lines + lines, axis=0))
         moving = jnp.concatenate(moving, axis=1)
         left = code[src, 0]
         digits = []
@@ -295,18 +308,20 @@
             jax.ShapeDtypeStruct((rank + rank // 2, LANES), BF16),
         ),
         in_specs=[pl.BlockSpec(memory_space=pltpu.HBM)] * 8,
-        out_specs=(vmem, vmem, vmem),
+        out_specs=(pl.BlockSpec(memory_space=pltpu.HBM), vmem, vmem),
         scratch_shapes=[pltpu.SMEM(a.shape, a.dtype) for a in ints]
         + [pltpu.VMEM(a.shape, a.dtype) for a in arrays]
         + [
             pltpu.VMEM(u_two.shape, F32),
+            pltpu.VMEM((sources, depth, LANES), BF16),
             pltpu.SemaphoreType.DMA((7,)),
             pltpu.SemaphoreType.DMA((count,)),
+            pltpu.SemaphoreType.DMA((3,)),
         ],
         compiler_params=narrow,
         name="first",
     )(*[pltpu.with_memory_space_constraint(a, pltpu.HBM) for a in ints + arrays])
-    theirs = [swap(pack, size, far | core | k * y) for k in range(4)]
+    theirs = [swap(pack, size, far | core | k * y) for k in (3, 2, 1, 0)][::-1]
     got = lax.all_to_all(sends, ("rest", "rep"), 0, 0, tiled=True)
     table, readers = pl.pallas_call(
         functools.partial(table_kernel, reps),

time: 40.3 us -> 40.2 us (level)
  no operation moved by 1% of the time
where the time goes in v11:
time: 40.2 us; the launch traced here: 40 us
  starting transfers between devices  19.5 us (49%)
  waiting for transfers between devices  14.7 us (37%)
  Pallas kernels  5.05 us (13%)
  between operations  0.69 us (2%)
    ppermute x10, waiting for transfers between devices, swap(): lax.ppermute(x, ('half', 'rest', 'rep'), [(i, i ^ mask) for i in range(si...  14.7 us
    ppermute x10, starting transfers between devices, swap(): lax.ppermute(x, ('half', 'rest', 'rep'), [(i, i ^ mask) for i in range(si...  13.2 us
    all_to_all x1, starting transfers between devices, sliced(): got = lax.all_to_all(sends, ('rest', 'rep'), 0, 0, tiled=True)  6.3 us
    pallas_call x1, Pallas kernels, sliced(): pl.pallas_call(first_kernel, out_shape=(jax.ShapeDtypeStruct((sources, de...  2.63 us
    pallas_call x1, Pallas kernels, sliced(): pl.pallas_call(final_kernel, out_shape=(jax.ShapeDtypeStruct(u_one.shape,...  1.29 us
  transfers between devices with their start and end apart: 11, of which 5 were waited for; matrix products, arithmetic and copies ran while one was open for 0% of the time, Pallas kernels for 0%

profile of v11, /device:TPU:0, one launch (start us, length us, event | category | flops | bytes accessed | tf_op | source)
XLA Modules:
  0.0 40.0 jit_solution(13471916613441399352)
XLA Ops:
  0.6 2.6 %first.1 = (bf16[16,144,128]{2,1,0:T(8,128)(2,1)}, s32[8,128]{1,0:T(8,128)S(1)}, bf16[48,128]{1,0:T(8,128)(2,1)S(1)}) custom-call(s32[2]{0:T(128)} %one_hbm.1, s32[2]{0:T(128)} %two_hbm.1, s32[2]{0:T(128)} %three_hbm.1, s32[8]{0:T(128)} %owner_hbm.1, bf16[2,64,4096]{2,1,0:T(8,128)(2,1)} %tiles_hbm.1, bf16[32,1024]{1,0:T(8,128)(2,1)} %u_three_hbm.1, ...), custom_call_target="tpu_custom_call" | custom-call | tf_op jit(solution)/shard_map/first/pallas_call | solution.py:303
  3.3 6.3 %all-to-all-start = ((bf16[16,144,128]{2,1,0:T(8,128)(2,1)}), bf16[16,144,128]{2,1,0:T(8,128)(2,1)S(1)}, u32[]{:S(2)}, u32[]{:S(2)}) async-start(bf16[16,144,128]{2,1,0:T(8,128)(2,1)} %get-tuple-element.8), calls=%async_computation | async-start | bytes 1179648 | tf_op jit(solution)/shard_map/all_to_all | solution.py:325
  9.6 4.6 %collective-permute-start.3 = (bf16[48,128]{1,0:T(8,128)(2,1)S(1)}, bf16[48,128]{1,0:T(8,128)(2,1)S(1)}, u32[]{:S(2)}, u32[]{:S(2)}) collective-permute-start(bf16[48,128]{1,0:T(8,128)(2,1)S(1)} %get-tuple-element.9), channel_id=1, source_target_pairs={{0,29},{1,28},{2,31},{3,30},{4,25},{5,24},{6,27},{7,26},{8,21},{9,... | collective-permute-start | bytes 36872 | tf_op jit(solution)/shard_map/ppermute | solution.py:286
  14.2 0.3 collective-permute-start.2
  14.5 0.3 collective-permute-start.1
  14.8 2.1 %collective-permute-start = (bf16[48,128]{1,0:T(8,128)(2,1)S(1)}, bf16[48,128]{1,0:T(8,128)(2,1)S(1)}, u32[]{:S(2)}, u32[]{:S(2)}) collective-permute-start(bf16[48,128]{1,0:T(8,128)(2,1)S(1)} %get-tuple-element.9), channel_id=1, source_target_pairs={{0,17},{1,16},{2,19},{3,18},{4,21},{5,20},{6,23},{7,22},{8,25},{9,... | collective-permute-start | bytes 36872 | tf_op jit(solution)/shard_map/ppermute | solution.py:286
  16.9 4.8 %collective-permute-done.3.far3 = bf16[48,128]{1,0:T(8,128)(2,1)S(1)} collective-permute-done((bf16[48,128]{1,0:T(8,128)(2,1)S(1)}, bf16[48,128]{1,0:T(8,128)(2,1)S(1)}, u32[]{:S(2)}, u32[]{:S(2)}) %collective-permute-start.3) | collective-permute-done | bytes 12320 | tf_op jit(solution)/shard_map/ppermute | solution.py:286
  21.7 0.0 collective-permute-done.2.far2
  21.7 0.0 collective-permute-done.1.far1
  21.7 0.0 collective-permute-done.far0
  21.8 0.0 all-to-all-done.got
  21.8 0.8 %table.1 = (bf16[64,512]{1,0:T(8,128)(2,1)S(1)}, bf16[32,512]{1,0:T(8,128)(2,1)S(1)}) custom-call(bf16[16,144,128]{2,1,0:T(8,128)(2,1)S(1)} %all-to-all-done.got, bf16[48,128]{1,0:T(8,128)(2,1)S(1)} %collective-permute-done.far0, bf16[48,128]{1,0:T(8,128)(2,1)S(1)} %collective-permute-done.1.far1, bf16[48,128]{1,0:T(8,128)(2,1)S(1)} %collective-permute-done.2.far2, ...), custom_call_target="tpu_custom_call" | custom-call | tf_op jit(solution)/shard_map/table/pallas_call | solution.py:326
  22.5 0.7 %collective-permute-start.4 = (bf16[64,512]{1,0:T(8,128)(2,1)S(1)}, bf16[64,512]{1,0:T(8,128)(2,1)S(1)}, u32[]{:S(2)}, u32[]{:S(2)}) collective-permute-start(bf16[64,512]{1,0:T(8,128)(2,1)S(1)} %get-tuple-element.10.mine), channel_id=1, source_target_pairs={{0,17},{1,16},{2,19},{3,18},{4,21},{5,20},{6,23},{7,22},{8,25},{9,... | collective-permute-start | bytes 196616 | tf_op jit(solution)/shard_map/ppermute | solution.py:286
  23.2 0.1 known.1
  23.3 5.4 %collective-permute-done.4.theirs = bf16[64,512]{1,0:T(8,128)(2,1)S(1)} collective-permute-done((bf16[64,512]{1,0:T(8,128)(2,1)S(1)}, bf16[64,512]{1,0:T(8,128)(2,1)S(1)}, u32[]{:S(2)}, u32[]{:S(2)}) %collective-permute-start.4) | collective-permute-done | bytes 65568 | tf_op jit(solution)/shard_map/ppermute | solution.py:286
  28.7 0.2 rows_part.1
  29.0 0.4 %collective-permute-start.5 = (bf16[32,512]{1,0:T(8,128)(2,1)S(1)}, bf16[32,512]{1,0:T(8,128)(2,1)S(1)}, u32[]{:S(2)}, u32[]{:S(2)}) collective-permute-start(bf16[32,512]{1,0:T(8,128)(2,1)S(1)} %rows_part.1), channel_id=1, source_target_pairs={{0,1},{1,0},{2,3},{3,2},{4,5},{5,4},{6,7},{7,6},{8,9},{9,8},{10,11... | collective-permute-start | bytes 98312 | tf_op jit(solution)/shard_map/ppermute | solution.py:286
  29.4 0.9 %collective-permute-done.5 = bf16[32,512]{1,0:T(8,128)(2,1)S(1)} collective-permute-done((bf16[32,512]{1,0:T(8,128)(2,1)S(1)}, bf16[32,512]{1,0:T(8,128)(2,1)S(1)}, u32[]{:S(2)}, u32[]{:S(2)}) %collective-permute-start.5) | collective-permute-done | bytes 32800 | tf_op jit(solution)/shard_map/ppermute | solution.py:286
  30.3 1.5 %collective-permute-start.6 = (bf16[32,512]{1,0:T(8,128)(2,1)S(1)}, bf16[32,512]{1,0:T(8,128)(2,1)S(1)}, u32[]{:S(2)}, u32[]{:S(2)}) collective-permute-start(bf16[32,512]{1,0:T(8,128)(2,1)S(1)} %add_convert_fusion.1), channel_id=1, source_target_pairs={{0,3},{1,2},{2,1},{3,0},{4,7},{5,6},{6,5},{7,4},{8,11},{9,10},{10,... | collective-permute-start | bytes 98312 | tf_op jit(solution)/shard_map/ppermute | solution.py:286
  31.7 1.9 %collective-permute-done.6 = bf16[32,512]{1,0:T(8,128)(2,1)S(1)} collective-permute-done((bf16[32,512]{1,0:T(8,128)(2,1)S(1)}, bf16[32,512]{1,0:T(8,128)(2,1)S(1)}, u32[]{:S(2)}, u32[]{:S(2)}) %collective-permute-start.6) | collective-permute-done | bytes 32800 | tf_op jit(solution)/shard_map/ppermute | solution.py:286
  33.7 0.6 %collective-permute-start.9 = (bf16[32,512]{1,0:T(8,128)(2,1)S(1)}, bf16[32,512]{1,0:T(8,128)(2,1)S(1)}, u32[]{:S(2)}, u32[]{:S(2)}) collective-permute-start(bf16[32,512]{1,0:T(8,128)(2,1)S(1)} %add_convert_fusion.a), channel_id=1, source_target_pairs={{0,12},{1,13},{2,14},{3,15},{4,8},{5,9},{6,10},{7,11},{8,4},{9,5},... | collective-permute-start | bytes 98312 | tf_op jit(solution)/shard_map/ppermute | solution.py:286
  34.3 0.3 collective-permute-start.8
  34.6 2.3 %collective-permute-start.7 = (bf16[32,512]{1,0:T(8,128)(2,1)S(1)}, bf16[32,512]{1,0:T(8,128)(2,1)S(1)}, u32[]{:S(2)}, u32[]{:S(2)}) collective-permute-start(bf16[32,512]{1,0:T(8,128)(2,1)S(1)} %add_convert_fusion.a), channel_id=1, source_target_pairs={{0,9},{1,8},{2,11},{3,10},{4,13},{5,12},{6,15},{7,14},{8,1},{9,0},... | collective-permute-start | bytes 98312 | tf_op jit(solution)/shard_map/ppermute | solution.py:286
  36.9 1.7 %collective-permute-done.9.d = bf16[32,512]{1,0:T(8,128)(2,1)S(1)} collective-permute-done((bf16[32,512]{1,0:T(8,128)(2,1)S(1)}, bf16[32,512]{1,0:T(8,128)(2,1)S(1)}, u32[]{:S(2)}, u32[]{:S(2)}) %collective-permute-start.9) | collective-permute-done | bytes 32800 | tf_op jit(solution)/shard_map/ppermute | solution.py:286
  38.7 0.0 collective-permute-done.8.c
  38.7 0.0 collective-permute-done.7.b
  38.7 1.3 %final.1 = (f32[32,64]{1,0:T(8,128)}, bf16[2,2048]{1,0:T(2,128)(2,1)}) custom-call(s32[8,128]{1,0:T(8,128)S(1)} %get-tuple-element.7.places, bf16[32,512]{1,0:T(8,128)(2,1)S(1)} %add_convert_fusion.a, bf16[32,512]{1,0:T(8,128)(2,1)S(1)} %collective-permute-done.7.b, bf16[32,512]{1,0:T(8,128)(2,1)S(1)} %collective-permute-done.8.c, ...), custom_call_target="tpu_custom_call" | custom-call | tf_op jit(solution)/shard_map/final/pallas_call | solution.py:361
  (2 shorter events, 0.0 us)
Async XLA Ops:
  3.3 18.5 %all-to-all-start = ((bf16[16,144,128]{2,1,0:T(8,128)(2,1)}), bf16[16,144,128]{2,1,0:T(8,128)(2,1)S(1)}, u32[]{:S(2)}, u32[]{:S(2)}) async-start(bf16[16,144,128]{2,1,0:T(8,128)(2,1)} %get-tuple-element.8), calls=%async_computation | async-start | bytes 1179648 | tf_op jit(solution)/shard_map/all_to_all | solution.py:325
  9.6 12.2 %collective-permute-start.3 = (bf16[48,128]{1,0:T(8,128)(2,1)S(1)}, bf16[48,128]{1,0:T(8,128)(2,1)S(1)}, u32[]{:S(2)}, u32[]{:S(2)}) collective-permute-start(bf16[48,128]{1,0:T(8,128)(2,1)S(1)} %get-tuple-element.9), channel_id=1, source_target_pairs={{0,29},{1,28},{2,31},{3,30},{4,25},{5,24},{6,27},{7,26},{8,21},{9,... | collective-permute-start | bytes 36872 | tf_op jit(solution)/shard_map/ppermute | solution.py:286
  14.2 7.6 %collective-permute-start.2 = (bf16[48,128]{1,0:T(8,128)(2,1)S(1)}, bf16[48,128]{1,0:T(8,128)(2,1)S(1)}, u32[]{:S(2)}, u32[]{:S(2)}) collective-permute-start(bf16[48,128]{1,0:T(8,128)(2,1)S(1)} %get-tuple-element.9), channel_id=1, source_target_pairs={{0,25},{1,24},{2,27},{3,26},{4,29},{5,28},{6,31},{7,30},{8,17},{9,... | collective-permute-start | bytes 36872 | tf_op jit(solution)/shard_map/ppermute | solution.py:286
  14.5 7.3 %collective-permute-start.1 = (bf16[48,128]{1,0:T(8,128)(2,1)S(1)}, bf16[48,128]{1,0:T(8,128)(2,1)S(1)}, u32[]{:S(2)}, u32[]{:S(2)}) collective-permute-start(bf16[48,128]{1,0:T(8,128)(2,1)S(1)} %get-tuple-element.9), channel_id=1, source_target_pairs={{0,21},{1,20},{2,23},{3,22},{4,17},{5,16},{6,19},{7,18},{8,29},{9,... | collective-permute-start | bytes 36872 | tf_op jit(solution)/shard_map/ppermute | solution.py:286
  14.8 6.9 %collective-permute-start = (bf16[48,128]{1,0:T(8,128)(2,1)S(1)}, bf16[48,128]{1,0:T(8,128)(2,1)S(1)}, u32[]{:S(2)}, u32[]{:S(2)}) collective-permute-start(bf16[48,128]{1,0:T(8,128)(2,1)S(1)} %get-tuple-element.9), channel_id=1, source_target_pairs={{0,17},{1,16},{2,19},{3,18},{4,21},{5,20},{6,23},{7,22},{8,25},{9,... | collective-permute-start | bytes 36872 | tf_op jit(solution)/shard_map/ppermute | solution.py:286
  22.5 6.2 %collective-permute-start.4 = (bf16[64,512]{1,0:T(8,128)(2,1)S(1)}, bf16[64,512]{1,0:T(8,128)(2,1)S(1)}, u32[]{:S(2)}, u32[]{:S(2)}) collective-permute-start(bf16[64,512]{1,0:T(8,128)(2,1)S(1)} %get-tuple-element.10.mine), channel_id=1, source_target_pairs={{0,17},{1,16},{2,19},{3,18},{4,21},{5,20},{6,23},{7,22},{8,25},{9,... | collective-permute-start | bytes 196616 | tf_op jit(solution)/shard_map/ppermute | solution.py:286
  29.0 1.3 %collective-permute-start.5 = (bf16[32,512]{1,0:T(8,128)(2,1)S(1)}, bf16[32,512]{1,0:T(8,128)(2,1)S(1)}, u32[]{:S(2)}, u32[]{:S(2)}) collective-permute-start(bf16[32,512]{1,0:T(8,128)(2,1)S(1)} %rows_part.1), channel_id=1, source_target_pairs={{0,1},{1,0},{2,3},{3,2},{4,5},{5,4},{6,7},{7,6},{8,9},{9,8},{10,11... | collective-permute-start | bytes 98312 | tf_op jit(solution)/shard_map/ppermute | solution.py:286
  30.3 3.4 %collective-permute-start.6 = (bf16[32,512]{1,0:T(8,128)(2,1)S(1)}, bf16[32,512]{1,0:T(8,128)(2,1)S(1)}, u32[]{:S(2)}, u32[]{:S(2)}) collective-permute-start(bf16[32,512]{1,0:T(8,128)(2,1)S(1)} %add_convert_fusion.1), channel_id=1, source_target_pairs={{0,3},{1,2},{2,1},{3,0},{4,7},{5,6},{6,5},{7,4},{8,11},{9,10},{10,... | collective-permute-start | bytes 98312 | tf_op jit(solution)/shard_map/ppermute | solution.py:286
  33.7 5.0 %collective-permute-start.9 = (bf16[32,512]{1,0:T(8,128)(2,1)S(1)}, bf16[32,512]{1,0:T(8,128)(2,1)S(1)}, u32[]{:S(2)}, u32[]{:S(2)}) collective-permute-start(bf16[32,512]{1,0:T(8,128)(2,1)S(1)} %add_convert_fusion.a), channel_id=1, source_target_pairs={{0,12},{1,13},{2,14},{3,15},{4,8},{5,9},{6,10},{7,11},{8,4},{9,5},... | collective-permute-start | bytes 98312 | tf_op jit(solution)/shard_map/ppermute | solution.py:286
  34.3 4.4 %collective-permute-start.8 = (bf16[32,512]{1,0:T(8,128)(2,1)S(1)}, bf16[32,512]{1,0:T(8,128)(2,1)S(1)}, u32[]{:S(2)}, u32[]{:S(2)}) collective-permute-start(bf16[32,512]{1,0:T(8,128)(2,1)S(1)} %add_convert_fusion.a), channel_id=1, source_target_pairs={{0,5},{1,4},{2,7},{3,6},{4,1},{5,0},{6,3},{7,2},{8,13},{9,12},{10,... | collective-permute-start | bytes 98312 | tf_op jit(solution)/shard_map/ppermute | solution.py:286
  34.6 4.0 %collective-permute-start.7 = (bf16[32,512]{1,0:T(8,128)(2,1)S(1)}, bf16[32,512]{1,0:T(8,128)(2,1)S(1)}, u32[]{:S(2)}, u32[]{:S(2)}) collective-permute-start(bf16[32,512]{1,0:T(8,128)(2,1)S(1)} %add_convert_fusion.a), channel_id=1, source_target_pairs={{0,9},{1,8},{2,11},{3,10},{4,13},{5,12},{6,15},{7,14},{8,1},{9,0},... | collective-permute-start | bytes 98312 | tf_op jit(solution)/shard_map/ppermute | solution.py:286

commit v12 on v11

--- a/solution.py
+++ b/solution.py
@@ -227,15 +227,15 @@
             digits.append(left % blocks)
             left = left // blocks
         stacked = jnp.concatenate([two[b] for b in digits[:count]], axis=0)
-        product = jnp.dot(stacked, moving, preferred_element_type=F32).astype(BF16).astype(F32)
+        product = jnp.dot(stacked, moving, preferred_element_type=F32)
         for t, p in enumerate(digits[count:]):
-            total[t, src % 2, p] += product[t * rank : (t + 1) * rank]
+            total[t, p] += product[t * rank : (t + 1) * rank]
     for s in range(2):
         sums = []
         lanes = slice(s * LANES, (s + 1) * LANES)
         for p in range(owners):
-            low = (total[0, 0, p, :, lanes] + total[0, 1, p, :, lanes])[:, :half]
-            high = total[1, 0, p, :, lanes] + total[1, 1, p, :, lanes]
+            low = total[0, p, :, lanes][:, :half]
+            high = total[1, p, :, lanes]
             sums.append(low + pltpu.roll(high, half, 1)[:, :half])
         out[s * rank : (s + 1) * rank, :] = jnp.concatenate(sums, axis=1).astype(BF16)
     readers[...] = jnp.concatenate([one[p][:, :half] for p in range(owners)], axis=1).astype(BF16)
@@ -334,7 +334,7 @@
         scratch_shapes=[
             pltpu.VMEM((2 * owners, rank, LANES), BF16),
             pltpu.VMEM((owners, rank, LANES), F32),
-            pltpu.VMEM((count, 2, owners, rank, 2 * LANES), F32),
+            pltpu.VMEM((count, owners, rank, 2 * LANES), F32),
         ],
         compiler_params=narrow,
         name="table",

time: 40.2 us -> 40.2 us (level)
  no operation moved by 1% of the time
where the time goes in v12:
time: 40.2 us; the launch traced here: 39.9 us
  starting transfers between devices  19.5 us (49%)
  waiting for transfers between devices  14.7 us (37%)
  Pallas kernels  5.04 us (13%)
  between operations  0.68 us (2%)
    ppermute x10, waiting for transfers between devices, swap(): lax.ppermute(x, ('half', 'rest', 'rep'), [(i, i ^ mask) for i in range(si...  14.7 us
    ppermute x10, starting transfers between devices, swap(): lax.ppermute(x, ('half', 'rest', 'rep'), [(i, i ^ mask) for i in range(si...  13.2 us
    all_to_all x1, starting transfers between devices, sliced(): got = lax.all_to_all(sends, ('rest', 'rep'), 0, 0, tiled=True)  6.3 us
    pallas_call x1, Pallas kernels, sliced(): pl.pallas_call(first_kernel, out_shape=(jax.ShapeDtypeStruct((sources, de...  2.63 us
    pallas_call x1, Pallas kernels, sliced(): pl.pallas_call(final_kernel, out_shape=(jax.ShapeDtypeStruct(u_one.shape,...  1.29 us
  transfers between devices with their start and end apart: 11, of which 5 were waited for; matrix products, arithmetic and copies ran while one was open for 0% of the time, Pallas kernels for 0%

profile of v12, /device:TPU:0, one launch (start us, length us, event | category | flops | bytes accessed | tf_op | source)
XLA Modules:
  0.0 39.9 jit_solution(5456398597095777816)
XLA Ops:
  0.6 2.6 %first.1 = (bf16[16,144,128]{2,1,0:T(8,128)(2,1)}, s32[8,128]{1,0:T(8,128)S(1)}, bf16[48,128]{1,0:T(8,128)(2,1)S(1)}) custom-call(s32[2]{0:T(128)} %one_hbm.1, s32[2]{0:T(128)} %two_hbm.1, s32[2]{0:T(128)} %three_hbm.1, s32[8]{0:T(128)} %owner_hbm.1, bf16[2,64,4096]{2,1,0:T(8,128)(2,1)} %tiles_hbm.1, bf16[32,1024]{1,0:T(8,128)(2,1)} %u_three_hbm.1, ...), custom_call_target="tpu_custom_call" | custom-call | tf_op jit(solution)/shard_map/first/pallas_call | solution.py:303
  3.3 6.3 %all-to-all-start = ((bf16[16,144,128]{2,1,0:T(8,128)(2,1)}), bf16[16,144,128]{2,1,0:T(8,128)(2,1)S(1)}, u32[]{:S(2)}, u32[]{:S(2)}) async-start(bf16[16,144,128]{2,1,0:T(8,128)(2,1)} %get-tuple-element.8), calls=%async_computation | async-start | bytes 1179648 | tf_op jit(solution)/shard_map/all_to_all | solution.py:325
  9.6 4.6 %collective-permute-start.3 = (bf16[48,128]{1,0:T(8,128)(2,1)S(1)}, bf16[48,128]{1,0:T(8,128)(2,1)S(1)}, u32[]{:S(2)}, u32[]{:S(2)}) collective-permute-start(bf16[48,128]{1,0:T(8,128)(2,1)S(1)} %get-tuple-element.9), channel_id=1, source_target_pairs={{0,29},{1,28},{2,31},{3,30},{4,25},{5,24},{6,27},{7,26},{8,21},{9,... | collective-permute-start | bytes 36872 | tf_op jit(solution)/shard_map/ppermute | solution.py:286
  14.2 0.3 collective-permute-start.2
  14.5 0.3 collective-permute-start.1
  14.8 2.1 %collective-permute-start = (bf16[48,128]{1,0:T(8,128)(2,1)S(1)}, bf16[48,128]{1,0:T(8,128)(2,1)S(1)}, u32[]{:S(2)}, u32[]{:S(2)}) collective-permute-start(bf16[48,128]{1,0:T(8,128)(2,1)S(1)} %get-tuple-element.9), channel_id=1, source_target_pairs={{0,17},{1,16},{2,19},{3,18},{4,21},{5,20},{6,23},{7,22},{8,25},{9,... | collective-permute-start | bytes 36872 | tf_op jit(solution)/shard_map/ppermute | solution.py:286
  16.9 4.8 %collective-permute-done.3.far3 = bf16[48,128]{1,0:T(8,128)(2,1)S(1)} collective-permute-done((bf16[48,128]{1,0:T(8,128)(2,1)S(1)}, bf16[48,128]{1,0:T(8,128)(2,1)S(1)}, u32[]{:S(2)}, u32[]{:S(2)}) %collective-permute-start.3) | collective-permute-done | bytes 12320 | tf_op jit(solution)/shard_map/ppermute | solution.py:286
  21.7 0.0 collective-permute-done.2.far2
  21.7 0.0 collective-permute-done.1.far1
  21.7 0.0 collective-permute-done.far0
  21.8 0.0 all-to-all-done.got
  21.8 0.7 %table.1 = (bf16[64,512]{1,0:T(8,128)(2,1)S(1)}, bf16[32,512]{1,0:T(8,128)(2,1)S(1)}) custom-call(bf16[16,144,128]{2,1,0:T(8,128)(2,1)S(1)} %all-to-all-done.got, bf16[48,128]{1,0:T(8,128)(2,1)S(1)} %collective-permute-done.far0, bf16[48,128]{1,0:T(8,128)(2,1)S(1)} %collective-permute-done.1.far1, bf16[48,128]{1,0:T(8,128)(2,1)S(1)} %collective-permute-done.2.far2, ...), custom_call_target="tpu_custom_call" | custom-call | tf_op jit(solution)/shard_map/table/pallas_call | solution.py:326
  22.5 0.7 %collective-permute-start.4 = (bf16[64,512]{1,0:T(8,128)(2,1)S(1)}, bf16[64,512]{1,0:T(8,128)(2,1)S(1)}, u32[]{:S(2)}, u32[]{:S(2)}) collective-permute-start(bf16[64,512]{1,0:T(8,128)(2,1)S(1)} %get-tuple-element.10.mine), channel_id=1, source_target_pairs={{0,17},{1,16},{2,19},{3,18},{4,21},{5,20},{6,23},{7,22},{8,25},{9,... | collective-permute-start | bytes 196616 | tf_op jit(solution)/shard_map/ppermute | solution.py:286
  23.2 0.1 known.1
  23.3 5.4 %collective-permute-done.4.theirs = bf16[64,512]{1,0:T(8,128)(2,1)S(1)} collective-permute-done((bf16[64,512]{1,0:T(8,128)(2,1)S(1)}, bf16[64,512]{1,0:T(8,128)(2,1)S(1)}, u32[]{:S(2)}, u32[]{:S(2)}) %collective-permute-start.4) | collective-permute-done | bytes 65568 | tf_op jit(solution)/shard_map/ppermute | solution.py:286
  28.7 0.2 rows_part.1
  29.0 0.4 %collective-permute-start.5 = (bf16[32,512]{1,0:T(8,128)(2,1)S(1)}, bf16[32,512]{1,0:T(8,128)(2,1)S(1)}, u32[]{:S(2)}, u32[]{:S(2)}) collective-permute-start(bf16[32,512]{1,0:T(8,128)(2,1)S(1)} %rows_part.1), channel_id=1, source_target_pairs={{0,1},{1,0},{2,3},{3,2},{4,5},{5,4},{6,7},{7,6},{8,9},{9,8},{10,11... | collective-permute-start | bytes 98312 | tf_op jit(solution)/shard_map/ppermute | solution.py:286
  29.4 0.9 %collective-permute-done.5 = bf16[32,512]{1,0:T(8,128)(2,1)S(1)} collective-permute-done((bf16[32,512]{1,0:T(8,128)(2,1)S(1)}, bf16[32,512]{1,0:T(8,128)(2,1)S(1)}, u32[]{:S(2)}, u32[]{:S(2)}) %collective-permute-start.5) | collective-permute-done | bytes 32800 | tf_op jit(solution)/shard_map/ppermute | solution.py:286
  30.2 1.5 %collective-permute-start.6 = (bf16[32,512]{1,0:T(8,128)(2,1)S(1)}, bf16[32,512]{1,0:T(8,128)(2,1)S(1)}, u32[]{:S(2)}, u32[]{:S(2)}) collective-permute-start(bf16[32,512]{1,0:T(8,128)(2,1)S(1)} %add_convert_fusion.1), channel_id=1, source_target_pairs={{0,3},{1,2},{2,1},{3,0},{4,7},{5,6},{6,5},{7,4},{8,11},{9,10},{10,... | collective-permute-start | bytes 98312 | tf_op jit(solution)/shard_map/ppermute | solution.py:286
  31.7 1.9 %collective-permute-done.6 = bf16[32,512]{1,0:T(8,128)(2,1)S(1)} collective-permute-done((bf16[32,512]{1,0:T(8,128)(2,1)S(1)}, bf16[32,512]{1,0:T(8,128)(2,1)S(1)}, u32[]{:S(2)}, u32[]{:S(2)}) %collective-permute-start.6) | collective-permute-done | bytes 32800 | tf_op jit(solution)/shard_map/ppermute | solution.py:286
  33.7 0.6 %collective-permute-start.9 = (bf16[32,512]{1,0:T(8,128)(2,1)S(1)}, bf16[32,512]{1,0:T(8,128)(2,1)S(1)}, u32[]{:S(2)}, u32[]{:S(2)}) collective-permute-start(bf16[32,512]{1,0:T(8,128)(2,1)S(1)} %add_convert_fusion.a), channel_id=1, source_target_pairs={{0,12},{1,13},{2,14},{3,15},{4,8},{5,9},{6,10},{7,11},{8,4},{9,5},... | collective-permute-start | bytes 98312 | tf_op jit(solution)/shard_map/ppermute | solution.py:286
  34.3 0.3 collective-permute-start.8
  34.6 2.3 %collective-permute-start.7 = (bf16[32,512]{1,0:T(8,128)(2,1)S(1)}, bf16[32,512]{1,0:T(8,128)(2,1)S(1)}, u32[]{:S(2)}, u32[]{:S(2)}) collective-permute-start(bf16[32,512]{1,0:T(8,128)(2,1)S(1)} %add_convert_fusion.a), channel_id=1, source_target_pairs={{0,9},{1,8},{2,11},{3,10},{4,13},{5,12},{6,15},{7,14},{8,1},{9,0},... | collective-permute-start | bytes 98312 | tf_op jit(solution)/shard_map/ppermute | solution.py:286
  36.9 1.7 %collective-permute-done.9.d = bf16[32,512]{1,0:T(8,128)(2,1)S(1)} collective-permute-done((bf16[32,512]{1,0:T(8,128)(2,1)S(1)}, bf16[32,512]{1,0:T(8,128)(2,1)S(1)}, u32[]{:S(2)}, u32[]{:S(2)}) %collective-permute-start.9) | collective-permute-done | bytes 32800 | tf_op jit(solution)/shard_map/ppermute | solution.py:286
  38.6 0.0 collective-permute-done.8.c
  38.7 0.0 collective-permute-done.7.b
  38.7 1.3 %final.1 = (f32[32,64]{1,0:T(8,128)}, bf16[2,2048]{1,0:T(2,128)(2,1)}) custom-call(s32[8,128]{1,0:T(8,128)S(1)} %get-tuple-element.7.places, bf16[32,512]{1,0:T(8,128)(2,1)S(1)} %add_convert_fusion.a, bf16[32,512]{1,0:T(8,128)(2,1)S(1)} %collective-permute-done.7.b, bf16[32,512]{1,0:T(8,128)(2,1)S(1)} %collective-permute-done.8.c, ...), custom_call_target="tpu_custom_call" | custom-call | tf_op jit(solution)/shard_map/final/pallas_call | solution.py:361
  (2 shorter events, 0.0 us)
Async XLA Ops:
  3.3 18.5 %all-to-all-start = ((bf16[16,144,128]{2,1,0:T(8,128)(2,1)}), bf16[16,144,128]{2,1,0:T(8,128)(2,1)S(1)}, u32[]{:S(2)}, u32[]{:S(2)}) async-start(bf16[16,144,128]{2,1,0:T(8,128)(2,1)} %get-tuple-element.8), calls=%async_computation | async-start | bytes 1179648 | tf_op jit(solution)/shard_map/all_to_all | solution.py:325
  9.6 12.2 %collective-permute-start.3 = (bf16[48,128]{1,0:T(8,128)(2,1)S(1)}, bf16[48,128]{1,0:T(8,128)(2,1)S(1)}, u32[]{:S(2)}, u32[]{:S(2)}) collective-permute-start(bf16[48,128]{1,0:T(8,128)(2,1)S(1)} %get-tuple-element.9), channel_id=1, source_target_pairs={{0,29},{1,28},{2,31},{3,30},{4,25},{5,24},{6,27},{7,26},{8,21},{9,... | collective-permute-start | bytes 36872 | tf_op jit(solution)/shard_map/ppermute | solution.py:286
  14.2 7.6 %collective-permute-start.2 = (bf16[48,128]{1,0:T(8,128)(2,1)S(1)}, bf16[48,128]{1,0:T(8,128)(2,1)S(1)}, u32[]{:S(2)}, u32[]{:S(2)}) collective-permute-start(bf16[48,128]{1,0:T(8,128)(2,1)S(1)} %get-tuple-element.9), channel_id=1, source_target_pairs={{0,25},{1,24},{2,27},{3,26},{4,29},{5,28},{6,31},{7,30},{8,17},{9,... | collective-permute-start | bytes 36872 | tf_op jit(solution)/shard_map/ppermute | solution.py:286
  14.5 7.3 %collective-permute-start.1 = (bf16[48,128]{1,0:T(8,128)(2,1)S(1)}, bf16[48,128]{1,0:T(8,128)(2,1)S(1)}, u32[]{:S(2)}, u32[]{:S(2)}) collective-permute-start(bf16[48,128]{1,0:T(8,128)(2,1)S(1)} %get-tuple-element.9), channel_id=1, source_target_pairs={{0,21},{1,20},{2,23},{3,22},{4,17},{5,16},{6,19},{7,18},{8,29},{9,... | collective-permute-start | bytes 36872 | tf_op jit(solution)/shard_map/ppermute | solution.py:286
  14.8 6.9 %collective-permute-start = (bf16[48,128]{1,0:T(8,128)(2,1)S(1)}, bf16[48,128]{1,0:T(8,128)(2,1)S(1)}, u32[]{:S(2)}, u32[]{:S(2)}) collective-permute-start(bf16[48,128]{1,0:T(8,128)(2,1)S(1)} %get-tuple-element.9), channel_id=1, source_target_pairs={{0,17},{1,16},{2,19},{3,18},{4,21},{5,20},{6,23},{7,22},{8,25},{9,... | collective-permute-start | bytes 36872 | tf_op jit(solution)/shard_map/ppermute | solution.py:286
  22.5 6.2 %collective-permute-start.4 = (bf16[64,512]{1,0:T(8,128)(2,1)S(1)}, bf16[64,512]{1,0:T(8,128)(2,1)S(1)}, u32[]{:S(2)}, u32[]{:S(2)}) collective-permute-start(bf16[64,512]{1,0:T(8,128)(2,1)S(1)} %get-tuple-element.10.mine), channel_id=1, source_target_pairs={{0,17},{1,16},{2,19},{3,18},{4,21},{5,20},{6,23},{7,22},{8,25},{9,... | collective-permute-start | bytes 196616 | tf_op jit(solution)/shard_map/ppermute | solution.py:286
  29.0 1.3 %collective-permute-start.5 = (bf16[32,512]{1,0:T(8,128)(2,1)S(1)}, bf16[32,512]{1,0:T(8,128)(2,1)S(1)}, u32[]{:S(2)}, u32[]{:S(2)}) collective-permute-start(bf16[32,512]{1,0:T(8,128)(2,1)S(1)} %rows_part.1), channel_id=1, source_target_pairs={{0,1},{1,0},{2,3},{3,2},{4,5},{5,4},{6,7},{7,6},{8,9},{9,8},{10,11... | collective-permute-start | bytes 98312 | tf_op jit(solution)/shard_map/ppermute | solution.py:286
  30.2 3.4 %collective-permute-start.6 = (bf16[32,512]{1,0:T(8,128)(2,1)S(1)}, bf16[32,512]{1,0:T(8,128)(2,1)S(1)}, u32[]{:S(2)}, u32[]{:S(2)}) collective-permute-start(bf16[32,512]{1,0:T(8,128)(2,1)S(1)} %add_convert_fusion.1), channel_id=1, source_target_pairs={{0,3},{1,2},{2,1},{3,0},{4,7},{5,6},{6,5},{7,4},{8,11},{9,10},{10,... | collective-permute-start | bytes 98312 | tf_op jit(solution)/shard_map/ppermute | solution.py:286
  33.7 5.0 %collective-permute-start.9 = (bf16[32,512]{1,0:T(8,128)(2,1)S(1)}, bf16[32,512]{1,0:T(8,128)(2,1)S(1)}, u32[]{:S(2)}, u32[]{:S(2)}) collective-permute-start(bf16[32,512]{1,0:T(8,128)(2,1)S(1)} %add_convert_fusion.a), channel_id=1, source_target_pairs={{0,12},{1,13},{2,14},{3,15},{4,8},{5,9},{6,10},{7,11},{8,4},{9,5},... | collective-permute-start | bytes 98312 | tf_op jit(solution)/shard_map/ppermute | solution.py:286
  34.3 4.4 %collective-permute-start.8 = (bf16[32,512]{1,0:T(8,128)(2,1)S(1)}, bf16[32,512]{1,0:T(8,128)(2,1)S(1)}, u32[]{:S(2)}, u32[]{:S(2)}) collective-permute-start(bf16[32,512]{1,0:T(8,128)(2,1)S(1)} %add_convert_fusion.a), channel_id=1, source_target_pairs={{0,5},{1,4},{2,7},{3,6},{4,1},{5,0},{6,3},{7,2},{8,13},{9,12},{10,... | collective-permute-start | bytes 98312 | tf_op jit(solution)/shard_map/ppermute | solution.py:286
  34.6 4.0 %collective-permute-start.7 = (bf16[32,512]{1,0:T(8,128)(2,1)S(1)}, bf16[32,512]{1,0:T(8,128)(2,1)S(1)}, u32[]{:S(2)}, u32[]{:S(2)}) collective-permute-start(bf16[32,512]{1,0:T(8,128)(2,1)S(1)} %add_convert_fusion.a), channel_id=1, source_target_pairs={{0,9},{1,8},{2,11},{3,10},{4,13},{5,12},{6,15},{7,14},{8,1},{9,0},... | collective-permute-start | bytes 98312 | tf_op jit(solution)/shard_map/ppermute | solution.py:286

commit v13 on v12

--- a/solution.py
+++ b/solution.py
@@ -107,7 +107,7 @@
     loads = [
         pltpu.make_async_copy(tiles_hbm.at[t], tiles.at[t], tile_sems.at[t]) for t in range(count)
     ]
-    for copy in copies + loads:
+    for copy in loads + copies:
         copy.start()
     copies[0].wait()
     copies[1].wait()

time: 40.2 us -> 40.2 us (level)
  no operation moved by 1% of the time
where the time goes in v13:
time: 40.2 us; the launch traced here: 39.9 us
  starting transfers between devices  19.5 us (49%)
  waiting for transfers between devices  14.7 us (37%)
  Pallas kernels  5.02 us (12%)
  between operations  0.68 us (2%)
    ppermute x10, waiting for transfers between devices, swap(): lax.ppermute(x, ('half', 'rest', 'rep'), [(i, i ^ mask) for i in range(si...  14.7 us
    ppermute x10, starting transfers between devices, swap(): lax.ppermute(x, ('half', 'rest', 'rep'), [(i, i ^ mask) for i in range(si...  13.2 us
    all_to_all x1, starting transfers between devices, sliced(): got = lax.all_to_all(sends, ('rest', 'rep'), 0, 0, tiled=True)  6.3 us
    pallas_call x1, Pallas kernels, sliced(): pl.pallas_call(first_kernel, out_shape=(jax.ShapeDtypeStruct((sources, de...  2.62 us
    pallas_call x1, Pallas kernels, sliced(): pl.pallas_call(final_kernel, out_shape=(jax.ShapeDtypeStruct(u_one.shape,...  1.29 us
  transfers between devices with their start and end apart: 11, of which 5 were waited for; matrix products, arithmetic and copies ran while one was open for 0% of the time, Pallas kernels for 0%

profile of v13, /device:TPU:0, one launch (start us, length us, event | category | flops | bytes accessed | tf_op | source)
XLA Modules:
  0.0 39.9 jit_solution(12524437527763960247)
XLA Ops:
  0.6 2.6 %first.1 = (bf16[16,144,128]{2,1,0:T(8,128)(2,1)}, s32[8,128]{1,0:T(8,128)S(1)}, bf16[48,128]{1,0:T(8,128)(2,1)S(1)}) custom-call(s32[2]{0:T(128)} %one_hbm.1, s32[2]{0:T(128)} %two_hbm.1, s32[2]{0:T(128)} %three_hbm.1, s32[8]{0:T(128)} %owner_hbm.1, bf16[2,64,4096]{2,1,0:T(8,128)(2,1)} %tiles_hbm.1, bf16[32,1024]{1,0:T(8,128)(2,1)} %u_three_hbm.1, ...), custom_call_target="tpu_custom_call" | custom-call | tf_op jit(solution)/shard_map/first/pallas_call | solution.py:303
  3.3 6.3 %all-to-all-start = ((bf16[16,144,128]{2,1,0:T(8,128)(2,1)}), bf16[16,144,128]{2,1,0:T(8,128)(2,1)S(1)}, u32[]{:S(2)}, u32[]{:S(2)}) async-start(bf16[16,144,128]{2,1,0:T(8,128)(2,1)} %get-tuple-element.8), calls=%async_computation | async-start | bytes 1179648 | tf_op jit(solution)/shard_map/all_to_all | solution.py:325
  9.6 4.6 %collective-permute-start.3 = (bf16[48,128]{1,0:T(8,128)(2,1)S(1)}, bf16[48,128]{1,0:T(8,128)(2,1)S(1)}, u32[]{:S(2)}, u32[]{:S(2)}) collective-permute-start(bf16[48,128]{1,0:T(8,128)(2,1)S(1)} %get-tuple-element.9), channel_id=1, source_target_pairs={{0,29},{1,28},{2,31},{3,30},{4,25},{5,24},{6,27},{7,26},{8,21},{9,... | collective-permute-start | bytes 36872 | tf_op jit(solution)/shard_map/ppermute | solution.py:286
  14.2 0.3 collective-permute-start.2
  14.5 0.3 collective-permute-start.1
  14.8 2.1 %collective-permute-start = (bf16[48,128]{1,0:T(8,128)(2,1)S(1)}, bf16[48,128]{1,0:T(8,128)(2,1)S(1)}, u32[]{:S(2)}, u32[]{:S(2)}) collective-permute-start(bf16[48,128]{1,0:T(8,128)(2,1)S(1)} %get-tuple-element.9), channel_id=1, source_target_pairs={{0,17},{1,16},{2,19},{3,18},{4,21},{5,20},{6,23},{7,22},{8,25},{9,... | collective-permute-start | bytes 36872 | tf_op jit(solution)/shard_map/ppermute | solution.py:286
  16.9 4.8 %collective-permute-done.3.far3 = bf16[48,128]{1,0:T(8,128)(2,1)S(1)} collective-permute-done((bf16[48,128]{1,0:T(8,128)(2,1)S(1)}, bf16[48,128]{1,0:T(8,128)(2,1)S(1)}, u32[]{:S(2)}, u32[]{:S(2)}) %collective-permute-start.3) | collective-permute-done | bytes 12320 | tf_op jit(solution)/shard_map/ppermute | solution.py:286
  21.7 0.0 collective-permute-done.2.far2
  21.7 0.0 collective-permute-done.1.far1
  21.7 0.0 collective-permute-done.far0
  21.7 0.0 all-to-all-done.got
  21.7 0.7 %table.1 = (bf16[64,512]{1,0:T(8,128)(2,1)S(1)}, bf16[32,512]{1,0:T(8,128)(2,1)S(1)}) custom-call(bf16[16,144,128]{2,1,0:T(8,128)(2,1)S(1)} %all-to-all-done.got, bf16[48,128]{1,0:T(8,128)(2,1)S(1)} %collective-permute-done.far0, bf16[48,128]{1,0:T(8,128)(2,1)S(1)} %collective-permute-done.1.far1, bf16[48,128]{1,0:T(8,128)(2,1)S(1)} %collective-permute-done.2.far2, ...), custom_call_target="tpu_custom_call" | custom-call | tf_op jit(solution)/shard_map/table/pallas_call | solution.py:326
  22.5 0.7 %collective-permute-start.4 = (bf16[64,512]{1,0:T(8,128)(2,1)S(1)}, bf16[64,512]{1,0:T(8,128)(2,1)S(1)}, u32[]{:S(2)}, u32[]{:S(2)}) collective-permute-start(bf16[64,512]{1,0:T(8,128)(2,1)S(1)} %get-tuple-element.10.mine), channel_id=1, source_target_pairs={{0,17},{1,16},{2,19},{3,18},{4,21},{5,20},{6,23},{7,22},{8,25},{9,... | collective-permute-start | bytes 196616 | tf_op jit(solution)/shard_map/ppermute | solution.py:286
  23.2 0.1 known.1
  23.3 5.4 %collective-permute-done.4.theirs = bf16[64,512]{1,0:T(8,128)(2,1)S(1)} collective-permute-done((bf16[64,512]{1,0:T(8,128)(2,1)S(1)}, bf16[64,512]{1,0:T(8,128)(2,1)S(1)}, u32[]{:S(2)}, u32[]{:S(2)}) %collective-permute-start.4) | collective-permute-done | bytes 65568 | tf_op jit(solution)/shard_map/ppermute | solution.py:286
  28.7 0.2 rows_part.1
  28.9 0.4 %collective-permute-start.5 = (bf16[32,512]{1,0:T(8,128)(2,1)S(1)}, bf16[32,512]{1,0:T(8,128)(2,1)S(1)}, u32[]{:S(2)}, u32[]{:S(2)}) collective-permute-start(bf16[32,512]{1,0:T(8,128)(2,1)S(1)} %rows_part.1), channel_id=1, source_target_pairs={{0,1},{1,0},{2,3},{3,2},{4,5},{5,4},{6,7},{7,6},{8,9},{9,8},{10,11... | collective-permute-start | bytes 98312 | tf_op jit(solution)/shard_map/ppermute | solution.py:286
  29.4 0.9 %collective-permute-done.5 = bf16[32,512]{1,0:T(8,128)(2,1)S(1)} collective-permute-done((bf16[32,512]{1,0:T(8,128)(2,1)S(1)}, bf16[32,512]{1,0:T(8,128)(2,1)S(1)}, u32[]{:S(2)}, u32[]{:S(2)}) %collective-permute-start.5) | collective-permute-done | bytes 32800 | tf_op jit(solution)/shard_map/ppermute | solution.py:286
  30.2 1.5 %collective-permute-start.6 = (bf16[32,512]{1,0:T(8,128)(2,1)S(1)}, bf16[32,512]{1,0:T(8,128)(2,1)S(1)}, u32[]{:S(2)}, u32[]{:S(2)}) collective-permute-start(bf16[32,512]{1,0:T(8,128)(2,1)S(1)} %add_convert_fusion.1), channel_id=1, source_target_pairs={{0,3},{1,2},{2,1},{3,0},{4,7},{5,6},{6,5},{7,4},{8,11},{9,10},{10,... | collective-permute-start | bytes 98312 | tf_op jit(solution)/shard_map/ppermute | solution.py:286
  31.7 1.9 %collective-permute-done.6 = bf16[32,512]{1,0:T(8,128)(2,1)S(1)} collective-permute-done((bf16[32,512]{1,0:T(8,128)(2,1)S(1)}, bf16[32,512]{1,0:T(8,128)(2,1)S(1)}, u32[]{:S(2)}, u32[]{:S(2)}) %collective-permute-start.6) | collective-permute-done | bytes 32800 | tf_op jit(solution)/shard_map/ppermute | solution.py:286
  33.6 0.6 %collective-permute-start.9 = (bf16[32,512]{1,0:T(8,128)(2,1)S(1)}, bf16[32,512]{1,0:T(8,128)(2,1)S(1)}, u32[]{:S(2)}, u32[]{:S(2)}) collective-permute-start(bf16[32,512]{1,0:T(8,128)(2,1)S(1)} %add_convert_fusion.a), channel_id=1, source_target_pairs={{0,12},{1,13},{2,14},{3,15},{4,8},{5,9},{6,10},{7,11},{8,4},{9,5},... | collective-permute-start | bytes 98312 | tf_op jit(solution)/shard_map/ppermute | solution.py:286
  34.3 0.3 collective-permute-start.8
  34.6 2.3 %collective-permute-start.7 = (bf16[32,512]{1,0:T(8,128)(2,1)S(1)}, bf16[32,512]{1,0:T(8,128)(2,1)S(1)}, u32[]{:S(2)}, u32[]{:S(2)}) collective-permute-start(bf16[32,512]{1,0:T(8,128)(2,1)S(1)} %add_convert_fusion.a), channel_id=1, source_target_pairs={{0,9},{1,8},{2,11},{3,10},{4,13},{5,12},{6,15},{7,14},{8,1},{9,0},... | collective-permute-start | bytes 98312 | tf_op jit(solution)/shard_map/ppermute | solution.py:286
  36.9 1.7 %collective-permute-done.9.d = bf16[32,512]{1,0:T(8,128)(2,1)S(1)} collective-permute-done((bf16[32,512]{1,0:T(8,128)(2,1)S(1)}, bf16[32,512]{1,0:T(8,128)(2,1)S(1)}, u32[]{:S(2)}, u32[]{:S(2)}) %collective-permute-start.9) | collective-permute-done | bytes 32800 | tf_op jit(solution)/shard_map/ppermute | solution.py:286
  38.6 0.0 collective-permute-done.8.c
  38.6 0.0 collective-permute-done.7.b
  38.6 1.3 %final.1 = (f32[32,64]{1,0:T(8,128)}, bf16[2,2048]{1,0:T(2,128)(2,1)}) custom-call(s32[8,128]{1,0:T(8,128)S(1)} %get-tuple-element.7.places, bf16[32,512]{1,0:T(8,128)(2,1)S(1)} %add_convert_fusion.a, bf16[32,512]{1,0:T(8,128)(2,1)S(1)} %collective-permute-done.7.b, bf16[32,512]{1,0:T(8,128)(2,1)S(1)} %collective-permute-done.8.c, ...), custom_call_target="tpu_custom_call" | custom-call | tf_op jit(solution)/shard_map/final/pallas_call | solution.py:361
  (2 shorter events, 0.0 us)
Async XLA Ops:
  3.3 18.5 %all-to-all-start = ((bf16[16,144,128]{2,1,0:T(8,128)(2,1)}), bf16[16,144,128]{2,1,0:T(8,128)(2,1)S(1)}, u32[]{:S(2)}, u32[]{:S(2)}) async-start(bf16[16,144,128]{2,1,0:T(8,128)(2,1)} %get-tuple-element.8), calls=%async_computation | async-start | bytes 1179648 | tf_op jit(solution)/shard_map/all_to_all | solution.py:325
  9.6 12.2 %collective-permute-start.3 = (bf16[48,128]{1,0:T(8,128)(2,1)S(1)}, bf16[48,128]{1,0:T(8,128)(2,1)S(1)}, u32[]{:S(2)}, u32[]{:S(2)}) collective-permute-start(bf16[48,128]{1,0:T(8,128)(2,1)S(1)} %get-tuple-element.9), channel_id=1, source_target_pairs={{0,29},{1,28},{2,31},{3,30},{4,25},{5,24},{6,27},{7,26},{8,21},{9,... | collective-permute-start | bytes 36872 | tf_op jit(solution)/shard_map/ppermute | solution.py:286
  14.2 7.6 %collective-permute-start.2 = (bf16[48,128]{1,0:T(8,128)(2,1)S(1)}, bf16[48,128]{1,0:T(8,128)(2,1)S(1)}, u32[]{:S(2)}, u32[]{:S(2)}) collective-permute-start(bf16[48,128]{1,0:T(8,128)(2,1)S(1)} %get-tuple-element.9), channel_id=1, source_target_pairs={{0,25},{1,24},{2,27},{3,26},{4,29},{5,28},{6,31},{7,30},{8,17},{9,... | collective-permute-start | bytes 36872 | tf_op jit(solution)/shard_map/ppermute | solution.py:286
  14.5 7.3 %collective-permute-start.1 = (bf16[48,128]{1,0:T(8,128)(2,1)S(1)}, bf16[48,128]{1,0:T(8,128)(2,1)S(1)}, u32[]{:S(2)}, u32[]{:S(2)}) collective-permute-start(bf16[48,128]{1,0:T(8,128)(2,1)S(1)} %get-tuple-element.9), channel_id=1, source_target_pairs={{0,21},{1,20},{2,23},{3,22},{4,17},{5,16},{6,19},{7,18},{8,29},{9,... | collective-permute-start | bytes 36872 | tf_op jit(solution)/shard_map/ppermute | solution.py:286
  14.8 6.9 %collective-permute-start = (bf16[48,128]{1,0:T(8,128)(2,1)S(1)}, bf16[48,128]{1,0:T(8,128)(2,1)S(1)}, u32[]{:S(2)}, u32[]{:S(2)}) collective-permute-start(bf16[48,128]{1,0:T(8,128)(2,1)S(1)} %get-tuple-element.9), channel_id=1, source_target_pairs={{0,17},{1,16},{2,19},{3,18},{4,21},{5,20},{6,23},{7,22},{8,25},{9,... | collective-permute-start | bytes 36872 | tf_op jit(solution)/shard_map/ppermute | solution.py:286
  22.5 6.2 %collective-permute-start.4 = (bf16[64,512]{1,0:T(8,128)(2,1)S(1)}, bf16[64,512]{1,0:T(8,128)(2,1)S(1)}, u32[]{:S(2)}, u32[]{:S(2)}) collective-permute-start(bf16[64,512]{1,0:T(8,128)(2,1)S(1)} %get-tuple-element.10.mine), channel_id=1, source_target_pairs={{0,17},{1,16},{2,19},{3,18},{4,21},{5,20},{6,23},{7,22},{8,25},{9,... | collective-permute-start | bytes 196616 | tf_op jit(solution)/shard_map/ppermute | solution.py:286
  28.9 1.3 %collective-permute-start.5 = (bf16[32,512]{1,0:T(8,128)(2,1)S(1)}, bf16[32,512]{1,0:T(8,128)(2,1)S(1)}, u32[]{:S(2)}, u32[]{:S(2)}) collective-permute-start(bf16[32,512]{1,0:T(8,128)(2,1)S(1)} %rows_part.1), channel_id=1, source_target_pairs={{0,1},{1,0},{2,3},{3,2},{4,5},{5,4},{6,7},{7,6},{8,9},{9,8},{10,11... | collective-permute-start | bytes 98312 | tf_op jit(solution)/shard_map/ppermute | solution.py:286
  30.2 3.4 %collective-permute-start.6 = (bf16[32,512]{1,0:T(8,128)(2,1)S(1)}, bf16[32,512]{1,0:T(8,128)(2,1)S(1)}, u32[]{:S(2)}, u32[]{:S(2)}) collective-permute-start(bf16[32,512]{1,0:T(8,128)(2,1)S(1)} %add_convert_fusion.1), channel_id=1, source_target_pairs={{0,3},{1,2},{2,1},{3,0},{4,7},{5,6},{6,5},{7,4},{8,11},{9,10},{10,... | collective-permute-start | bytes 98312 | tf_op jit(solution)/shard_map/ppermute | solution.py:286
  33.6 5.0 %collective-permute-start.9 = (bf16[32,512]{1,0:T(8,128)(2,1)S(1)}, bf16[32,512]{1,0:T(8,128)(2,1)S(1)}, u32[]{:S(2)}, u32[]{:S(2)}) collective-permute-start(bf16[32,512]{1,0:T(8,128)(2,1)S(1)} %add_convert_fusion.a), channel_id=1, source_target_pairs={{0,12},{1,13},{2,14},{3,15},{4,8},{5,9},{6,10},{7,11},{8,4},{9,5},... | collective-permute-start | bytes 98312 | tf_op jit(solution)/shard_map/ppermute | solution.py:286
  34.3 4.3 %collective-permute-start.8 = (bf16[32,512]{1,0:T(8,128)(2,1)S(1)}, bf16[32,512]{1,0:T(8,128)(2,1)S(1)}, u32[]{:S(2)}, u32[]{:S(2)}) collective-permute-start(bf16[32,512]{1,0:T(8,128)(2,1)S(1)} %add_convert_fusion.a), channel_id=1, source_target_pairs={{0,5},{1,4},{2,7},{3,6},{4,1},{5,0},{6,3},{7,2},{8,13},{9,12},{10,... | collective-permute-start | bytes 98312 | tf_op jit(solution)/shard_map/ppermute | solution.py:286
  34.6 4.0 %collective-permute-start.7 = (bf16[32,512]{1,0:T(8,128)(2,1)S(1)}, bf16[32,512]{1,0:T(8,128)(2,1)S(1)}, u32[]{:S(2)}, u32[]{:S(2)}) collective-permute-start(bf16[32,512]{1,0:T(8,128)(2,1)S(1)} %add_convert_fusion.a), channel_id=1, source_target_pairs={{0,9},{1,8},{2,11},{3,10},{4,13},{5,12},{6,15},{7,14},{8,1},{9,0},... | collective-permute-start | bytes 98312 | tf_op jit(solution)/shard_map/ppermute | solution.py:286
